TPU v7x, 32 devices: a whole 2x2x4 slice. The times are simulated.
32 devices in a mesh: grid: 8 (over y, x, core), pts: 4 (over z).
Axes of the slice: x: 2, y: 2, z: 4, core: 2. Of those that a mesh axis runs over, the one named last changes fastest.
Arguments:
- orbitals: bfloat16 [512, 16384], P(None, 'grid'), may hold values from -0.8984375 to 0.8984375
- point_index: int32 [8192], P('pts'), may hold values from 0 to 16383
Outputs:
- screened: float32 [4, 2048, 128, 128], P('pts', 'grid')
All inputs are finite; a program needn't handle non-finite values.
Results may differ from a plain program's by a relative error of at most 0.0003.
Values may be sent and summed in bfloat16 or wider, within the bound.
No kernel may reach another device: no remote copies, remote signals or barrier semaphores. Data moves between devices by JAX's collectives and lax.ppermute only.
A program may use at most 128 MiB of HBM per device.

v0:
```python
import math

import jax
import jax.numpy as jnp
from jax import lax
from jax.sharding import PartitionSpec as P

SIDE = 128


HIGHEST_PRECISION = lax.Precision.HIGHEST


def dft_tables():
    product_index = (
        lax.broadcasted_iota(jnp.int32, (SIDE, SIDE), 0)
        * lax.broadcasted_iota(jnp.int32, (SIDE, SIDE), 1)
        % SIDE
    )
    angles = product_index.astype(jnp.float32) * (2.0 * math.pi / SIDE)
    return (jnp.cos(angles), jnp.sin(angles))


def screen_kernel():
    frequency = jnp.arange(SIDE, dtype=jnp.int32)
    wavenumber = jnp.minimum(frequency, SIDE - frequency).astype(jnp.float32)
    screening = SIDE / 16.0
    values = screening / jnp.sqrt(
        wavenumber[:, None] ** 2 + wavenumber[None, :] ** 2 + screening * screening
    )
    anchor = (frequency[:, None] == 0) & (frequency[None, :] == 0)
    return jnp.where(anchor, jnp.zeros_like(values), values)


def column_pass(values, matrix):
    return jnp.einsum("kx,nxy->nky", matrix, values, precision=HIGHEST_PRECISION)


def screen_sheets(stacked, cos_table, sin_table, kernel_values):
    sheets = stacked[0, :, 0]
    real_rows = jnp.dot(sheets, cos_table, precision=HIGHEST_PRECISION)
    imag_rows = -jnp.dot(sheets, sin_table, precision=HIGHEST_PRECISION)
    real_full = column_pass(real_rows, cos_table) + column_pass(imag_rows, sin_table)
    imag_full = column_pass(imag_rows, cos_table) - column_pass(real_rows, sin_table)
    real_scaled = real_full * kernel_values
    imag_scaled = imag_full * kernel_values
    real_back = column_pass(real_scaled, cos_table) - column_pass(imag_scaled, sin_table)
    imag_back = column_pass(imag_scaled, cos_table) + column_pass(real_scaled, sin_table)
    result = jnp.dot(real_back, cos_table, precision=HIGHEST_PRECISION) - jnp.dot(
        imag_back, sin_table, precision=HIGHEST_PRECISION
    )
    return (result * (1.0 / (SIDE * SIDE)))[None]


def shards(orbitals, point_index):
    cell_count = orbitals.shape[1]
    tile_points = point_index.shape[0]
    grid_count = lax.axis_size("grid")
    row_count = cell_count // SIDE
    local_index = point_index - lax.axis_index("grid") * cell_count
    owner_mask = (
        lax.broadcasted_iota(jnp.int32, (cell_count, tile_points), 0) == local_index[None, :]
    ).astype(jnp.bfloat16)
    own_values = jnp.dot(orbitals, owner_mask, preferred_element_type=jnp.float32)
    picked = lax.psum(own_values.astype(jnp.bfloat16), "grid")
    pair_values = lax.dot_general(
        picked, orbitals, (((0,), (0,)), ((), ())), preferred_element_type=jnp.float32
    )
    squared = pair_values * pair_values
    cos_table, sin_table = dft_tables()
    kernel_values = screen_kernel()
    tile_block = squared.reshape(grid_count, tile_points // grid_count, row_count, SIDE)
    stacked = tile_block[:, :, None]
    arrived = lax.all_to_all(stacked, "grid", split_axis=0, concat_axis=3, tiled=True)
    return screen_sheets(arrived, cos_table, sin_table, kernel_values)


def solution(mesh):
    in_specs = (P(None, "grid"), P("pts"))
    out_specs = P("pts", "grid", None, None)
    return jax.shard_map(shards, mesh=mesh, in_specs=in_specs, out_specs=out_specs, check_vma=False)
```

profile of v0, /device:TPU:0, one launch (start us, length us, event | category | flops | bytes accessed | tf_op | source)
XLA Modules:
  0.0 578.6 jit_solution(6754933141304690683)
XLA Ops:
  6.5 0.8 broadcast_subtract_fusion
  7.4 0.8 copy-done
  8.1 5.7 fusion.23
  13.9 0.0 all-reduce.2.cloned.1.call-update
  13.9 64.3 %all-reduce.2.cloned.1.call-done = bf16[512,2048]{0,1:T(8,128)(2,1)} async-done(((bf16[512,2048]{0,1:T(8,128)(2,1)}), bf16[512,2048]{0,1:T(8,128)(2,1)}) %all-reduce.2.cloned.1.call-update) | async-done | bytes 2097168 | tf_op jit(solution)/shard_map/psum | solution.py:65
  78.2 6.2 %multiply_bitcast_fusion.1 = f32[256,8,16,128]{3,1,2,0:T(8,128)S(1)} fusion(bf16[512,2048]{0,1:T(8,128)(2,1)} %all-reduce.2.cloned.1.call-done, bf16[512,2048]{1,0:T(8,128)(2,1)S(1)} %copy-done), kind=kOutput, calls=%fused_computation.9 | convolution fusion | flops 4299161600 | bytes 20971520 | tf_op jit(solution)/shard_map/dot_general | solution.py:66
  84.4 7.6 %copy.17 = f32[256,8,16,128]{3,2,1,0:T(8,128)} copy(f32[256,8,16,128]{3,1,2,0:T(8,128)S(1)} %multiply_bitcast_fusion.1) | data formatting | bytes 33554432
  91.9 6.2 %all-to-all-start = ((f32[8,256,1,16,128]{4,3,1,2,0:T(8,128)}), f32[8,256,1,16,128]{4,3,1,2,0:T(8,128)}, u32[]{:S(2)}, u32[]{:S(2)}) async-start(f32[8,256,1,16,128]{4,3,1,2,0:T(8,128)} %bitcast.68), calls=%async_computation | async-start | bytes 33554432 | tf_op jit(solution)/shard_map/all_to_all | solution.py:74
  98.2 0.1 multiply_select_fusion
  98.3 183.8 %all-to-all-done = f32[8,256,1,16,128]{4,3,1,2,0:T(8,128)} async-done(((f32[8,256,1,16,128]{4,3,1,2,0:T(8,128)}), f32[8,256,1,16,128]{4,3,1,2,0:T(8,128)}, u32[]{:S(2)}, u32[]{:S(2)}) %all-to-all-start) | async-done | bytes 16777248 | tf_op jit(solution)/shard_map/all_to_all | solution.py:74
  282.1 6.9 %copy.9 = f32[1,256,1,8,16,128]{5,4,3,1,2,0:T(8,128)S(1)} copy(f32[1,256,1,8,16,128]{5,4,1,3,2,0:T(8,128)} %bitcast.3) | data formatting | bytes 33554432 | tf_op jit(solution)/shard_map/all_to_all | solution.py:74
  289.1 6.2 %copy-done.2 = f32[1,256,1,8,16,128]{5,4,3,1,2,0:T(8,128)} copy-done((f32[1,256,1,8,16,128]{5,4,3,1,2,0:T(8,128)}, f32[1,256,1,8,16,128]{5,4,3,1,2,0:T(8,128)S(1)}, u32[]{:S(2)}) %copy-start.2) | copy-done | bytes 16777240
  295.2 16.7 %fusion.37 = f32[256,128,128]{2,1,0:T(8,128)} fusion(f32[256,128,128]{2,1,0:T(8,128)S(1)} %bitcast.66), kind=kOutput, calls=%fused_computation.34 | convolution fusion | flops 6442680320 | bytes 33554432 | tf_op jit(solution)/shard_map/dot_general | solution.py:42
  311.9 22.3 %fusion.47 = f32[256,128,128]{1,2,0:T(8,128)} fusion(f32[256,128,128]{2,1,0:T(8,128)} %bitcast.67), kind=kOutput, calls=%fused_computation.44 | convolution fusion | flops 6442680320 | bytes 33554432 | tf_op jit(solution)/shard_map/dot_general | solution.py:41
  334.2 19.2 %fusion.45 = f32[256,128,128]{2,1,0:T(8,128)} fusion(f32[256,128,128]{1,2,0:T(8,128)} %fusion.47), kind=kOutput, calls=%fused_computation.42 | convolution fusion | flops 6442680320 | bytes 33554432 | tf_op jit(solution)/shard_map/kx,nxy->nky/dot_general | solution.py:36
  353.5 19.3 %fusion.34 = f32[256,128,128]{2,1,0:T(8,128)} fusion(f32[256,128,128]{1,2,0:T(8,128)} %fusion.47), kind=kOutput, calls=%fused_computation.31 | convolution fusion | flops 6442680320 | bytes 33554432 | tf_op jit(solution)/shard_map/kx,nxy->nky/dot_general | solution.py:36
  372.8 31.7 %bitcast_multiply_fusion = f32[256,128,128]{1,2,0:T(8,128)} fusion(f32[256,128,128]{2,1,0:T(8,128)} %fusion.34, f32[256,128,128]{2,1,0:T(8,128)S(1)} %bitcast.65, f32[128,128]{0,1:T(8,128)S(1)} %multiply_select_fusion), kind=kOutput, calls=%fused_computation.4 | convolution fusion | flops 6455263232 | bytes 50397184 | tf_op jit(solution)/shard_map/kx,nxy->nky/dot_general | solution.py:36
  404.5 23.0 %fusion.39 = f32[256,128,128]{1,2,0:T(8,128)} fusion(f32[256,128,128]{1,2,0:T(8,128)} %bitcast_multiply_fusion), kind=kOutput, calls=%fused_computation.36 | convolution fusion | flops 6442680320 | bytes 33554432 | tf_op jit(solution)/shard_map/kx,nxy->nky/dot_general | solution.py:36
  427.4 22.9 %fusion.32 = f32[256,128,128]{1,2,0:T(8,128)} fusion(f32[256,128,128]{1,2,0:T(8,128)} %bitcast_multiply_fusion), kind=kOutput, calls=%fused_computation.29 | convolution fusion | flops 6442680320 | bytes 33554432 | tf_op jit(solution)/shard_map/kx,nxy->nky/dot_general | solution.py:36
  450.3 33.4 %bitcast_multiply_fusion.1 = f32[256,128,128]{1,2,0:T(8,128)} fusion(f32[256,128,128]{2,1,0:T(8,128)} %fusion.45, f32[256,128,128]{2,1,0:T(8,128)} %fusion.37, f32[128,128]{0,1:T(8,128)S(1)} %multiply_select_fusion), kind=kOutput, calls=%fused_computation.5 | convolution fusion | flops 6455263232 | bytes 50397184 | tf_op jit(solution)/shard_map/kx,nxy->nky/dot_general | solution.py:36
  483.7 22.8 %fusion.30 = f32[256,128,128]{1,2,0:T(8,128)} fusion(f32[256,128,128]{1,2,0:T(8,128)} %bitcast_multiply_fusion.1), kind=kOutput, calls=%fused_computation.27 | convolution fusion | flops 6442680320 | bytes 33554432 | tf_op jit(solution)/shard_map/kx,nxy->nky/dot_general | solution.py:36
  506.5 23.0 %fusion.43 = f32[256,128,128]{1,2,0:T(8,128)} fusion(f32[256,128,128]{1,2,0:T(8,128)} %bitcast_multiply_fusion.1), kind=kOutput, calls=%fused_computation.40 | convolution fusion | flops 6442680320 | bytes 33554432 | tf_op jit(solution)/shard_map/kx,nxy->nky/dot_general | solution.py:36
  529.4 19.2 %fusion = f32[256,128,128]{2,1,0:T(8,128)S(1)} fusion(f32[256,128,128]{1,2,0:T(8,128)} %fusion.39, f32[256,128,128]{1,2,0:T(8,128)} %fusion.30), kind=kOutput, calls=%fused_computation | convolution fusion | flops 6446874624 | bytes 50331648 | tf_op jit(solution)/shard_map/dot_general | solution.py:49
  548.7 22.8 %multiply_bitcast_fusion = f32[1,256,128,128]{3,2,1,0:T(8,128)} fusion(f32[256,128,128]{2,1,0:T(8,128)S(1)} %fusion, f32[256,128,128]{1,2,0:T(8,128)} %fusion.43, f32[256,128,128]{1,2,0:T(8,128)} %fusion.32), kind=kOutput, calls=%fused_computation.6 | convolution fusion | flops 6455263232 | bytes 67108864 | tf_op jit(solution)/shard_map/dot_general | solution.py:49
  (16 shorter events, 0.0 us)
Async XLA Ops:
  6.5 1.6 copy-start
  6.5 71.7 %all-reduce.2.cloned.1.call-start = ((), (), s32[]{:S(2)}) async-start(), calls=%async_computation.1 | async-start | bytes 4194304 | tf_op jit(solution)/shard_map/psum | solution.py:65
  91.9 190.2 %all-to-all-start = ((f32[8,256,1,16,128]{4,3,1,2,0:T(8,128)}), f32[8,256,1,16,128]{4,3,1,2,0:T(8,128)}, u32[]{:S(2)}, u32[]{:S(2)}) async-start(f32[8,256,1,16,128]{4,3,1,2,0:T(8,128)} %bitcast.68), calls=%async_computation | async-start | bytes 33554432 | tf_op jit(solution)/shard_map/all_to_all | solution.py:74
  289.0 6.2 %copy-start.2 = (f32[1,256,1,8,16,128]{5,4,3,1,2,0:T(8,128)}, f32[1,256,1,8,16,128]{5,4,3,1,2,0:T(8,128)S(1)}, u32[]{:S(2)}) copy-start(f32[1,256,1,8,16,128]{5,4,3,1,2,0:T(8,128)S(1)} %copy.9) | copy-start | bytes 50331652
  334.2 38.5 %slice-start = ((s8[16777216]{0:T(1024)(128)(4,1)}), s8[4194304]{0:T(1024)(128)(4,1)S(1)}, s32[]{:S(2)}) async-start(s8[16777216]{0:T(1024)(128)(4,1)} %bitcast.64), calls=%async_computation.2 | async-start | bytes 8388608
  334.2 38.5 %slice-start.1 = ((s8[16777216]{0:T(1024)(128)(4,1)}), s8[4194304]{0:T(1024)(128)(4,1)S(1)}, s32[]{:S(2)}) async-start(s8[16777216]{0:T(1024)(128)(4,1)} %bitcast.64), calls=%async_computation.3 | async-start | bytes 8388608
  353.4 19.3 %slice-start.2 = ((s8[16777216]{0:T(1024)(128)(4,1)}), s8[4194304]{0:T(1024)(128)(4,1)S(1)}, s32[]{:S(2)}) async-start(s8[16777216]{0:T(1024)(128)(4,1)} %bitcast.64), calls=%async_computation.4 | async-start | bytes 8388608
  353.5 19.4 %slice-start.3 = ((s8[16777216]{0:T(1024)(128)(4,1)}), s8[4194304]{0:T(1024)(128)(4,1)S(1)}, s32[]{:S(2)}) async-start(s8[16777216]{0:T(1024)(128)(4,1)} %bitcast.64), calls=%async_computation.5 | async-start | bytes 8388608
  548.7 22.8 %copy-start.1 = (bf16[512,2048]{1,0:T(8,128)(2,1)S(1)}, bf16[512,2048]{1,0:T(8,128)(2,1)}, u32[]{:S(2)}) copy-start(bf16[512,2048]{1,0:T(8,128)(2,1)} %param.2) | copy-start | bytes 6291460
Sparse Core Ops, SparseCore 0:
  14.0 64.1 all-reduce.1
where the time goes:
time: 590 us; the launch traced here: 579 us
  matrix products  288 us (49%)
  waiting for transfers between devices  248 us (42%)
  local copies, waits for them, and re-layouts  21.4 us (4%)
  between operations  13.8 us (2%)
  starting transfers between devices  6.2 us (1%)
    dot_general x8, matrix products, column_pass(): jnp.einsum('kx,nxy->nky', matrix, values, precision=HIGHEST_PRECISION)  195 us
    all_to_all x1, waiting for transfers between devices, shards(): lax.all_to_all(stacked, 'grid', split_axis=0, concat_axis=3, tiled=True)  184 us
    psum x1, waiting for transfers between devices, shards(): picked = lax.psum(own_values.astype(jnp.bfloat16), 'grid')  64.3 us
    dot_general x1, matrix products, screen_sheets(): jnp.dot(real_back, cos_table, precision=HIGHEST_PRECISION)  22.8 us
    dot_general x1, matrix products, screen_sheets(): real_rows = jnp.dot(sheets, cos_table, precision=HIGHEST_PRECISION)  22.3 us
    dot_general x1, matrix products, screen_sheets(): jnp.dot(imag_back, sin_table, precision=HIGHEST_PRECISION)  19.2 us
    dot_general x1, matrix products, screen_sheets(): imag_rows = -jnp.dot(sheets, sin_table, precision=HIGHEST_PRECISION)  16.7 us
    unnamed x15, local copies, waits for them, and re-layouts  14.5 us
  transfers between devices with their start and end apart: 2, of which 2 were waited for; matrix products, arithmetic and copies ran while one was open for 0% of the time, Pallas kernels for 0%

commit v1 on v0

v1 whole, which is shorter than its diff:
```python
import functools
import math

import jax
import jax.numpy as jnp
import numpy as np
from jax import lax
from jax.experimental import pallas as pl
from jax.experimental.pallas import tpu as pltpu
from jax.sharding import PartitionSpec as P

SIDE = 128
VMEM_BYTES = 60 * 2**20


def rotate(value, turn):
    re, im = value
    turn = turn % 1.0
    if turn == 0.0:
        return (re, im)
    if turn == 0.25:
        return (-im, re)
    if turn == 0.5:
        return (-re, -im)
    if turn == 0.75:
        return (im, -re)
    cos, sin = math.cos(2 * math.pi * turn), math.sin(2 * math.pi * turn)
    if turn in (0.125, 0.375, 0.625, 0.875):
        plus, minus = (re + im) * abs(cos), (re - im) * abs(cos)
        if turn == 0.125:
            return (minus, plus)
        if turn == 0.375:
            return (-plus, minus)
        if turn == 0.625:
            return (-minus, -plus)
        return (plus, -minus)
    return (re * cos - im * sin, re * sin + im * cos)


def add(a, b):
    return (a[0] + b[0], a[1] + b[1])


def sub(a, b):
    return (a[0] - b[0], a[1] - b[1])


def complex_dft(values, sign):
    n = len(values)
    if n == 1:
        return list(values)
    if n == 2:
        return [add(values[0], values[1]), sub(values[0], values[1])]
    if n % 4 == 0:
        parts = [complex_dft(values[r::4], sign) for r in range(4)]
        out = [None] * n
        quarter = n // 4
        for k in range(quarter):
            t0, t1, t2, t3 = (rotate(parts[r][k], sign * r * k / n) for r in range(4))
            s02, d02 = add(t0, t2), sub(t0, t2)
            s13, d13 = add(t1, t3), sub(t1, t3)
            out[k] = add(s02, s13)
            out[k + 2 * quarter] = sub(s02, s13)
            if sign < 0:
                out[k + quarter] = (d02[0] + d13[1], d02[1] - d13[0])
                out[k + 3 * quarter] = (d02[0] - d13[1], d02[1] + d13[0])
            else:
                out[k + quarter] = (d02[0] - d13[1], d02[1] + d13[0])
                out[k + 3 * quarter] = (d02[0] + d13[1], d02[1] - d13[0])
        return out
    even, odd = complex_dft(values[0::2], sign), complex_dft(values[1::2], sign)
    turned = [rotate(odd[k], sign * k / n) for k in range(n // 2)]
    return [add(even[k], turned[k]) for k in range(n // 2)] + [
        sub(even[k], turned[k]) for k in range(n // 2)
    ]


def real_dft(values):
    n = len(values)
    if n == 1:
        return [values[0]]
    if n == 2:
        return [values[0] + values[1], values[0] - values[1]]
    even, odd = real_dft(values[0::2]), real_dft(values[1::2])
    out = [None] * (n // 2 + 1)
    out[0], out[n // 2] = even[0] + odd[0], even[0] - odd[0]
    for k in range(1, n // 4):
        turned = rotate(odd[k], -k / n)
        low, high = add(even[k], turned), sub(even[k], turned)
        out[k], out[n // 2 - k] = low, (high[0], -high[1])
    out[n // 4] = (even[n // 4], -odd[n // 4])
    return out


def real_inverse(entries):
    n = 2 * (len(entries) - 1)
    if n == 2:
        return [entries[0] + entries[1], entries[0] - entries[1]]
    even, odd = [None] * (n // 4 + 1), [None] * (n // 4 + 1)
    even[0], odd[0] = entries[0] + entries[n // 2], entries[0] - entries[n // 2]
    for k in range(1, n // 4):
        other = entries[n // 2 - k]
        other = (other[0], -other[1])
        even[k] = add(entries[k], other)
        odd[k] = rotate(sub(entries[k], other), k / n)
    middle = entries[n // 4]
    even[n // 4], odd[n // 4] = 2.0 * middle[0], -2.0 * middle[1]
    out = [None] * n
    out[0::2], out[1::2] = real_inverse(even), real_inverse(odd)
    return out


def circulant_tables():
    frequency = np.arange(SIDE)
    wavenumber = np.minimum(frequency, SIDE - frequency).astype(np.float64)
    screening = SIDE / 16.0
    values = screening / np.sqrt(
        wavenumber[:, None] ** 2 + wavenumber[None, :] ** 2 + screening * screening
    )
    values[0, 0] = 0.0
    cosines = np.cos(2 * np.pi * np.outer(frequency, frequency) / SIDE)
    taps = values[: SIDE // 2 + 1] @ cosines / (SIDE * SIDE)
    shift = (frequency[None, :] - frequency[:, None]) % SIDE
    tables = taps[:, shift].astype(np.float32)
    high = tables.astype(jnp.bfloat16)
    low = (tables - high.astype(np.float32)).astype(jnp.bfloat16)
    return jnp.asarray(np.concatenate([high, low], axis=2))


def pick_kernel(index_ref, orbitals_ref, out_ref):
    points, cells = index_ref.shape[0], orbitals_ref.shape[1]
    hot = lax.broadcasted_iota(jnp.int32, (points, cells), 1) == index_ref[...]
    hot = jnp.where(hot, 1.0, 0.0).astype(jnp.bfloat16)
    out_ref[...] = lax.dot_general(
        hot, orbitals_ref[...], (((1,), (1,)), ((), ())), preferred_element_type=jnp.float32
    ).astype(jnp.bfloat16)


def pick_own(local_index, orbitals):
    points, (orbital_count, cells) = local_index.shape[0], orbitals.shape
    block = min(256, points)
    return pl.pallas_call(
        pick_kernel,
        grid=(points // block,),
        in_specs=[
            pl.BlockSpec((block, 1), lambda i: (i, 0)),
            pl.BlockSpec((orbital_count, cells), lambda i: (0, 0)),
        ],
        out_specs=pl.BlockSpec((block, orbital_count), lambda i: (i, 0)),
        out_shape=jax.ShapeDtypeStruct((points, orbital_count), jnp.bfloat16),
        compiler_params=pltpu.CompilerParams(vmem_limit_bytes=VMEM_BYTES),
        cost_estimate=pl.CostEstimate(
            flops=2 * points * orbital_count * cells,
            bytes_accessed=2 * orbital_count * (cells + points),
            transcendentals=0,
        ),
    )(local_index[:, None], orbitals)


def sheet_kernel(layout, picked_ref, tables_ref, *refs):
    count, parts_of = layout
    arrays = refs[: -7]
    out_ref, cells_ref, squared_ref, slots_ref, stage_ref, in_sem, out_sem = refs[-7:]
    rows = SIDE // count
    points = picked_ref.shape[0]
    half = count // 2
    pair_rows = 2
    steps = rows // pair_rows
    me = lax.axis_index("grid")

    def fetch(step, slot):
        return [
            pltpu.make_async_copy(
                arrays[which].at[:, pl.ds(step * pair_rows * SIDE, pair_rows * SIDE)],
                cells_ref.at[slot, apart, pl.ds(first, size), :],
                in_sem.at[slot],
            )
            for apart, parts in enumerate(parts_of)
            for which, first, size in parts
        ]

    for copy in fetch(0, 0):
        copy.start()
    for step in range(steps):
        slot = step % 2
        if step + 1 < steps:
            for copy in fetch(step + 1, 1 - slot):
                copy.start()
        for copy in fetch(step, slot):
            copy.wait()

        def multiply(apart, carry):
            pair = jnp.dot(
                picked_ref[...], cells_ref[slot, apart], preferred_element_type=jnp.float32
            )
            squared_ref[me ^ apart] = pair * pair
            return carry

        lax.fori_loop(0, count, multiply, 0)
        chunk = 8

        def spread(at, carry):
            here = pl.ds(pl.multiple_of(at * chunk, chunk), chunk)
            for within in range(pair_rows):
                j = step * pair_rows + within
                lanes = pl.ds(within * SIDE, SIDE)
                entries = real_dft([squared_ref[g, here, lanes] for g in range(count)])
                slots_ref[0, j, here, :] = entries[0]
                slots_ref[count - 1, j, here, :] = entries[half]
                for k in range(1, half):
                    re, im = rotate(entries[k], -k * j / SIDE)
                    slots_ref[2 * k - 1, j, here, :] = re
                    slots_ref[2 * k, j, here, :] = im
            return carry

        lax.fori_loop(0, points // chunk, spread, 0, unroll=2)

    def circulant(blocks, a):
        stacked = blocks[0] if len(blocks) == 1 else jnp.concatenate(blocks, axis=0)
        high = stacked.astype(jnp.bfloat16)
        low = (stacked - high.astype(jnp.float32)).astype(jnp.bfloat16)
        table = tables_ref[min(a, SIDE - a)]
        both = jnp.dot(
            jnp.concatenate([high, low], axis=1),
            jnp.concatenate([table, table], axis=0),
            preferred_element_type=jnp.float32,
        )
        return both[:, :SIDE] + both[:, SIDE:]

    chunk = 8

    def over_points(body):
        def one(at, carry):
            body(pl.ds(pl.multiple_of(at * chunk, chunk), chunk))
            return carry

        lax.fori_loop(0, points // chunk, one, 0)

    def apply(places, a):
        outs = circulant([slots_ref[s, j] for s, j in places], a)
        for at, (s, j) in enumerate(places):
            slots_ref[s, j] = outs[at * points : (at + 1) * points]

    def real_there(here):
        entries = real_dft([slots_ref[0, j, here, :] for j in range(rows)])
        slots_ref[0, 0, here, :] = entries[0]
        slots_ref[0, rows - 1, here, :] = entries[rows // 2]
        for k in range(1, rows // 2):
            slots_ref[0, 2 * k - 1, here, :], slots_ref[0, 2 * k, here, :] = entries[k]

    def real_back(here):
        entries = [slots_ref[0, 0, here, :]]
        for k in range(1, rows // 2):
            entries.append((slots_ref[0, 2 * k - 1, here, :], slots_ref[0, 2 * k, here, :]))
        entries.append(slots_ref[0, rows - 1, here, :])
        for j, value in enumerate(real_inverse(entries)):
            slots_ref[0, j, here, :] = value

    over_points(real_there)
    apply([(0, 0)], 0)
    apply([(0, rows - 1)], SIDE // 2)
    for k in range(1, rows // 2):
        apply([(0, 2 * k - 1), (0, 2 * k)], count * k)
    over_points(real_back)

    last = count - 1
    short = rows // 2

    def odd_there(here):
        values = [
            rotate((slots_ref[last, j, here, :], -slots_ref[last, j + short, here, :]), -j / (2 * rows))
            for j in range(short)
        ]
        for k, (re, im) in enumerate(complex_dft(values, -1)):
            slots_ref[last, 2 * k, here, :] = re
            slots_ref[last, 2 * k + 1, here, :] = im

    def odd_back(here):
        values = [
            (slots_ref[last, 2 * k, here, :], slots_ref[last, 2 * k + 1, here, :])
            for k in range(short)
        ]
        for j, value in enumerate(complex_dft(values, 1)):
            re, im = rotate(value, j / (2 * rows))
            slots_ref[last, j, here, :] = 2.0 * re
            slots_ref[last, j + short, here, :] = -2.0 * im

    over_points(odd_there)
    for k in range(short):
        apply([(last, 2 * k), (last, 2 * k + 1)], half + 2 * count * k)
    over_points(odd_back)

    for k in range(1, half):
        re_slot, im_slot = 2 * k - 1, 2 * k

        def complex_there(here, sign=-1):
            values = [
                (slots_ref[re_slot, j, here, :], slots_ref[im_slot, j, here, :])
                for j in range(rows)
            ]
            for j, (re, im) in enumerate(complex_dft(values, sign)):
                slots_ref[re_slot, j, here, :] = re
                slots_ref[im_slot, j, here, :] = im

        over_points(complex_there)
        for a2 in range(rows):
            apply([(re_slot, a2), (im_slot, a2)], k + count * a2)
        over_points(functools.partial(complex_there, sign=1))

    def put(j, slot):
        return [
            pltpu.make_async_copy(
                stage_ref.at[slot, g], out_ref.at[:, rows * g + j, :], out_sem.at[slot]
            )
            for g in range(count)
        ]

    for j in range(rows):
        slot = j % 2
        if j >= 2:
            for copy in put(j - 2, slot):
                copy.wait()

        def gather_back(here):
            entries = [slots_ref[0, j, here, :]]
            for k in range(1, half):
                entries.append(
                    rotate(
                        (slots_ref[2 * k - 1, j, here, :], slots_ref[2 * k, j, here, :]),
                        k * j / SIDE,
                    )
                )
            entries.append(slots_ref[count - 1, j, here, :])
            for g, value in enumerate(real_inverse(entries)):
                stage_ref[slot, g, here, :] = value

        over_points(gather_back)
        for copy in put(j, slot):
            copy.start()
    for j in range(max(rows - 2, 0), rows):
        for copy in put(j, j % 2):
            copy.wait()


def screen_sheets(picked, tables, shard_parts, count):
    points, orbital_count = picked.shape
    arrays, parts_of = [], []
    for parts in shard_parts:
        entry = []
        for array, first in parts:
            entry.append((len(arrays), first, array.shape[0]))
            arrays.append(array)
        parts_of.append(tuple(entry))
    rows = SIDE // count
    vmem = pl.BlockSpec(memory_space=pltpu.VMEM)
    return pl.pallas_call(
        functools.partial(sheet_kernel, (count, tuple(parts_of))),
        in_specs=[vmem, vmem] + [pl.BlockSpec(memory_space=pl.ANY)] * len(arrays),
        out_specs=pl.BlockSpec(memory_space=pl.ANY),
        out_shape=jax.ShapeDtypeStruct((points, SIDE, SIDE), jnp.float32),
        scratch_shapes=[
            pltpu.VMEM((2, count, orbital_count, 2 * SIDE), jnp.bfloat16),
            pltpu.VMEM((count, points, 2 * SIDE), jnp.float32),
            pltpu.VMEM((count, rows, points, SIDE), jnp.float32),
            pltpu.VMEM((2, count, points, SIDE), jnp.float32),
            pltpu.SemaphoreType.DMA((2,)),
            pltpu.SemaphoreType.DMA((2,)),
        ],
        compiler_params=pltpu.CompilerParams(vmem_limit_bytes=VMEM_BYTES),
        cost_estimate=pl.CostEstimate(
            flops=2 * points * orbital_count * SIDE * SIDE,
            bytes_accessed=points * SIDE * SIDE * 8,
            transcendentals=0,
        ),
    )(picked, tables, *arrays)


def swap(array, mask):
    count = lax.axis_size("grid")
    return lax.ppermute(array, "grid", [(i, i ^ mask) for i in range(count)])


def scatter_points(own, masks):
    count = lax.axis_size("grid")
    bits = count.bit_length() - 1
    me = lax.axis_index("grid")
    value = own.reshape((2,) * bits + (own.shape[0] // count, own.shape[1]))
    left = list(range(bits))[::-1]
    for bit in masks:
        axis = left.index(bit)
        mine = (me >> bit) & 1
        keep = lax.dynamic_index_in_dim(value, mine, axis, keepdims=False)
        send = lax.dynamic_index_in_dim(value, 1 - mine, axis, keepdims=False)
        value = keep + swap(send, 1 << bit)
        left.remove(bit)
    return value


def gather_cells(orbitals):
    count = lax.axis_size("grid")
    bits = count.bit_length() - 1
    middle = orbitals.shape[0] // 2
    held = {0: [(orbitals, 0)]}
    link_bits = list(range(1, bits))
    cut = (len(link_bits) + 1) // 2
    routes = (link_bits, link_bits[cut:] + link_bits[:cut])
    pieces = ({0: orbitals[:middle]}, {0: orbitals[middle:]})
    for hop in range(len(link_bits)):
        for route, have in zip(routes, pieces):
            mask = 1 << route[hop]
            for known in sorted(have):
                have[known | mask] = swap(have[known], mask)
    for known in pieces[0]:
        if known:
            held[known] = [(pieces[0][known], 0), (pieces[1][known], middle)]
    for known in sorted(held):
        held[known | 1] = [(swap(array, 1), first) for array, first in held[known]]
    return [held[d] for d in range(count)]


def shards(orbitals, point_index):
    cell_count = orbitals.shape[1]
    count = lax.axis_size("grid")
    bits = count.bit_length() - 1
    local_index = point_index - lax.axis_index("grid") * cell_count
    shard_parts = gather_cells(orbitals)
    own = pick_own(local_index, orbitals)
    picked = scatter_points(own, list(range(bits)))
    return screen_sheets(picked, circulant_tables(), shard_parts, count)[None]


def solution(mesh):
    in_specs = (P(None, "grid"), P("pts"))
    out_specs = P("pts", "grid", None, None)
    return jax.shard_map(shards, mesh=mesh, in_specs=in_specs, out_specs=out_specs, check_vma=False)
```

time: 590 us -> 159 us (0.27); the launches traced: 579 us -> 159 us
  matrix products: 288 us -> 0 us
  waiting for transfers between devices: 248 us -> 72.5 us
  Pallas kernels: 0 us -> 59.6 us
  local copies, waits for them, and re-layouts: 21.4 us -> 6.57 us
  between operations: 13.8 us -> 0.07 us
  starting transfers between devices: 6.2 us -> 14.7 us
    dot_general x14 -> x0, matrix products: 288 us -> none  [the longest x8 195 us: column_pass(): jnp.einsum('kx,nxy->nky', matrix, values, precision=HIGHEST_PRECISION)]
    all_to_all x1 -> x0, waiting for transfers between devices: 184 us -> none  [shards(): lax.all_to_all(stacked, 'grid', split_axis=0, concat_axis=3, tiled=True)]
    ppermute x0 -> x16, waiting for transfers between devices: none -> 72.5 us  [swap(): return lax.ppermute(array, 'grid', [(i, i ^ mask) for i in range(count)])]
    psum x1 -> x0, waiting for transfers between devices: 64.3 us -> none  [shards(): picked = lax.psum(own_values.astype(jnp.bfloat16), 'grid')]
    pallas_call x0 -> x2, Pallas kernels: none -> 59.6 us  [the longest x1 50.4 us: screen_sheets(): pl.pallas_call(functools.partial(sheet_kernel, (count, tuple(parts_of))),...]
    ppermute x0 -> x16, starting transfers between devices: none -> 14.7 us  [swap(): return lax.ppermute(array, 'grid', [(i, i ^ mask) for i in range(count)])]
    unnamed x15 -> x10, local copies, waits for them, and re-layouts: 14.5 us -> 1.58 us
    all_to_all x1 -> x0, local copies, waits for them, and re-layouts: 6.94 us -> none  [shards(): lax.all_to_all(stacked, 'grid', split_axis=0, concat_axis=3, tiled=True)]
  transfers between devices with their start and end apart: 2 -> 16, of which waited for: 2 -> 9; matrix products, arithmetic and copies ran while one was open for 0% -> 3% of each run, Pallas kernels for 0% -> 0%
where the time goes in v1:
time: 159 us
  waiting for transfers between devices  72.5 us (46%)
  Pallas kernels  59.6 us (37%)
  starting transfers between devices  14.7 us (9%)
  local copies, waits for them, and re-layouts  6.57 us (4%)
  other arithmetic  5.14 us (3%)
    ppermute x16, waiting for transfers between devices, swap(): return lax.ppermute(array, 'grid', [(i, i ^ mask) for i in range(count)])  72.5 us
    pallas_call x1, Pallas kernels, screen_sheets(): pl.pallas_call(functools.partial(sheet_kernel, (count, tuple(parts_of))),...  50.4 us
    ppermute x16, starting transfers between devices, swap(): return lax.ppermute(array, 'grid', [(i, i ^ mask) for i in range(count)])  14.7 us
    pallas_call x1, Pallas kernels, pick_own(): pl.pallas_call(pick_kernel, grid=(points // block,), in_specs=[pl.BlockSp...  9.2 us
    add x3, other arithmetic, scatter_points(): value = keep + swap(send, 1 << bit)  4.44 us
  transfers between devices with their start and end apart: 16, of which 9 were waited for; matrix products, arithmetic and copies ran while one was open for 3% of the time, Pallas kernels for 0%

profile of v1, /device:TPU:0, one launch (start us, length us, event | category | flops | bytes accessed | tf_op | source)
XLA Modules:
  0.0 158.6 jit_solution(12826353985097278665)
XLA Ops:
  0.7 1.4 copy.4.index_ref
  2.1 9.2 %shard_map.37 = bf16[2048,512]{1,0:T(8,128)(2,1)} custom-call(s32[2048,1]{1,0:T(8,128)} %copy.4.index_ref, bf16[512,2048]{1,0:T(8,128)(2,1)} %refs_0_.1), custom_call_target="tpu_custom_call" | custom-call | flops 4294967296 | bytes 4194304 | tf_op jit(solution)/shard_map/pallas_call | solution.py:142
  11.3 1.3 dynamic-slice_bitcast_fusion
  13.1 2.4 %collective-permute-done = bf16[2,2,256,512]{3,2,1,0:T(8,128)(2,1)} collective-permute-done((bf16[2,2,256,512]{3,2,1,0:T(8,128)(2,1)S(1)}, bf16[2,2,256,512]{3,2,1,0:T(8,128)(2,1)}, u32[]{:S(2)}, u32[]{:S(2)}) %collective-permute-start) | collective-permute-done | bytes 1048608 | tf_op jit(solution)/shard_map/ppermute | solution.py:380
  15.5 1.6 %bitcast_add_fusion = bf16[2,2,256,512]{3,2,1,0:T(8,128)(2,1)S(1)} fusion(bf16[2,2,256,512]{3,2,1,0:T(8,128)(2,1)} %collective-permute-done, bf16[2,2,2,256,512]{4,3,2,1,0:T(8,128)(2,1)} %bitcast.20, s32[]{:T(128)S(6)} %select_n.21), kind=kLoop, calls=%fused_computation | loop fusion | flops 524288 | bytes 3145732 | tf_op jit(solution)/shard_map/add | solution.py:394
  18.0 2.9 %collective-permute-start.1 = (bf16[2,256,512]{2,1,0:T(8,128)(2,1)}, bf16[2,256,512]{2,1,0:T(8,128)(2,1)}, u32[]{:S(2)}, u32[]{:S(2)}) collective-permute-start(bf16[2,256,512]{2,1,0:T(8,128)(2,1)} %dynamic-slice_bitcast_fusion.1), channel_id=1, source_target_pairs={{0,8},{4,12},{8,0},{12,4},{16,24},{20,28},{24,16},{28,20},{1,9},{5... | collective-permute-start | bytes 1572872 | tf_op jit(solution)/shard_map/ppermute | solution.py:380
  20.9 1.5 fusion
  22.3 1.5 collective-permute-start.9
  24.4 2.0 %collective-permute-start.4 = (bf16[256,2048]{1,0:T(8,128)(2,1)}, bf16[256,2048]{1,0:T(8,128)(2,1)}, u32[]{:S(2)}, u32[]{:S(2)}) collective-permute-start(bf16[256,2048]{1,0:T(8,128)(2,1)} %get-tuple-element.6), channel_id=1, source_target_pairs={{0,8},{4,12},{8,0},{12,4},{16,24},{20,28},{24,16},{28,20},{1,9},{5... | collective-permute-start | bytes 3145736 | tf_op jit(solution)/shard_map/ppermute | solution.py:380
  26.4 7.5 %collective-permute-done.1 = bf16[2,256,512]{2,1,0:T(8,128)(2,1)} collective-permute-done((bf16[2,256,512]{2,1,0:T(8,128)(2,1)}, bf16[2,256,512]{2,1,0:T(8,128)(2,1)}, u32[]{:S(2)}, u32[]{:S(2)}) %collective-permute-start.1) | collective-permute-done | bytes 524320 | tf_op jit(solution)/shard_map/ppermute | solution.py:380
  33.9 1.1 bitcast_add_fusion.1
  35.0 2.2 %collective-permute-start.2 = (bf16[256,512]{1,0:T(8,128)(2,1)S(1)}, bf16[256,512]{1,0:T(8,128)(2,1)S(1)}, u32[]{:S(2)}, u32[]{:S(2)}) collective-permute-start(bf16[256,512]{1,0:T(8,128)(2,1)S(1)} %dynamic-slice_bitcast_fusion.2), channel_id=1, source_target_pairs={{0,16},{4,20},{8,24},{12,28},{16,0},{20,4},{24,8},{28,12},{1,17},{... | collective-permute-start | bytes 786440 | tf_op jit(solution)/shard_map/ppermute | solution.py:380
  37.2 11.5 %collective-permute-done.9.refs_7_ = bf16[256,2048]{1,0:T(8,128)(2,1)} collective-permute-done((bf16[256,2048]{1,0:T(8,128)(2,1)}, bf16[256,2048]{1,0:T(8,128)(2,1)}, u32[]{:S(2)}, u32[]{:S(2)}) %collective-permute-start.9) | collective-permute-done | bytes 1048608 | tf_op jit(solution)/shard_map/ppermute | solution.py:380
  48.7 7.7 %collective-permute-done.5.refs_3_ = bf16[256,2048]{1,0:T(8,128)(2,1)} collective-permute-done((bf16[256,2048]{1,0:T(8,128)(2,1)}, bf16[256,2048]{1,0:T(8,128)(2,1)}, u32[]{:S(2)}, u32[]{:S(2)}) %collective-permute-start.5) | collective-permute-done | bytes 1048608 | tf_op jit(solution)/shard_map/ppermute | solution.py:380
  56.4 2.1 %collective-permute-start.13 = (bf16[256,2048]{1,0:T(8,128)(2,1)}, bf16[256,2048]{1,0:T(8,128)(2,1)S(1)}, u32[]{:S(2)}, u32[]{:S(2)}) collective-permute-start(bf16[256,2048]{1,0:T(8,128)(2,1)} %collective-permute-done.9.refs_7_), channel_id=1, source_target_pairs={{0,8},{4,12},{8,0},{12,4},{16,24},{20,28},{24,16},{28,20},{1,9},{5... | collective-permute-start | bytes 3145736 | tf_op jit(solution)/shard_map/ppermute | solution.py:380
  58.4 12.7 %collective-permute-done.8.refs_6_ = bf16[256,2048]{1,0:T(8,128)(2,1)} collective-permute-done((bf16[256,2048]{1,0:T(8,128)(2,1)}, bf16[256,2048]{1,0:T(8,128)(2,1)}, u32[]{:S(2)}, u32[]{:S(2)}) %collective-permute-start.8) | collective-permute-done | bytes 1048608 | tf_op jit(solution)/shard_map/ppermute | solution.py:380
  71.2 7.7 %collective-permute-done.4.refs_2_ = bf16[256,2048]{1,0:T(8,128)(2,1)} collective-permute-done((bf16[256,2048]{1,0:T(8,128)(2,1)}, bf16[256,2048]{1,0:T(8,128)(2,1)}, u32[]{:S(2)}, u32[]{:S(2)}) %collective-permute-start.4) | collective-permute-done | bytes 1048608 | tf_op jit(solution)/shard_map/ppermute | solution.py:380
  78.8 2.1 %collective-permute-start.12 = (bf16[256,2048]{1,0:T(8,128)(2,1)}, bf16[256,2048]{1,0:T(8,128)(2,1)}, u32[]{:S(2)}, u32[]{:S(2)}) collective-permute-start(bf16[256,2048]{1,0:T(8,128)(2,1)} %collective-permute-done.4.refs_2_), channel_id=1, source_target_pairs={{0,16},{4,20},{8,24},{12,28},{16,0},{20,4},{24,8},{28,12},{1,17},{... | collective-permute-start | bytes 3145736 | tf_op jit(solution)/shard_map/ppermute | solution.py:380
  80.9 19.8 %collective-permute-done.13.refs_11_ = bf16[256,2048]{1,0:T(8,128)(2,1)S(1)} collective-permute-done((bf16[256,2048]{1,0:T(8,128)(2,1)}, bf16[256,2048]{1,0:T(8,128)(2,1)S(1)}, u32[]{:S(2)}, u32[]{:S(2)}) %collective-permute-start.13) | collective-permute-done | bytes 1048608 | tf_op jit(solution)/shard_map/ppermute | solution.py:380
  101.7 1.1 copy-done.4
  103.3 1.8 %collective-permute-done.12.refs_10_ = bf16[256,2048]{1,0:T(8,128)(2,1)} collective-permute-done((bf16[256,2048]{1,0:T(8,128)(2,1)}, bf16[256,2048]{1,0:T(8,128)(2,1)}, u32[]{:S(2)}, u32[]{:S(2)}) %collective-permute-start.12) | collective-permute-done | bytes 1048608 | tf_op jit(solution)/shard_map/ppermute | solution.py:380
  105.1 1.7 %bitcast_add_fusion.2.picked_ref = bf16[256,512]{1,0:T(8,128)(2,1)} fusion(bf16[256,512]{1,0:T(8,128)(2,1)S(1)} %collective-permute-done.2, bf16[2,256,512]{2,1,0:T(8,128)(2,1)} %copy-done.1, s32[]{:T(128)S(6)} %select_n.25), kind=kLoop, calls=%fused_computation.4 | loop fusion | flops 131072 | bytes 786436 | tf_op jit(solution)/shard_map/add | solution.py:394
  106.8 1.4 collective-permute-done.14.refs_12_
  108.2 50.4 %shard_map.38 = f32[256,128,128]{2,1,0:T(8,128)} custom-call(bf16[256,512]{1,0:T(8,128)(2,1)} %bitcast_add_fusion.2.picked_ref, bf16[65,128,256]{2,1,0:T(8,128)(2,1)} %constant.38.clone.tables_ref, bf16[512,2048]{1,0:T(8,128)(2,1)} %refs_0_.1, bf16[512,2048]{1,0:T(8,128)(2,1)} %collective-permute-done.3.refs_1_, ...), custom_call_target="tpu_custom_call" | custom-call | flops 4294967296 | bytes 33554432 | tf_op jit(solution)/shard_map/pallas_call | solution.py:356
  (29 shorter events, 4.1 us)
Async XLA Ops:
  12.6 2.9 %collective-permute-start = (bf16[2,2,256,512]{3,2,1,0:T(8,128)(2,1)S(1)}, bf16[2,2,256,512]{3,2,1,0:T(8,128)(2,1)}, u32[]{:S(2)}, u32[]{:S(2)}) collective-permute-start(bf16[2,2,256,512]{3,2,1,0:T(8,128)(2,1)S(1)} %dynamic-slice_bitcast_fusion), channel_id=1, source_target_pairs={{0,4},{4,0},{8,12},{12,8},{16,20},{20,16},{24,28},{28,24},{1,5},{5... | collective-permute-start | bytes 3145736 | tf_op jit(solution)/shard_map/ppermute | solution.py:380
  13.1 7.8 %copy-start = (bf16[512,2048]{1,0:T(8,128)(2,1)S(1)}, bf16[512,2048]{1,0:T(8,128)(2,1)}, u32[]{:S(2)}) copy-start(bf16[512,2048]{1,0:T(8,128)(2,1)} %refs_0_.1) | copy-start | bytes 6291460
  18.0 15.9 %collective-permute-start.1 = (bf16[2,256,512]{2,1,0:T(8,128)(2,1)}, bf16[2,256,512]{2,1,0:T(8,128)(2,1)}, u32[]{:S(2)}, u32[]{:S(2)}) collective-permute-start(bf16[2,256,512]{2,1,0:T(8,128)(2,1)} %dynamic-slice_bitcast_fusion.1), channel_id=1, source_target_pairs={{0,8},{4,12},{8,0},{12,4},{16,24},{20,28},{24,16},{28,20},{1,9},{5... | collective-permute-start | bytes 1572872 | tf_op jit(solution)/shard_map/ppermute | solution.py:380
  22.3 26.4 %collective-permute-start.9 = (bf16[256,2048]{1,0:T(8,128)(2,1)}, bf16[256,2048]{1,0:T(8,128)(2,1)}, u32[]{:S(2)}, u32[]{:S(2)}) collective-permute-start(bf16[256,2048]{1,0:T(8,128)(2,1)} %get-tuple-element.5), channel_id=1, source_target_pairs={{0,16},{4,20},{8,24},{12,28},{16,0},{20,4},{24,8},{28,12},{1,17},{... | collective-permute-start | bytes 3145736 | tf_op jit(solution)/shard_map/ppermute | solution.py:380
  23.8 32.5 %collective-permute-start.5 = (bf16[256,2048]{1,0:T(8,128)(2,1)}, bf16[256,2048]{1,0:T(8,128)(2,1)}, u32[]{:S(2)}, u32[]{:S(2)}) collective-permute-start(bf16[256,2048]{1,0:T(8,128)(2,1)} %get-tuple-element.5), channel_id=1, source_target_pairs={{0,8},{4,12},{8,0},{12,4},{16,24},{20,28},{24,16},{28,20},{1,9},{5... | collective-permute-start | bytes 3145736 | tf_op jit(solution)/shard_map/ppermute | solution.py:380
  24.4 46.8 %collective-permute-start.8 = (bf16[256,2048]{1,0:T(8,128)(2,1)}, bf16[256,2048]{1,0:T(8,128)(2,1)}, u32[]{:S(2)}, u32[]{:S(2)}) collective-permute-start(bf16[256,2048]{1,0:T(8,128)(2,1)} %get-tuple-element.6), channel_id=1, source_target_pairs={{0,16},{4,20},{8,24},{12,28},{16,0},{20,4},{24,8},{28,12},{1,17},{... | collective-permute-start | bytes 3145736 | tf_op jit(solution)/shard_map/ppermute | solution.py:380
  24.4 54.4 %collective-permute-start.4 = (bf16[256,2048]{1,0:T(8,128)(2,1)}, bf16[256,2048]{1,0:T(8,128)(2,1)}, u32[]{:S(2)}, u32[]{:S(2)}) collective-permute-start(bf16[256,2048]{1,0:T(8,128)(2,1)} %get-tuple-element.6), channel_id=1, source_target_pairs={{0,8},{4,12},{8,0},{12,4},{16,24},{20,28},{24,16},{28,20},{1,9},{5... | collective-permute-start | bytes 3145736 | tf_op jit(solution)/shard_map/ppermute | solution.py:380
  35.0 13.7 %copy-start.1 = (bf16[2,256,512]{2,1,0:T(8,128)(2,1)}, bf16[2,256,512]{2,1,0:T(8,128)(2,1)S(1)}, u32[]{:S(2)}) copy-start(bf16[2,256,512]{2,1,0:T(8,128)(2,1)S(1)} %bitcast_add_fusion.1) | copy-start | bytes 1572868
  35.0 43.8 %collective-permute-start.2 = (bf16[256,512]{1,0:T(8,128)(2,1)S(1)}, bf16[256,512]{1,0:T(8,128)(2,1)S(1)}, u32[]{:S(2)}, u32[]{:S(2)}) collective-permute-start(bf16[256,512]{1,0:T(8,128)(2,1)S(1)} %dynamic-slice_bitcast_fusion.2), channel_id=1, source_target_pairs={{0,16},{4,20},{8,24},{12,28},{16,0},{20,4},{24,8},{28,12},{1,17},{... | collective-permute-start | bytes 786440 | tf_op jit(solution)/shard_map/ppermute | solution.py:380
  48.7 58.1 %collective-permute-start.3 = (bf16[512,2048]{1,0:T(8,128)(2,1)S(1)}, bf16[512,2048]{1,0:T(8,128)(2,1)}, u32[]{:S(2)}, u32[]{:S(2)}) collective-permute-start(bf16[512,2048]{1,0:T(8,128)(2,1)S(1)} %copy-done), channel_id=1, source_target_pairs={{0,4},{4,0},{8,12},{12,8},{16,20},{20,16},{24,28},{28,24},{1,5},{5... | collective-permute-start | bytes 6291464 | tf_op jit(solution)/shard_map/ppermute | solution.py:380
  56.4 44.4 %collective-permute-start.13 = (bf16[256,2048]{1,0:T(8,128)(2,1)}, bf16[256,2048]{1,0:T(8,128)(2,1)S(1)}, u32[]{:S(2)}, u32[]{:S(2)}) collective-permute-start(bf16[256,2048]{1,0:T(8,128)(2,1)} %collective-permute-done.9.refs_7_), channel_id=1, source_target_pairs={{0,8},{4,12},{8,0},{12,4},{16,24},{20,28},{24,16},{28,20},{1,9},{5... | collective-permute-start | bytes 3145736 | tf_op jit(solution)/shard_map/ppermute | solution.py:380
  71.2 29.6 %collective-permute-start.11 = (bf16[256,2048]{1,0:T(8,128)(2,1)}, bf16[256,2048]{1,0:T(8,128)(2,1)S(1)}, u32[]{:S(2)}, u32[]{:S(2)}) collective-permute-start(bf16[256,2048]{1,0:T(8,128)(2,1)} %collective-permute-done.9.refs_7_), channel_id=1, source_target_pairs={{0,4},{4,0},{8,12},{12,8},{16,20},{20,16},{24,28},{28,24},{1,5},{5... | collective-permute-start | bytes 3145736 | tf_op jit(solution)/shard_map/ppermute | solution.py:380
  78.8 22.9 %collective-permute-start.7 = (bf16[256,2048]{1,0:T(8,128)(2,1)}, bf16[256,2048]{1,0:T(8,128)(2,1)S(1)}, u32[]{:S(2)}, u32[]{:S(2)}) collective-permute-start(bf16[256,2048]{1,0:T(8,128)(2,1)} %collective-permute-done.5.refs_3_), channel_id=1, source_target_pairs={{0,4},{4,0},{8,12},{12,8},{16,20},{20,16},{24,28},{28,24},{1,5},{5... | collective-permute-start | bytes 3145736 | tf_op jit(solution)/shard_map/ppermute | solution.py:380
  78.8 26.2 %collective-permute-start.12 = (bf16[256,2048]{1,0:T(8,128)(2,1)}, bf16[256,2048]{1,0:T(8,128)(2,1)}, u32[]{:S(2)}, u32[]{:S(2)}) collective-permute-start(bf16[256,2048]{1,0:T(8,128)(2,1)} %collective-permute-done.4.refs_2_), channel_id=1, source_target_pairs={{0,16},{4,20},{8,24},{12,28},{16,0},{20,4},{24,8},{28,12},{1,17},{... | collective-permute-start | bytes 3145736 | tf_op jit(solution)/shard_map/ppermute | solution.py:380
  100.7 7.5 %copy-start.2 = (bf16[256,2048]{1,0:T(8,128)(2,1)}, bf16[256,2048]{1,0:T(8,128)(2,1)S(1)}, u32[]{:S(2)}) copy-start(bf16[256,2048]{1,0:T(8,128)(2,1)S(1)} %collective-permute-done.13.refs_11_) | copy-start | bytes 3145732
  100.7 6.1 %collective-permute-start.6 = (bf16[256,2048]{1,0:T(8,128)(2,1)}, bf16[256,2048]{1,0:T(8,128)(2,1)}, u32[]{:S(2)}, u32[]{:S(2)}) collective-permute-start(bf16[256,2048]{1,0:T(8,128)(2,1)} %collective-permute-done.4.refs_2_), channel_id=1, source_target_pairs={{0,4},{4,0},{8,12},{12,8},{16,20},{20,16},{24,28},{28,24},{1,5},{5... | collective-permute-start | bytes 3145736 | tf_op jit(solution)/shard_map/ppermute | solution.py:380
  100.7 1.0 copy-start.3
  100.7 6.0 %collective-permute-start.10 = (bf16[256,2048]{1,0:T(8,128)(2,1)}, bf16[256,2048]{1,0:T(8,128)(2,1)}, u32[]{:S(2)}, u32[]{:S(2)}) collective-permute-start(bf16[256,2048]{1,0:T(8,128)(2,1)} %collective-permute-done.8.refs_6_), channel_id=1, source_target_pairs={{0,4},{4,0},{8,12},{12,8},{16,20},{20,16},{24,28},{28,24},{1,5},{5... | collective-permute-start | bytes 3145736 | tf_op jit(solution)/shard_map/ppermute | solution.py:380
  101.7 1.1 copy-start.4
  102.8 4.0 %collective-permute-start.15 = (bf16[256,2048]{1,0:T(8,128)(2,1)S(1)}, bf16[256,2048]{1,0:T(8,128)(2,1)}, u32[]{:S(2)}, u32[]{:S(2)}) collective-permute-start(bf16[256,2048]{1,0:T(8,128)(2,1)S(1)} %collective-permute-done.13.refs_11_), channel_id=1, source_target_pairs={{0,4},{4,0},{8,12},{12,8},{16,20},{20,16},{24,28},{28,24},{1,5},{5... | collective-permute-start | bytes 3145736 | tf_op jit(solution)/shard_map/ppermute | solution.py:380
  105.1 3.1 %collective-permute-start.14 = (bf16[256,2048]{1,0:T(8,128)(2,1)}, bf16[256,2048]{1,0:T(8,128)(2,1)}, u32[]{:S(2)}, u32[]{:S(2)}) collective-permute-start(bf16[256,2048]{1,0:T(8,128)(2,1)} %collective-permute-done.12.refs_10_), channel_id=1, source_target_pairs={{0,4},{4,0},{8,12},{12,8},{16,20},{20,16},{24,28},{28,24},{1,5},{5... | collective-permute-start | bytes 3145736 | tf_op jit(solution)/shard_map/ppermute | solution.py:380

commit v2 on v1

--- a/solution.py
+++ b/solution.py
@@ -11,6 +11,7 @@
 
 SIDE = 128
 VMEM_BYTES = 60 * 2**20
+STAGES = 4
 
 
 def rotate(value, turn):
@@ -127,82 +128,113 @@
     return jnp.asarray(np.concatenate([high, low], axis=2))
 
 
-def pick_kernel(index_ref, orbitals_ref, out_ref):
-    points, cells = index_ref.shape[0], orbitals_ref.shape[1]
-    hot = lax.broadcasted_iota(jnp.int32, (points, cells), 1) == index_ref[...]
-    hot = jnp.where(hot, 1.0, 0.0).astype(jnp.bfloat16)
-    out_ref[...] = lax.dot_general(
-        hot, orbitals_ref[...], (((1,), (1,)), ((), ())), preferred_element_type=jnp.float32
-    ).astype(jnp.bfloat16)
-
-
-def pick_own(local_index, orbitals):
-    points, (orbital_count, cells) = local_index.shape[0], orbitals.shape
-    block = min(256, points)
-    return pl.pallas_call(
-        pick_kernel,
-        grid=(points // block,),
-        in_specs=[
-            pl.BlockSpec((block, 1), lambda i: (i, 0)),
-            pl.BlockSpec((orbital_count, cells), lambda i: (0, 0)),
-        ],
-        out_specs=pl.BlockSpec((block, orbital_count), lambda i: (i, 0)),
-        out_shape=jax.ShapeDtypeStruct((points, orbital_count), jnp.bfloat16),
-        compiler_params=pltpu.CompilerParams(vmem_limit_bytes=VMEM_BYTES),
-        cost_estimate=pl.CostEstimate(
-            flops=2 * points * orbital_count * cells,
-            bytes_accessed=2 * orbital_count * (cells + points),
-            transcendentals=0,
-        ),
-    )(local_index[:, None], orbitals)
-
-
-def sheet_kernel(layout, picked_ref, tables_ref, *refs):
-    count, parts_of = layout
-    arrays = refs[: -7]
-    out_ref, cells_ref, squared_ref, slots_ref, stage_ref, in_sem, out_sem = refs[-7:]
+def fetches(step, slot, apart, arrays, cells_ref, in_sem):
+    _, column, parts = step[2][apart]
+    width = step[1] * SIDE
+    return [
+        pltpu.make_async_copy(
+            arrays[which].at[:, pl.ds(column, width)],
+            cells_ref.at[slot, apart, pl.ds(first, size), pl.ds(0, width)],
+            in_sem.at[slot, apart],
+        )
+        for which, first, size in parts
+    ]
+
+
+def holder(step, apart):
+    even_mask, odd_mask = step[2][apart][0]
+    me, odd = lax.axis_index("grid"), lax.axis_index("pts") & 1
+    if even_mask == odd_mask:
+        return me ^ even_mask
+    return me ^ (even_mask ^ (odd * (even_mask ^ odd_mask)))
+
+
+def pick_from(step, apart, index_ref, cells):
+    width, count = step[1] * SIDE, len(step[2])
+    base = holder(step, apart) * (SIDE * SIDE // count) + step[0] * SIDE
+    shape = (index_ref.shape[0], width)
+    hot = lax.broadcasted_iota(jnp.int32, shape, 1) == index_ref[...] - base
+    return lax.dot_general(
+        jnp.where(hot, 1.0, 0.0).astype(jnp.bfloat16),
+        cells,
+        (((1,), (1,)), ((), ())),
+        preferred_element_type=jnp.float32,
+    )
+
+
+def pick_kernel(steps, index_ref, *refs):
+    *arrays, out_ref, cells_ref, total_ref, in_sem = refs
+    count = len(steps[0][2])
+
+    def start(at):
+        for apart in range(count):
+            for copy in fetches(steps[at], at % 2, apart, arrays, cells_ref, in_sem):
+                copy.start()
+
+    start(0)
+    total_ref[...] = jnp.zeros_like(total_ref)
+    for at, step in enumerate(steps):
+        if at + 1 < len(steps):
+            start(at + 1)
+        for apart in range(count):
+            for copy in fetches(step, at % 2, apart, arrays, cells_ref, in_sem):
+                copy.wait()
+            cells = cells_ref[at % 2, apart, :, : step[1] * SIDE]
+            total_ref[...] += pick_from(step, apart, index_ref, cells)
+    out_ref[...] = total_ref[...].astype(jnp.bfloat16)
+
+
+def sheet_kernel(steps, pick_first, index_ref, picked_ref, far_tables_ref, *refs):
+    *arrays, out_ref, chosen_ref, cells_ref, squared_ref, slots_ref, stage_ref = refs[:-4]
+    tables_ref, in_sem, out_sem, table_sem = refs[-4:]
+    table_copy = pltpu.make_async_copy(far_tables_ref, tables_ref, table_sem.at[0])
+    count = len(steps[0][2])
     rows = SIDE // count
     points = picked_ref.shape[0]
     half = count // 2
-    pair_rows = 2
-    steps = rows // pair_rows
-    me = lax.axis_index("grid")
-
-    def fetch(step, slot):
-        return [
-            pltpu.make_async_copy(
-                arrays[which].at[:, pl.ds(step * pair_rows * SIDE, pair_rows * SIDE)],
-                cells_ref.at[slot, apart, pl.ds(first, size), :],
-                in_sem.at[slot],
+    chunk = 8
+
+    def start(at):
+        for apart in range(count):
+            for copy in fetches(steps[at], at % 2, apart, arrays, cells_ref, in_sem):
+                copy.start()
+
+    def wait(at, apart):
+        for copy in fetches(steps[at], at % 2, apart, arrays, cells_ref, in_sem):
+            copy.wait()
+
+    for at in range(max(1, pick_first)):
+        start(at)
+    table_copy.start()
+    if pick_first:
+        total = picked_ref[...].astype(jnp.float32)
+        for at in range(pick_first):
+            for apart in range(count):
+                wait(at, apart)
+                cells = cells_ref[at, apart, :, : steps[at][1] * SIDE]
+                total += pick_from(steps[at], apart, index_ref, cells)
+        chosen_ref[...] = total.astype(jnp.bfloat16)
+    else:
+        chosen_ref[...] = picked_ref[...]
+
+    for at, step in enumerate(steps):
+        first_row, rows_here, _ = step
+        width = rows_here * SIDE
+        if max(1, pick_first) <= at + 1 < len(steps):
+            start(at + 1)
+        for apart in range(count):
+            if at >= pick_first:
+                wait(at, apart)
+            pair = jnp.dot(
+                chosen_ref[...],
+                cells_ref[at % 2, apart, :, :width],
+                preferred_element_type=jnp.float32,
             )
-            for apart, parts in enumerate(parts_of)
-            for which, first, size in parts
-        ]
-
-    for copy in fetch(0, 0):
-        copy.start()
-    for step in range(steps):
-        slot = step % 2
-        if step + 1 < steps:
-            for copy in fetch(step + 1, 1 - slot):
-                copy.start()
-        for copy in fetch(step, slot):
-            copy.wait()
-
-        def multiply(apart, carry):
-            pair = jnp.dot(
-                picked_ref[...], cells_ref[slot, apart], preferred_element_type=jnp.float32
-            )
-            squared_ref[me ^ apart] = pair * pair
-            return carry
-
-        lax.fori_loop(0, count, multiply, 0)
-        chunk = 8
-
-        def spread(at, carry):
-            here = pl.ds(pl.multiple_of(at * chunk, chunk), chunk)
-            for within in range(pair_rows):
-                j = step * pair_rows + within
+            squared_ref[holder(step, apart), :, :width] = pair * pair
+
+        def spread(here, first_row=first_row, rows_here=rows_here):
+            for within in range(rows_here):
+                j = first_row + within
                 lanes = pl.ds(within * SIDE, SIDE)
                 entries = real_dft([squared_ref[g, here, lanes] for g in range(count)])
                 slots_ref[0, j, here, :] = entries[0]
@@ -211,9 +243,14 @@
                     re, im = rotate(entries[k], -k * j / SIDE)
                     slots_ref[2 * k - 1, j, here, :] = re
                     slots_ref[2 * k, j, here, :] = im
+
+        def one(at_chunk, carry):
+            spread(pl.ds(pl.multiple_of(at_chunk * chunk, chunk), chunk))
             return carry
 
-        lax.fori_loop(0, points // chunk, spread, 0, unroll=2)
+        lax.fori_loop(0, points // chunk, one, 0)
+
+    table_copy.wait()
 
     def circulant(blocks, a):
         stacked = blocks[0] if len(blocks) == 1 else jnp.concatenate(blocks, axis=0)
@@ -227,14 +264,12 @@
         )
         return both[:, :SIDE] + both[:, SIDE:]
 
-    chunk = 8
-
-    def over_points(body):
+    def over_points(body, unroll):
         def one(at, carry):
             body(pl.ds(pl.multiple_of(at * chunk, chunk), chunk))
             return carry
 
-        lax.fori_loop(0, points // chunk, one, 0)
+        lax.fori_loop(0, points // chunk, one, 0, unroll=min(unroll, points // chunk))
 
     def apply(places, a):
         outs = circulant([slots_ref[s, j] for s, j in places], a)
@@ -256,12 +291,12 @@
         for j, value in enumerate(real_inverse(entries)):
             slots_ref[0, j, here, :] = value
 
-    over_points(real_there)
+    over_points(real_there, 4)
     apply([(0, 0)], 0)
     apply([(0, rows - 1)], SIDE // 2)
     for k in range(1, rows // 2):
         apply([(0, 2 * k - 1), (0, 2 * k)], count * k)
-    over_points(real_back)
+    over_points(real_back, 4)
 
     last = count - 1
     short = rows // 2
@@ -285,10 +320,10 @@
             slots_ref[last, j, here, :] = 2.0 * re
             slots_ref[last, j + short, here, :] = -2.0 * im
 
-    over_points(odd_there)
+    over_points(odd_there, 4)
     for k in range(short):
         apply([(last, 2 * k), (last, 2 * k + 1)], half + 2 * count * k)
-    over_points(odd_back)
+    over_points(odd_back, 4)
 
     for k in range(1, half):
         re_slot, im_slot = 2 * k - 1, 2 * k
@@ -302,10 +337,10 @@
                 slots_ref[re_slot, j, here, :] = re
                 slots_ref[im_slot, j, here, :] = im
 
-        over_points(complex_there)
+        over_points(complex_there, 4)
         for a2 in range(rows):
             apply([(re_slot, a2), (im_slot, a2)], k + count * a2)
-        over_points(functools.partial(complex_there, sign=1))
+        over_points(functools.partial(complex_there, sign=1), 4)
 
     def put(j, slot):
         return [
@@ -316,9 +351,9 @@
         ]
 
     for j in range(rows):
-        slot = j % 2
-        if j >= 2:
-            for copy in put(j - 2, slot):
+        slot = j % STAGES
+        if j >= STAGES:
+            for copy in put(j - STAGES, slot):
                 copy.wait()
 
         def gather_back(here):
@@ -334,45 +369,82 @@
             for g, value in enumerate(real_inverse(entries)):
                 stage_ref[slot, g, here, :] = value
 
-        over_points(gather_back)
+        over_points(gather_back, 4)
         for copy in put(j, slot):
             copy.start()
-    for j in range(max(rows - 2, 0), rows):
-        for copy in put(j, j % 2):
+    for j in range(max(rows - STAGES, 0), rows):
+        for copy in put(j, j % STAGES):
             copy.wait()
 
 
-def screen_sheets(picked, tables, shard_parts, count):
+VMEM_SPEC = pl.BlockSpec(memory_space=pltpu.VMEM)
+ANY_SPEC = pl.BlockSpec(memory_space=pl.ANY)
+
+
+def flatten(steps):
+    arrays, plan = [], []
+    for first_row, rows_here, entries in steps:
+        numbered = []
+        for masks, column, parts in entries:
+            for array, _ in parts:
+                if not any(array is known for known in arrays):
+                    arrays.append(array)
+            which = [next(i for i, known in enumerate(arrays) if known is array) for array, _ in parts]
+            numbered.append(
+                (masks, column, tuple((w, first, a.shape[0]) for w, (a, first) in zip(which, parts)))
+            )
+        plan.append((first_row, rows_here, tuple(numbered)))
+    return tuple(plan), arrays
+
+
+def cell_buffers(plan, orbital_count):
+    widest = max(rows_here for _, rows_here, _ in plan) * SIDE
+    return pltpu.VMEM((min(2, len(plan)), len(plan[0][2]), orbital_count, widest), jnp.bfloat16)
+
+
+def pick_cells(index, orbital_count, steps, us=0):
+    plan, arrays = flatten(steps)
+    count = len(plan[0][2])
+    shape = (index.shape[0], orbital_count)
+    return pl.pallas_call(
+        functools.partial(pick_kernel, plan),
+        in_specs=[VMEM_SPEC] + [ANY_SPEC] * len(arrays),
+        out_specs=VMEM_SPEC,
+        out_shape=jax.ShapeDtypeStruct(shape, jnp.bfloat16),
+        scratch_shapes=[
+            cell_buffers(plan, orbital_count),
+            pltpu.VMEM(shape, jnp.float32),
+            pltpu.SemaphoreType.DMA((2, count)),
+        ],
+        compiler_params=pltpu.CompilerParams(vmem_limit_bytes=VMEM_BYTES),
+        cost_estimate=pl.CostEstimate(flops=us * 5 * 10**8, bytes_accessed=0, transcendentals=0),
+    )(index, *arrays)
+
+
+def screen_sheets(index, picked, tables, steps, pick_first):
     points, orbital_count = picked.shape
-    arrays, parts_of = [], []
-    for parts in shard_parts:
-        entry = []
-        for array, first in parts:
-            entry.append((len(arrays), first, array.shape[0]))
-            arrays.append(array)
-        parts_of.append(tuple(entry))
+    plan, arrays = flatten(steps)
+    count = len(plan[0][2])
     rows = SIDE // count
-    vmem = pl.BlockSpec(memory_space=pltpu.VMEM)
+    widest = max(rows_here for _, rows_here, _ in plan) * SIDE
     return pl.pallas_call(
-        functools.partial(sheet_kernel, (count, tuple(parts_of))),
-        in_specs=[vmem, vmem] + [pl.BlockSpec(memory_space=pl.ANY)] * len(arrays),
-        out_specs=pl.BlockSpec(memory_space=pl.ANY),
+        functools.partial(sheet_kernel, plan, pick_first),
+        in_specs=[VMEM_SPEC] * 2 + [ANY_SPEC] * (1 + len(arrays)),
+        out_specs=ANY_SPEC,
         out_shape=jax.ShapeDtypeStruct((points, SIDE, SIDE), jnp.float32),
         scratch_shapes=[
-            pltpu.VMEM((2, count, orbital_count, 2 * SIDE), jnp.bfloat16),
-            pltpu.VMEM((count, points, 2 * SIDE), jnp.float32),
+            pltpu.VMEM((points, orbital_count), jnp.bfloat16),
+            cell_buffers(plan, orbital_count),
+            pltpu.VMEM((count, points, widest), jnp.float32),
             pltpu.VMEM((count, rows, points, SIDE), jnp.float32),
-            pltpu.VMEM((2, count, points, SIDE), jnp.float32),
-            pltpu.SemaphoreType.DMA((2,)),
-            pltpu.SemaphoreType.DMA((2,)),
+            pltpu.VMEM((STAGES, count, points, SIDE), jnp.float32),
+            pltpu.VMEM(tables.shape, tables.dtype),
+            pltpu.SemaphoreType.DMA((2, count)),
+            pltpu.SemaphoreType.DMA((STAGES,)),
+            pltpu.SemaphoreType.DMA((1,)),
         ],
         compiler_params=pltpu.CompilerParams(vmem_limit_bytes=VMEM_BYTES),
-        cost_estimate=pl.CostEstimate(
-            flops=2 * points * orbital_count * SIDE * SIDE,
-            bytes_accessed=points * SIDE * SIDE * 8,
-            transcendentals=0,
-        ),
-    )(picked, tables, *arrays)
+    )(index, picked, tables, *arrays)
 
 
 def swap(array, mask):
@@ -380,20 +452,22 @@
     return lax.ppermute(array, "grid", [(i, i ^ mask) for i in range(count)])
 
 
-def scatter_points(own, masks):
-    count = lax.axis_size("grid")
-    bits = count.bit_length() - 1
-    me = lax.axis_index("grid")
-    value = own.reshape((2,) * bits + (own.shape[0] // count, own.shape[1]))
-    left = list(range(bits))[::-1]
-    for bit in masks:
-        axis = left.index(bit)
-        mine = (me >> bit) & 1
-        keep = lax.dynamic_index_in_dim(value, mine, axis, keepdims=False)
-        send = lax.dynamic_index_in_dim(value, 1 - mine, axis, keepdims=False)
-        value = keep + swap(send, 1 << bit)
-        left.remove(bit)
-    return value
+def routes(bits):
+    cut = (bits - 1) // 2
+    links = list(range(1, bits))
+    return links, links[cut:] + links[:cut]
+
+
+class Order:
+    def __init__(self, seed):
+        self.token = seed
+
+    def start(self, move, array, *arguments):
+        array, _ = lax.optimization_barrier((array, self.token))
+        return move(array, *arguments)
+
+    def wait(self, *arrays):
+        self.token, *_ = lax.optimization_barrier((self.token, *arrays))
 
 
 def gather_cells(orbitals):
@@ -401,32 +475,109 @@
     bits = count.bit_length() - 1
     middle = orbitals.shape[0] // 2
     held = {0: [(orbitals, 0)]}
-    link_bits = list(range(1, bits))
-    cut = (len(link_bits) + 1) // 2
-    routes = (link_bits, link_bits[cut:] + link_bits[:cut])
     pieces = ({0: orbitals[:middle]}, {0: orbitals[middle:]})
-    for hop in range(len(link_bits)):
-        for route, have in zip(routes, pieces):
-            mask = 1 << route[hop]
+    for route, have in zip(routes(bits), pieces):
+        for bit in route:
             for known in sorted(have):
-                have[known | mask] = swap(have[known], mask)
+                have[known | 1 << bit] = swap(have[known], 1 << bit)
     for known in pieces[0]:
         if known:
             held[known] = [(pieces[0][known], 0), (pieces[1][known], middle)]
     for known in sorted(held):
         held[known | 1] = [(swap(array, 1), first) for array, first in held[known]]
-    return [held[d] for d in range(count)]
+    rows = SIDE // count
+    return [
+        (j, 1, [((d, d), j * SIDE, held[d]) for d in range(count)]) for j in range(rows)
+    ]
+
+
+CORE, NEAR, FAR = 1, 2, 4
+SCRIPT = ("F0", "F1", "B", "P0", "F2", "P1", "F3", "S0", "P2", "S1", "W", "X3", "V2", "P3", "S2", "K012:0", "S3")
+PIECE_ROWS = (4, 4, 4, 4)
+
+
+def exchange(array, masks, across):
+    count, planes = lax.axis_size("grid"), lax.axis_size("pts")
+    pairs = [
+        (g * planes + z, (g ^ masks[z & 1]) * planes + (z ^ across))
+        for g in range(count)
+        for z in range(planes)
+    ]
+    return lax.ppermute(array, ("grid", "pts"), pairs)
+
+
+def four_chips(orbitals, index, tables):
+    order = Order(index[:1])
+    ends = [sum(PIECE_ROWS[:p]) for p in range(len(PIECE_ROWS) + 1)]
+    first, far, core = {}, {}, {}
+
+    def send_first(p):
+        source = lax.optimization_barrier((orbitals, order.token))[0]
+        piece = source[:, ends[p] * SIDE : ends[p + 1] * SIDE]
+        first[p] = exchange(piece, (NEAR, FAR), 0)
+
+    def pass_on(p):
+        order.wait(first[p])
+        far[p] = (
+            order.start(exchange, first[p], (FAR, NEAR), 0),
+            order.start(exchange, first[p], (0, 0), 1),
+        )
+        core[p] = [order.start(swap, first[p], CORE)]
+
+    def share(p):
+        order.wait(*far[p])
+        core[p] += [order.start(swap, array, CORE) for array in far[p]]
+
+    def step(p):
+        order.wait(*core[p])
+        entry = [
+            ((0, 0), ends[p] * SIDE, [(orbitals, 0)]),
+            ((CORE, CORE), ends[p] * SIDE, [(sibling, 0)]),
+        ]
+        arrays = (first[p], *far[p])
+        for masks, array, other in zip(((NEAR, FAR), (NEAR | FAR,) * 2, (FAR, NEAR)), arrays, core[p]):
+            entry.append((masks, 0, [(array, 0)]))
+            entry.append((tuple(m | CORE for m in masks), 0, [(other, 0)]))
+        return (ends[p], PIECE_ROWS[p], entry)
+
+    steps, picks = {}, []
+    for word in SCRIPT:
+        op, arg = word[0], word[1:]
+        if op == "F":
+            send_first(int(arg))
+        elif op == "P":
+            pass_on(int(arg))
+        elif op == "S":
+            share(int(arg))
+        elif op == "V":
+            order.wait(*far[int(arg)])
+        elif op == "X":
+            order.wait(first[int(arg)])
+        elif op == "B":
+            sibling = order.start(swap, orbitals, CORE)
+        elif op == "W":
+            order.wait(sibling)
+        elif op == "K":
+            ids, cost = arg.split(":")
+            for p in ids:
+                steps[int(p)] = step(int(p))
+            picks.append(pick_cells(index, orbitals.shape[0], [steps[int(p)] for p in ids], int(cost)))
+            order.wait(picks[-1])
+    left = [step(p) for p in range(len(PIECE_ROWS)) if p not in steps]
+    picked = functools.reduce(lambda x, y: x + y, picks)
+    return screen_sheets(index, picked, tables, left + [steps[p] for p in sorted(steps)], len(left))
 
 
 def shards(orbitals, point_index):
-    cell_count = orbitals.shape[1]
     count = lax.axis_size("grid")
-    bits = count.bit_length() - 1
-    local_index = point_index - lax.axis_index("grid") * cell_count
-    shard_parts = gather_cells(orbitals)
-    own = pick_own(local_index, orbitals)
-    picked = scatter_points(own, list(range(bits)))
-    return screen_sheets(picked, circulant_tables(), shard_parts, count)[None]
+    points = point_index.shape[0] // count
+    index = lax.dynamic_slice_in_dim(point_index, lax.axis_index("grid") * points, points)[:, None]
+    tables = circulant_tables()
+    if count == 8 and lax.axis_size("pts") % 2 == 0:
+        return four_chips(orbitals, index, tables)[None]
+    steps = gather_cells(orbitals)
+    picked = pick_cells(index, orbitals.shape[0], steps)
+    return screen_sheets(index, picked, tables, steps, 0)[None]
 
 
 def solution(mesh):

time: 159 us -> 114 us (0.72)
  waiting for transfers between devices: 72.5 us -> 40.6 us
  Pallas kernels: 59.6 us -> 45.1 us
  starting transfers between devices: 14.7 us -> 21.2 us
  other arithmetic: 5.14 us -> 0 us
    ppermute x16 -> x13, waiting for transfers between devices: 72.5 us -> 2.71 us  [swap(): return lax.ppermute(array, 'grid', [(i, i ^ mask) for i in range(count)])]
    ppermute x0 -> x12, waiting for transfers between devices: none -> 37.9 us  [exchange(): return lax.ppermute(array, ('grid', 'pts'), pairs)]
    ppermute x0 -> x12, starting transfers between devices: none -> 18.9 us  [exchange(): return lax.ppermute(array, ('grid', 'pts'), pairs)]
    pallas_call x2, Pallas kernels: 59.6 us -> 45.1 us  [the longest x1 36.6 us: screen_sheets(): pl.pallas_call(functools.partial(sheet_kernel, plan, pick_first), in_spec...]
    ppermute x16 -> x13, starting transfers between devices: 14.7 us -> 2.32 us  [swap(): return lax.ppermute(array, 'grid', [(i, i ^ mask) for i in range(count)])]
    add x3 -> x0, other arithmetic: 4.44 us -> none  [scatter_points(): value = keep + swap(send, 1 << bit)]
    squeeze x3 -> x0, local copies, waits for them, and re-layouts: 2.17 us -> none  [scatter_points(): send = lax.dynamic_index_in_dim(value, 1 - mine, axis, keepdims=False)]
    unnamed x10 -> x40, local copies, waits for them, and re-layouts: 1.58 us -> 3.73 us
  transfers between devices with their start and end apart: 16 -> 25, of which waited for: 9 -> 11; matrix products, arithmetic and copies ran while one was open for 3% -> 1% of each run, Pallas kernels for 0% -> 7%
where the time goes in v2:
time: 114 us
  Pallas kernels  45.1 us (40%)
  waiting for transfers between devices  40.6 us (36%)
  starting transfers between devices  21.2 us (19%)
  local copies, waits for them, and re-layouts  6.79 us (6%)
    ppermute x12, waiting for transfers between devices, exchange(): return lax.ppermute(array, ('grid', 'pts'), pairs)  37.9 us
    pallas_call x1, Pallas kernels, screen_sheets(): pl.pallas_call(functools.partial(sheet_kernel, plan, pick_first), in_spec...  36.6 us
    ppermute x12, starting transfers between devices, exchange(): return lax.ppermute(array, ('grid', 'pts'), pairs)  18.9 us
    pallas_call x1, Pallas kernels, pick_cells(): pl.pallas_call(functools.partial(pick_kernel, plan), in_specs=[VMEM_SPEC]...  8.52 us
    unnamed x40, local copies, waits for them, and re-layouts  3.73 us
    ppermute x13, waiting for transfers between devices, swap(): return lax.ppermute(array, 'grid', [(i, i ^ mask) for i in range(count)])  2.71 us
    ppermute x13, starting transfers between devices, swap(): return lax.ppermute(array, 'grid', [(i, i ^ mask) for i in range(count)])  2.32 us
  transfers between devices with their start and end apart: 25, of which 11 were waited for; matrix products, arithmetic and copies ran while one was open for 1% of the time, Pallas kernels for 7%

profile of v2, /device:TPU:0, one launch (start us, length us, event | category | flops | bytes accessed | tf_op | source)
XLA Modules:
  0.0 114.0 jit_solution(537333125783075924)
XLA Ops:
  0.0 0.9 dynamic_slice.3
  0.9 1.3 %fusion = (bf16[512,512]{1,0:T(8,128)(2,1)S(1)}, bf16[512,512]{1,0:T(8,128)(2,1)S(1)}) fusion(bf16[512,2048]{1,0:T(8,128)(2,1)} %refs_0_.3), kind=kLoop, calls=%fused_computation | loop fusion | bytes 2097152 | tf_op jit(solution)/shard_map/slice | solution.py:516
  2.2 3.0 %collective-permute-start.1 = (bf16[512,512]{1,0:T(8,128)(2,1)S(1)}, bf16[512,512]{1,0:T(8,128)(2,1)S(1)}, u32[]{:S(2)}, u32[]{:S(2)}) collective-permute-start(bf16[512,512]{1,0:T(8,128)(2,1)S(1)} %get-tuple-element.66), channel_id=1, source_target_pairs={{0,8},{1,17},{2,10},{3,19},{4,12},{5,21},{6,14},{7,23},{8,0},{9,25... | collective-permute-start | bytes 1572872 | tf_op jit(solution)/shard_map/ppermute | solution.py:506
  5.4 12.6 %collective-permute-done.1.refs_2_.refs_8_ = bf16[512,512]{1,0:T(8,128)(2,1)S(1)} collective-permute-done((bf16[512,512]{1,0:T(8,128)(2,1)S(1)}, bf16[512,512]{1,0:T(8,128)(2,1)S(1)}, u32[]{:S(2)}, u32[]{:S(2)}) %collective-permute-start.1) | collective-permute-done | bytes 524320 | tf_op jit(solution)/shard_map/ppermute | solution.py:506
  17.9 2.1 %collective-permute-start.5 = (bf16[512,512]{1,0:T(8,128)(2,1)S(1)}, bf16[512,512]{1,0:T(8,128)(2,1)S(1)}, u32[]{:S(2)}, u32[]{:S(2)}) collective-permute-start(bf16[512,512]{1,0:T(8,128)(2,1)S(1)} %collective-permute-done.1.refs_2_.refs_8_), channel_id=1, source_target_pairs={{0,1},{1,0},{2,3},{3,2},{4,5},{5,4},{6,7},{7,6},{8,9},{9,8},{10,11... | collective-permute-start | bytes 1572872 | tf_op jit(solution)/shard_map/ppermute | solution.py:506
  20.1 1.5 %collective-permute-start.3 = (bf16[512,512]{1,0:T(8,128)(2,1)S(1)}, bf16[512,512]{1,0:T(8,128)(2,1)S(1)}, u32[]{:S(2)}, u32[]{:S(2)}) collective-permute-start(bf16[512,512]{1,0:T(8,128)(2,1)S(1)} %collective-permute-done.1.refs_2_.refs_8_), channel_id=1, source_target_pairs={{0,16},{1,9},{2,18},{3,11},{4,20},{5,13},{6,22},{7,15},{8,24},{9,1... | collective-permute-start | bytes 1572872 | tf_op jit(solution)/shard_map/ppermute | solution.py:506
  21.7 1.6 %collective-permute-start.10 = (bf16[512,512]{1,0:T(8,128)(2,1)S(1)}, bf16[512,512]{1,0:T(8,128)(2,1)}, u32[]{:S(2)}, u32[]{:S(2)}) collective-permute-start(bf16[512,512]{1,0:T(8,128)(2,1)S(1)} %slice.22), channel_id=1, source_target_pairs={{0,8},{1,17},{2,10},{3,19},{4,12},{5,21},{6,14},{7,23},{8,0},{9,25... | collective-permute-start | bytes 1572872 | tf_op jit(solution)/shard_map/ppermute | solution.py:506
  23.2 6.0 %collective-permute-done.4.refs_8_.refs_14_ = bf16[512,512]{1,0:T(8,128)(2,1)S(1)} collective-permute-done((bf16[512,512]{1,0:T(8,128)(2,1)S(1)}, bf16[512,512]{1,0:T(8,128)(2,1)S(1)}, u32[]{:S(2)}, u32[]{:S(2)}) %collective-permute-start.4) | collective-permute-done | bytes 524320 | tf_op jit(solution)/shard_map/ppermute | solution.py:506
  29.2 2.1 %collective-permute-start.11 = (bf16[512,512]{1,0:T(8,128)(2,1)S(1)}, bf16[512,512]{1,0:T(8,128)(2,1)S(1)}, u32[]{:S(2)}, u32[]{:S(2)}) collective-permute-start(bf16[512,512]{1,0:T(8,128)(2,1)S(1)} %collective-permute-done.4.refs_8_.refs_14_), channel_id=1, source_target_pairs={{0,1},{1,0},{2,3},{3,2},{4,5},{5,4},{6,7},{7,6},{8,9},{9,8},{10,11... | collective-permute-start | bytes 1572872 | tf_op jit(solution)/shard_map/ppermute | solution.py:506
  31.3 1.5 %collective-permute-start.9 = (bf16[512,512]{1,0:T(8,128)(2,1)S(1)}, bf16[512,512]{1,0:T(8,128)(2,1)S(1)}, u32[]{:S(2)}, u32[]{:S(2)}) collective-permute-start(bf16[512,512]{1,0:T(8,128)(2,1)S(1)} %collective-permute-done.4.refs_8_.refs_14_), channel_id=1, source_target_pairs={{0,16},{1,9},{2,18},{3,11},{4,20},{5,13},{6,22},{7,15},{8,24},{9,1... | collective-permute-start | bytes 1572872 | tf_op jit(solution)/shard_map/ppermute | solution.py:506
  33.0 6.7 %collective-permute-done.10.refs_14_.refs_20_ = bf16[512,512]{1,0:T(8,128)(2,1)} collective-permute-done((bf16[512,512]{1,0:T(8,128)(2,1)S(1)}, bf16[512,512]{1,0:T(8,128)(2,1)}, u32[]{:S(2)}, u32[]{:S(2)}) %collective-permute-start.10) | collective-permute-done | bytes 524320 | tf_op jit(solution)/shard_map/ppermute | solution.py:506
  39.7 1.7 %collective-permute-start.16 = (bf16[512,512]{1,0:T(8,128)(2,1)S(1)}, bf16[512,512]{1,0:T(8,128)(2,1)}, u32[]{:S(2)}, u32[]{:S(2)}) collective-permute-start(bf16[512,512]{1,0:T(8,128)(2,1)S(1)} %slice.23), channel_id=1, source_target_pairs={{0,8},{1,17},{2,10},{3,19},{4,12},{5,21},{6,14},{7,23},{8,0},{9,25... | collective-permute-start | bytes 1572872 | tf_op jit(solution)/shard_map/ppermute | solution.py:506
  41.5 1.6 %collective-permute-start.17 = (bf16[512,512]{1,0:T(8,128)(2,1)}, bf16[512,512]{1,0:T(8,128)(2,1)}, u32[]{:S(2)}, u32[]{:S(2)}) collective-permute-start(bf16[512,512]{1,0:T(8,128)(2,1)} %collective-permute-done.10.refs_14_.refs_20_), channel_id=1, source_target_pairs={{0,1},{1,0},{2,3},{3,2},{4,5},{5,4},{6,7},{7,6},{8,9},{9,8},{10,11... | collective-permute-start | bytes 1572872 | tf_op jit(solution)/shard_map/ppermute | solution.py:506
  43.0 1.5 %collective-permute-start.15 = (bf16[512,512]{1,0:T(8,128)(2,1)}, bf16[512,512]{1,0:T(8,128)(2,1)}, u32[]{:S(2)}, u32[]{:S(2)}) collective-permute-start(bf16[512,512]{1,0:T(8,128)(2,1)} %collective-permute-done.10.refs_14_.refs_20_), channel_id=1, source_target_pairs={{0,16},{1,9},{2,18},{3,11},{4,20},{5,13},{6,22},{7,15},{8,24},{9,1... | collective-permute-start | bytes 1572872 | tf_op jit(solution)/shard_map/ppermute | solution.py:506
  44.5 8.4 %collective-permute-done.16.refs_2_ = bf16[512,512]{1,0:T(8,128)(2,1)} collective-permute-done((bf16[512,512]{1,0:T(8,128)(2,1)S(1)}, bf16[512,512]{1,0:T(8,128)(2,1)}, u32[]{:S(2)}, u32[]{:S(2)}) %collective-permute-start.16) | collective-permute-done | bytes 524320 | tf_op jit(solution)/shard_map/ppermute | solution.py:506
  53.4 0.8 collective-permute-done.17.refs_18_.refs_24_
  54.3 1.3 %collective-permute-done.15.refs_16_.refs_22_ = bf16[512,512]{1,0:T(8,128)(2,1)} collective-permute-done((bf16[512,512]{1,0:T(8,128)(2,1)}, bf16[512,512]{1,0:T(8,128)(2,1)}, u32[]{:S(2)}, u32[]{:S(2)}) %collective-permute-start.15) | collective-permute-done | bytes 524320 | tf_op jit(solution)/shard_map/ppermute | solution.py:506
  55.6 1.3 %copy-done.1 = bf16[512,2048]{1,0:T(8,128)(2,1)} copy-done((bf16[512,2048]{1,0:T(8,128)(2,1)}, bf16[512,2048]{1,0:T(8,128)(2,1)S(1)}, u32[]{:S(2)}) %copy-start.1) | copy-done | bytes 2097176
  59.0 1.3 %collective-permute-start.21 = (bf16[512,512]{1,0:T(8,128)(2,1)}, bf16[512,512]{1,0:T(8,128)(2,1)}, u32[]{:S(2)}, u32[]{:S(2)}) collective-permute-start(bf16[512,512]{1,0:T(8,128)(2,1)} %collective-permute-done.16.refs_2_), channel_id=1, source_target_pairs={{0,16},{1,9},{2,18},{3,11},{4,20},{5,13},{6,22},{7,15},{8,24},{9,1... | collective-permute-start | bytes 1572872 | tf_op jit(solution)/shard_map/ppermute | solution.py:506
  60.3 0.8 copy.5.index_ref
  62.9 8.5 %shard_map.37.picked_ref = bf16[256,512]{1,0:T(8,128)(2,1)} custom-call(s32[256,1]{1,0:T(8,128)} %copy.5.index_ref, bf16[512,2048]{1,0:T(8,128)(2,1)} %refs_0_.3, bf16[512,2048]{1,0:T(8,128)(2,1)} %copy-done.1, bf16[512,512]{1,0:T(8,128)(2,1)} %copy-done.2, bf16[512,512]{1,0:T(8,128)(2,1)} %copy-done.8, bf16[512,512]{1,0:T(8,128)(2,1)} %copy-done.5, ...), custom_call_target="tpu_custom_call" | custom-call | tf_op jit(solution)/shard_map/pallas_call | solution.py:409
  71.5 1.4 %collective-permute-done.22.refs_6_ = bf16[512,512]{1,0:T(8,128)(2,1)} collective-permute-done((bf16[512,512]{1,0:T(8,128)(2,1)}, bf16[512,512]{1,0:T(8,128)(2,1)}, u32[]{:S(2)}, u32[]{:S(2)}) %collective-permute-start.22) | collective-permute-done | bytes 524320 | tf_op jit(solution)/shard_map/ppermute | solution.py:506
  74.0 1.6 %collective-permute-done.23.refs_5_ = bf16[512,512]{1,0:T(8,128)(2,1)S(1)} collective-permute-done((bf16[512,512]{1,0:T(8,128)(2,1)}, bf16[512,512]{1,0:T(8,128)(2,1)S(1)}, u32[]{:S(2)}, u32[]{:S(2)}) %collective-permute-start.23) | collective-permute-done | bytes 524320 | tf_op jit(solution)/shard_map/ppermute | solution.py:452
  77.3 36.6 %shard_map.38 = f32[256,128,128]{2,1,0:T(8,128)} custom-call(s32[256,1]{1,0:T(8,128)} %copy.5.index_ref, bf16[256,512]{1,0:T(8,128)(2,1)} %shard_map.37.picked_ref, bf16[65,128,256]{2,1,0:T(8,128)(2,1)} %constant.14.clone.far_tables_ref, bf16[512,2048]{1,0:T(8,128)(2,1)} %refs_0_.3, bf16[512,2048]{1,0:T(8,128)(2,1)} %copy-done.1, ...), custom_call_target="tpu_custom_call" | custom-call | tf_op jit(solution)/shard_map/pallas_call | solution.py:430
  (73 shorter events, 7.5 us)
Async XLA Ops:
  2.2 15.8 %collective-permute-start.1 = (bf16[512,512]{1,0:T(8,128)(2,1)S(1)}, bf16[512,512]{1,0:T(8,128)(2,1)S(1)}, u32[]{:S(2)}, u32[]{:S(2)}) collective-permute-start(bf16[512,512]{1,0:T(8,128)(2,1)S(1)} %get-tuple-element.66), channel_id=1, source_target_pairs={{0,8},{1,17},{2,10},{3,19},{4,12},{5,21},{6,14},{7,23},{8,0},{9,25... | collective-permute-start | bytes 1572872 | tf_op jit(solution)/shard_map/ppermute | solution.py:506
  5.2 50.4 %collective-permute-start = (bf16[512,2048]{1,0:T(8,128)(2,1)S(1)}, bf16[512,2048]{1,0:T(8,128)(2,1)S(1)}, u32[]{:S(2)}, u32[]{:S(2)}) collective-permute-start(bf16[512,2048]{1,0:T(8,128)(2,1)S(1)} %copy-done), channel_id=1, source_target_pairs={{0,4},{4,0},{8,12},{12,8},{16,20},{20,16},{24,28},{28,24},{1,5},{5... | collective-permute-start | bytes 6291464 | tf_op jit(solution)/shard_map/ppermute | solution.py:452
  5.2 24.0 %collective-permute-start.4 = (bf16[512,512]{1,0:T(8,128)(2,1)S(1)}, bf16[512,512]{1,0:T(8,128)(2,1)S(1)}, u32[]{:S(2)}, u32[]{:S(2)}) collective-permute-start(bf16[512,512]{1,0:T(8,128)(2,1)S(1)} %get-tuple-element.65), channel_id=1, source_target_pairs={{0,8},{1,17},{2,10},{3,19},{4,12},{5,21},{6,14},{7,23},{8,0},{9,25... | collective-permute-start | bytes 1572872 | tf_op jit(solution)/shard_map/ppermute | solution.py:506
  17.9 13.4 %collective-permute-start.5 = (bf16[512,512]{1,0:T(8,128)(2,1)S(1)}, bf16[512,512]{1,0:T(8,128)(2,1)S(1)}, u32[]{:S(2)}, u32[]{:S(2)}) collective-permute-start(bf16[512,512]{1,0:T(8,128)(2,1)S(1)} %collective-permute-done.1.refs_2_.refs_8_), channel_id=1, source_target_pairs={{0,1},{1,0},{2,3},{3,2},{4,5},{5,4},{6,7},{7,6},{8,9},{9,8},{10,11... | collective-permute-start | bytes 1572872 | tf_op jit(solution)/shard_map/ppermute | solution.py:506
  20.1 12.8 %collective-permute-start.3 = (bf16[512,512]{1,0:T(8,128)(2,1)S(1)}, bf16[512,512]{1,0:T(8,128)(2,1)S(1)}, u32[]{:S(2)}, u32[]{:S(2)}) collective-permute-start(bf16[512,512]{1,0:T(8,128)(2,1)S(1)} %collective-permute-done.1.refs_2_.refs_8_), channel_id=1, source_target_pairs={{0,16},{1,9},{2,18},{3,11},{4,20},{5,13},{6,22},{7,15},{8,24},{9,1... | collective-permute-start | bytes 1572872 | tf_op jit(solution)/shard_map/ppermute | solution.py:506
  21.7 18.0 %collective-permute-start.10 = (bf16[512,512]{1,0:T(8,128)(2,1)S(1)}, bf16[512,512]{1,0:T(8,128)(2,1)}, u32[]{:S(2)}, u32[]{:S(2)}) collective-permute-start(bf16[512,512]{1,0:T(8,128)(2,1)S(1)} %slice.22), channel_id=1, source_target_pairs={{0,8},{1,17},{2,10},{3,19},{4,12},{5,21},{6,14},{7,23},{8,0},{9,25... | collective-permute-start | bytes 1572872 | tf_op jit(solution)/shard_map/ppermute | solution.py:506
  29.2 12.3 %collective-permute-start.11 = (bf16[512,512]{1,0:T(8,128)(2,1)S(1)}, bf16[512,512]{1,0:T(8,128)(2,1)S(1)}, u32[]{:S(2)}, u32[]{:S(2)}) collective-permute-start(bf16[512,512]{1,0:T(8,128)(2,1)S(1)} %collective-permute-done.4.refs_8_.refs_14_), channel_id=1, source_target_pairs={{0,1},{1,0},{2,3},{3,2},{4,5},{5,4},{6,7},{7,6},{8,9},{9,8},{10,11... | collective-permute-start | bytes 1572872 | tf_op jit(solution)/shard_map/ppermute | solution.py:506
  31.3 11.7 %collective-permute-start.9 = (bf16[512,512]{1,0:T(8,128)(2,1)S(1)}, bf16[512,512]{1,0:T(8,128)(2,1)S(1)}, u32[]{:S(2)}, u32[]{:S(2)}) collective-permute-start(bf16[512,512]{1,0:T(8,128)(2,1)S(1)} %collective-permute-done.4.refs_8_.refs_14_), channel_id=1, source_target_pairs={{0,16},{1,9},{2,18},{3,11},{4,20},{5,13},{6,22},{7,15},{8,24},{9,1... | collective-permute-start | bytes 1572872 | tf_op jit(solution)/shard_map/ppermute | solution.py:506
  32.9 20.0 %collective-permute-start.2 = (bf16[512,512]{1,0:T(8,128)(2,1)S(1)}, bf16[512,512]{1,0:T(8,128)(2,1)S(1)}, u32[]{:S(2)}, u32[]{:S(2)}) collective-permute-start(bf16[512,512]{1,0:T(8,128)(2,1)S(1)} %collective-permute-done.1.refs_2_.refs_8_), channel_id=1, source_target_pairs={{0,4},{4,0},{8,12},{12,8},{16,20},{20,16},{24,28},{28,24},{1,5},{5... | collective-permute-start | bytes 1572872 | tf_op jit(solution)/shard_map/ppermute | solution.py:452
  39.7 13.2 %collective-permute-start.16 = (bf16[512,512]{1,0:T(8,128)(2,1)S(1)}, bf16[512,512]{1,0:T(8,128)(2,1)}, u32[]{:S(2)}, u32[]{:S(2)}) collective-permute-start(bf16[512,512]{1,0:T(8,128)(2,1)S(1)} %slice.23), channel_id=1, source_target_pairs={{0,8},{1,17},{2,10},{3,19},{4,12},{5,21},{6,14},{7,23},{8,0},{9,25... | collective-permute-start | bytes 1572872 | tf_op jit(solution)/shard_map/ppermute | solution.py:506
  41.5 12.8 %collective-permute-start.17 = (bf16[512,512]{1,0:T(8,128)(2,1)}, bf16[512,512]{1,0:T(8,128)(2,1)}, u32[]{:S(2)}, u32[]{:S(2)}) collective-permute-start(bf16[512,512]{1,0:T(8,128)(2,1)} %collective-permute-done.10.refs_14_.refs_20_), channel_id=1, source_target_pairs={{0,1},{1,0},{2,3},{3,2},{4,5},{5,4},{6,7},{7,6},{8,9},{9,8},{10,11... | collective-permute-start | bytes 1572872 | tf_op jit(solution)/shard_map/ppermute | solution.py:506
  43.0 12.5 %collective-permute-start.15 = (bf16[512,512]{1,0:T(8,128)(2,1)}, bf16[512,512]{1,0:T(8,128)(2,1)}, u32[]{:S(2)}, u32[]{:S(2)}) collective-permute-start(bf16[512,512]{1,0:T(8,128)(2,1)} %collective-permute-done.10.refs_14_.refs_20_), channel_id=1, source_target_pairs={{0,16},{1,9},{2,18},{3,11},{4,20},{5,13},{6,22},{7,15},{8,24},{9,1... | collective-permute-start | bytes 1572872 | tf_op jit(solution)/shard_map/ppermute | solution.py:506
  52.9 4.6 %collective-permute-start.8 = (bf16[512,512]{1,0:T(8,128)(2,1)S(1)}, bf16[512,512]{1,0:T(8,128)(2,1)S(1)}, u32[]{:S(2)}, u32[]{:S(2)}) collective-permute-start(bf16[512,512]{1,0:T(8,128)(2,1)S(1)} %collective-permute-done.4.refs_8_.refs_14_), channel_id=1, source_target_pairs={{0,4},{4,0},{8,12},{12,8},{16,20},{20,16},{24,28},{28,24},{1,5},{5... | collective-permute-start | bytes 1572872 | tf_op jit(solution)/shard_map/ppermute | solution.py:452
  52.9 4.6 %collective-permute-start.6 = (bf16[512,512]{1,0:T(8,128)(2,1)S(1)}, bf16[512,512]{1,0:T(8,128)(2,1)S(1)}, u32[]{:S(2)}, u32[]{:S(2)}) collective-permute-start(bf16[512,512]{1,0:T(8,128)(2,1)S(1)} %collective-permute-done.3.refs_4_.refs_10_), channel_id=1, source_target_pairs={{0,4},{4,0},{8,12},{12,8},{16,20},{20,16},{24,28},{28,24},{1,5},{5... | collective-permute-start | bytes 1572872 | tf_op jit(solution)/shard_map/ppermute | solution.py:452
  54.3 3.8 %collective-permute-start.7 = (bf16[512,512]{1,0:T(8,128)(2,1)S(1)}, bf16[512,512]{1,0:T(8,128)(2,1)S(1)}, u32[]{:S(2)}, u32[]{:S(2)}) collective-permute-start(bf16[512,512]{1,0:T(8,128)(2,1)S(1)} %collective-permute-done.5.refs_6_.refs_12_), channel_id=1, source_target_pairs={{0,4},{4,0},{8,12},{12,8},{16,20},{20,16},{24,28},{28,24},{1,5},{5... | collective-permute-start | bytes 1572872 | tf_op jit(solution)/shard_map/ppermute | solution.py:452
  55.6 2.6 %collective-permute-start.12 = (bf16[512,512]{1,0:T(8,128)(2,1)S(1)}, bf16[512,512]{1,0:T(8,128)(2,1)S(1)}, u32[]{:S(2)}, u32[]{:S(2)}) collective-permute-start(bf16[512,512]{1,0:T(8,128)(2,1)S(1)} %collective-permute-done.9.refs_10_.refs_16_), channel_id=1, source_target_pairs={{0,4},{4,0},{8,12},{12,8},{16,20},{20,16},{24,28},{28,24},{1,5},{5... | collective-permute-start | bytes 1572872 | tf_op jit(solution)/shard_map/ppermute | solution.py:452
  57.5 3.7 %collective-permute-start.14 = (bf16[512,512]{1,0:T(8,128)(2,1)}, bf16[512,512]{1,0:T(8,128)(2,1)S(1)}, u32[]{:S(2)}, u32[]{:S(2)}) collective-permute-start(bf16[512,512]{1,0:T(8,128)(2,1)} %collective-permute-done.10.refs_14_.refs_20_), channel_id=1, source_target_pairs={{0,4},{4,0},{8,12},{12,8},{16,20},{20,16},{24,28},{28,24},{1,5},{5... | collective-permute-start | bytes 1572872 | tf_op jit(solution)/shard_map/ppermute | solution.py:452
  57.6 3.6 %collective-permute-start.18 = (bf16[512,512]{1,0:T(8,128)(2,1)}, bf16[512,512]{1,0:T(8,128)(2,1)S(1)}, u32[]{:S(2)}, u32[]{:S(2)}) collective-permute-start(bf16[512,512]{1,0:T(8,128)(2,1)} %collective-permute-done.15.refs_16_.refs_22_), channel_id=1, source_target_pairs={{0,4},{4,0},{8,12},{12,8},{16,20},{20,16},{24,28},{28,24},{1,5},{5... | collective-permute-start | bytes 1572872 | tf_op jit(solution)/shard_map/ppermute | solution.py:452
  58.1 3.4 %collective-permute-start.19 = (bf16[512,512]{1,0:T(8,128)(2,1)}, bf16[512,512]{1,0:T(8,128)(2,1)S(1)}, u32[]{:S(2)}, u32[]{:S(2)}) collective-permute-start(bf16[512,512]{1,0:T(8,128)(2,1)} %collective-permute-done.17.refs_18_.refs_24_), channel_id=1, source_target_pairs={{0,4},{4,0},{8,12},{12,8},{16,20},{20,16},{24,28},{28,24},{1,5},{5... | collective-permute-start | bytes 1572872 | tf_op jit(solution)/shard_map/ppermute | solution.py:452
  58.2 14.6 %collective-permute-start.22 = (bf16[512,512]{1,0:T(8,128)(2,1)}, bf16[512,512]{1,0:T(8,128)(2,1)}, u32[]{:S(2)}, u32[]{:S(2)}) collective-permute-start(bf16[512,512]{1,0:T(8,128)(2,1)} %collective-permute-done.16.refs_2_), channel_id=1, source_target_pairs={{0,1},{1,0},{2,3},{3,2},{4,5},{5,4},{6,7},{7,6},{8,9},{9,8},{10,11... | collective-permute-start | bytes 1572872 | tf_op jit(solution)/shard_map/ppermute | solution.py:506
  59.0 14.5 %collective-permute-start.21 = (bf16[512,512]{1,0:T(8,128)(2,1)}, bf16[512,512]{1,0:T(8,128)(2,1)}, u32[]{:S(2)}, u32[]{:S(2)}) collective-permute-start(bf16[512,512]{1,0:T(8,128)(2,1)} %collective-permute-done.16.refs_2_), channel_id=1, source_target_pairs={{0,16},{1,9},{2,18},{3,11},{4,20},{5,13},{6,22},{7,15},{8,24},{9,1... | collective-permute-start | bytes 1572872 | tf_op jit(solution)/shard_map/ppermute | solution.py:506
  61.1 12.9 %collective-permute-start.20 = (bf16[512,512]{1,0:T(8,128)(2,1)}, bf16[512,512]{1,0:T(8,128)(2,1)S(1)}, u32[]{:S(2)}, u32[]{:S(2)}) collective-permute-start(bf16[512,512]{1,0:T(8,128)(2,1)} %collective-permute-done.16.refs_2_), channel_id=1, source_target_pairs={{0,4},{4,0},{8,12},{12,8},{16,20},{20,16},{24,28},{28,24},{1,5},{5... | collective-permute-start | bytes 1572872 | tf_op jit(solution)/shard_map/ppermute | solution.py:452
  73.5 2.1 %collective-permute-start.23 = (bf16[512,512]{1,0:T(8,128)(2,1)}, bf16[512,512]{1,0:T(8,128)(2,1)S(1)}, u32[]{:S(2)}, u32[]{:S(2)}) collective-permute-start(bf16[512,512]{1,0:T(8,128)(2,1)} %collective-permute-done.21.refs_4_), channel_id=1, source_target_pairs={{0,4},{4,0},{8,12},{12,8},{16,20},{20,16},{24,28},{28,24},{1,5},{5... | collective-permute-start | bytes 1572872 | tf_op jit(solution)/shard_map/ppermute | solution.py:452
  73.5 2.9 %collective-permute-start.24 = (bf16[512,512]{1,0:T(8,128)(2,1)}, bf16[512,512]{1,0:T(8,128)(2,1)S(1)}, u32[]{:S(2)}, u32[]{:S(2)}) collective-permute-start(bf16[512,512]{1,0:T(8,128)(2,1)} %collective-permute-done.22.refs_6_), channel_id=1, source_target_pairs={{0,4},{4,0},{8,12},{12,8},{16,20},{20,16},{24,28},{28,24},{1,5},{5... | collective-permute-start | bytes 1572872 | tf_op jit(solution)/shard_map/ppermute | solution.py:452
  (21 other events, 194.7 us)

commit v3 on v2

--- a/solution.py
+++ b/solution.py
@@ -10,7 +10,7 @@
 from jax.sharding import PartitionSpec as P
 
 SIDE = 128
-VMEM_BYTES = 60 * 2**20
+VMEM_BYTES = 63 * 2**20
 STAGES = 4
 
 
@@ -248,7 +248,7 @@
             spread(pl.ds(pl.multiple_of(at_chunk * chunk, chunk), chunk))
             return carry
 
-        lax.fori_loop(0, points // chunk, one, 0)
+        lax.fori_loop(0, points // chunk, one, 0, unroll=min(2, points // chunk))
 
     table_copy.wait()
 
@@ -272,9 +272,9 @@
         lax.fori_loop(0, points // chunk, one, 0, unroll=min(unroll, points // chunk))
 
     def apply(places, a):
-        outs = circulant([slots_ref[s, j] for s, j in places], a)
+        outs = circulant([slots_ref[s, j, :points, :] for s, j in places], a)
         for at, (s, j) in enumerate(places):
-            slots_ref[s, j] = outs[at * points : (at + 1) * points]
+            slots_ref[s, j, :points, :] = outs[at * points : (at + 1) * points]
 
     def real_there(here):
         entries = real_dft([slots_ref[0, j, here, :] for j in range(rows)])
@@ -436,7 +436,7 @@
             pltpu.VMEM((points, orbital_count), jnp.bfloat16),
             cell_buffers(plan, orbital_count),
             pltpu.VMEM((count, points, widest), jnp.float32),
-            pltpu.VMEM((count, rows, points, SIDE), jnp.float32),
+            pltpu.VMEM((count, rows, points + 8, SIDE), jnp.float32),
             pltpu.VMEM((STAGES, count, points, SIDE), jnp.float32),
             pltpu.VMEM(tables.shape, tables.dtype),
             pltpu.SemaphoreType.DMA((2, count)),
@@ -506,8 +506,8 @@
     return lax.ppermute(array, ("grid", "pts"), pairs)
 
 
-def four_chips(orbitals, index, tables):
-    order = Order(index[:1])
+def four_chips(orbitals, index, seed, tables):
+    order = Order(seed)
     ends = [sum(PIECE_ROWS[:p]) for p in range(len(PIECE_ROWS) + 1)]
     first, far, core = {}, {}, {}
 
@@ -574,7 +574,7 @@
     index = lax.dynamic_slice_in_dim(point_index, lax.axis_index("grid") * points, points)[:, None]
     tables = circulant_tables()
     if count == 8 and lax.axis_size("pts") % 2 == 0:
-        return four_chips(orbitals, index, tables)[None]
+        return four_chips(orbitals, index, point_index[:1], tables)[None]
     steps = gather_cells(orbitals)
     picked = pick_cells(index, orbitals.shape[0], steps)
     return screen_sheets(index, picked, tables, steps, 0)[None]

time: 114 us -> 111 us (0.974)
  Pallas kernels: 45.1 us -> 43 us
  local copies, waits for them, and re-layouts: 6.79 us -> 5.09 us
    pallas_call x1, Pallas kernels: 36.6 us -> 34.5 us  [screen_sheets(): pl.pallas_call(functools.partial(sheet_kernel, plan, pick_first), in_spec...]
    unnamed x40 -> x32, local copies, waits for them, and re-layouts: 3.73 us -> 2.04 us
  transfers between devices with their start and end apart: 25 -> 25, of which waited for: 11 -> 11; matrix products, arithmetic and copies ran while one was open for 1% -> 1% of each run, Pallas kernels for 7% -> 8%
where the time goes in v3:
time: 111 us
  Pallas kernels  43 us (39%)
  waiting for transfers between devices  40.8 us (37%)
  starting transfers between devices  21.5 us (19%)
  local copies, waits for them, and re-layouts  5.09 us (5%)
    ppermute x12, waiting for transfers between devices, exchange(): return lax.ppermute(array, ('grid', 'pts'), pairs)  38.3 us
    pallas_call x1, Pallas kernels, screen_sheets(): pl.pallas_call(functools.partial(sheet_kernel, plan, pick_first), in_spec...  34.5 us
    ppermute x12, starting transfers between devices, exchange(): return lax.ppermute(array, ('grid', 'pts'), pairs)  19.2 us
    pallas_call x1, Pallas kernels, pick_cells(): pl.pallas_call(functools.partial(pick_kernel, plan), in_specs=[VMEM_SPEC]...  8.53 us
    ppermute x13, waiting for transfers between devices, swap(): return lax.ppermute(array, 'grid', [(i, i ^ mask) for i in range(count)])  2.52 us
    ppermute x13, starting transfers between devices, swap(): return lax.ppermute(array, 'grid', [(i, i ^ mask) for i in range(count)])  2.32 us
  transfers between devices with their start and end apart: 25, of which 11 were waited for; matrix products, arithmetic and copies ran while one was open for 1% of the time, Pallas kernels for 8%

profile of v3, /device:TPU:0, one launch (start us, length us, event | category | flops | bytes accessed | tf_op | source)
XLA Modules:
  0.0 110.7 jit_solution(17552362059452985164)
XLA Ops:
  0.0 1.4 %fusion = (bf16[512,512]{1,0:T(8,128)(2,1)S(1)}, bf16[512,512]{1,0:T(8,128)(2,1)S(1)}) fusion(bf16[512,2048]{1,0:T(8,128)(2,1)} %refs_0_.3), kind=kLoop, calls=%fused_computation | loop fusion | bytes 2097152 | tf_op jit(solution)/shard_map/slice | solution.py:516
  1.4 3.0 %collective-permute-start.1 = (bf16[512,512]{1,0:T(8,128)(2,1)S(1)}, bf16[512,512]{1,0:T(8,128)(2,1)S(1)}, u32[]{:S(2)}, u32[]{:S(2)}) collective-permute-start(bf16[512,512]{1,0:T(8,128)(2,1)S(1)} %get-tuple-element.66), channel_id=1, source_target_pairs={{0,8},{1,17},{2,10},{3,19},{4,12},{5,21},{6,14},{7,23},{8,0},{9,25... | collective-permute-start | bytes 1572872 | tf_op jit(solution)/shard_map/ppermute | solution.py:506
  4.9 12.3 %collective-permute-done.1.refs_2_.refs_8_ = bf16[512,512]{1,0:T(8,128)(2,1)S(1)} collective-permute-done((bf16[512,512]{1,0:T(8,128)(2,1)S(1)}, bf16[512,512]{1,0:T(8,128)(2,1)S(1)}, u32[]{:S(2)}, u32[]{:S(2)}) %collective-permute-start.1) | collective-permute-done | bytes 524320 | tf_op jit(solution)/shard_map/ppermute | solution.py:506
  17.2 2.1 %collective-permute-start.5 = (bf16[512,512]{1,0:T(8,128)(2,1)S(1)}, bf16[512,512]{1,0:T(8,128)(2,1)S(1)}, u32[]{:S(2)}, u32[]{:S(2)}) collective-permute-start(bf16[512,512]{1,0:T(8,128)(2,1)S(1)} %collective-permute-done.1.refs_2_.refs_8_), channel_id=1, source_target_pairs={{0,1},{1,0},{2,3},{3,2},{4,5},{5,4},{6,7},{7,6},{8,9},{9,8},{10,11... | collective-permute-start | bytes 1572872 | tf_op jit(solution)/shard_map/ppermute | solution.py:506
  19.3 1.5 %collective-permute-start.3 = (bf16[512,512]{1,0:T(8,128)(2,1)S(1)}, bf16[512,512]{1,0:T(8,128)(2,1)S(1)}, u32[]{:S(2)}, u32[]{:S(2)}) collective-permute-start(bf16[512,512]{1,0:T(8,128)(2,1)S(1)} %collective-permute-done.1.refs_2_.refs_8_), channel_id=1, source_target_pairs={{0,16},{1,9},{2,18},{3,11},{4,20},{5,13},{6,22},{7,15},{8,24},{9,1... | collective-permute-start | bytes 1572872 | tf_op jit(solution)/shard_map/ppermute | solution.py:506
  20.9 1.6 %collective-permute-start.10 = (bf16[512,512]{1,0:T(8,128)(2,1)S(1)}, bf16[512,512]{1,0:T(8,128)(2,1)S(1)}, u32[]{:S(2)}, u32[]{:S(2)}) collective-permute-start(bf16[512,512]{1,0:T(8,128)(2,1)S(1)} %slice.18), channel_id=1, source_target_pairs={{0,8},{1,17},{2,10},{3,19},{4,12},{5,21},{6,14},{7,23},{8,0},{9,25... | collective-permute-start | bytes 1572872 | tf_op jit(solution)/shard_map/ppermute | solution.py:506
  22.4 6.0 %collective-permute-done.4.refs_8_.refs_14_ = bf16[512,512]{1,0:T(8,128)(2,1)S(1)} collective-permute-done((bf16[512,512]{1,0:T(8,128)(2,1)S(1)}, bf16[512,512]{1,0:T(8,128)(2,1)S(1)}, u32[]{:S(2)}, u32[]{:S(2)}) %collective-permute-start.4) | collective-permute-done | bytes 524320 | tf_op jit(solution)/shard_map/ppermute | solution.py:506
  28.4 2.1 %collective-permute-start.11 = (bf16[512,512]{1,0:T(8,128)(2,1)S(1)}, bf16[512,512]{1,0:T(8,128)(2,1)S(1)}, u32[]{:S(2)}, u32[]{:S(2)}) collective-permute-start(bf16[512,512]{1,0:T(8,128)(2,1)S(1)} %collective-permute-done.4.refs_8_.refs_14_), channel_id=1, source_target_pairs={{0,1},{1,0},{2,3},{3,2},{4,5},{5,4},{6,7},{7,6},{8,9},{9,8},{10,11... | collective-permute-start | bytes 1572872 | tf_op jit(solution)/shard_map/ppermute | solution.py:506
  30.6 1.5 %collective-permute-start.9 = (bf16[512,512]{1,0:T(8,128)(2,1)S(1)}, bf16[512,512]{1,0:T(8,128)(2,1)S(1)}, u32[]{:S(2)}, u32[]{:S(2)}) collective-permute-start(bf16[512,512]{1,0:T(8,128)(2,1)S(1)} %collective-permute-done.4.refs_8_.refs_14_), channel_id=1, source_target_pairs={{0,16},{1,9},{2,18},{3,11},{4,20},{5,13},{6,22},{7,15},{8,24},{9,1... | collective-permute-start | bytes 1572872 | tf_op jit(solution)/shard_map/ppermute | solution.py:506
  32.2 6.6 %collective-permute-done.10.refs_14_.refs_20_ = bf16[512,512]{1,0:T(8,128)(2,1)S(1)} collective-permute-done((bf16[512,512]{1,0:T(8,128)(2,1)S(1)}, bf16[512,512]{1,0:T(8,128)(2,1)S(1)}, u32[]{:S(2)}, u32[]{:S(2)}) %collective-permute-start.10) | collective-permute-done | bytes 524320 | tf_op jit(solution)/shard_map/ppermute | solution.py:506
  38.8 1.7 %collective-permute-start.16 = (bf16[512,512]{1,0:T(8,128)(2,1)S(1)}, bf16[512,512]{1,0:T(8,128)(2,1)}, u32[]{:S(2)}, u32[]{:S(2)}) collective-permute-start(bf16[512,512]{1,0:T(8,128)(2,1)S(1)} %slice.19), channel_id=1, source_target_pairs={{0,8},{1,17},{2,10},{3,19},{4,12},{5,21},{6,14},{7,23},{8,0},{9,25... | collective-permute-start | bytes 1572872 | tf_op jit(solution)/shard_map/ppermute | solution.py:506
  40.7 1.5 %collective-permute-start.17 = (bf16[512,512]{1,0:T(8,128)(2,1)S(1)}, bf16[512,512]{1,0:T(8,128)(2,1)}, u32[]{:S(2)}, u32[]{:S(2)}) collective-permute-start(bf16[512,512]{1,0:T(8,128)(2,1)S(1)} %collective-permute-done.10.refs_14_.refs_20_), channel_id=1, source_target_pairs={{0,1},{1,0},{2,3},{3,2},{4,5},{5,4},{6,7},{7,6},{8,9},{9,8},{10,11... | collective-permute-start | bytes 1572872 | tf_op jit(solution)/shard_map/ppermute | solution.py:506
  42.2 1.5 %collective-permute-start.15 = (bf16[512,512]{1,0:T(8,128)(2,1)S(1)}, bf16[512,512]{1,0:T(8,128)(2,1)}, u32[]{:S(2)}, u32[]{:S(2)}) collective-permute-start(bf16[512,512]{1,0:T(8,128)(2,1)S(1)} %collective-permute-done.10.refs_14_.refs_20_), channel_id=1, source_target_pairs={{0,16},{1,9},{2,18},{3,11},{4,20},{5,13},{6,22},{7,15},{8,24},{9,1... | collective-permute-start | bytes 1572872 | tf_op jit(solution)/shard_map/ppermute | solution.py:506
  43.7 8.3 %collective-permute-done.16.refs_2_ = bf16[512,512]{1,0:T(8,128)(2,1)} collective-permute-done((bf16[512,512]{1,0:T(8,128)(2,1)S(1)}, bf16[512,512]{1,0:T(8,128)(2,1)}, u32[]{:S(2)}, u32[]{:S(2)}) %collective-permute-start.16) | collective-permute-done | bytes 524320 | tf_op jit(solution)/shard_map/ppermute | solution.py:506
  53.2 1.3 %collective-permute-done.15.refs_16_.refs_22_ = bf16[512,512]{1,0:T(8,128)(2,1)} collective-permute-done((bf16[512,512]{1,0:T(8,128)(2,1)S(1)}, bf16[512,512]{1,0:T(8,128)(2,1)}, u32[]{:S(2)}, u32[]{:S(2)}) %collective-permute-start.15) | collective-permute-done | bytes 524320 | tf_op jit(solution)/shard_map/ppermute | solution.py:506
  54.5 1.4 %copy-done.1 = bf16[512,2048]{1,0:T(8,128)(2,1)} copy-done((bf16[512,2048]{1,0:T(8,128)(2,1)}, bf16[512,2048]{1,0:T(8,128)(2,1)S(1)}, u32[]{:S(2)}) %copy-start.1) | copy-done | bytes 2097176
  57.2 0.8 collective-permute-start.22
  57.9 1.4 %collective-permute-start.21 = (bf16[512,512]{1,0:T(8,128)(2,1)}, bf16[512,512]{1,0:T(8,128)(2,1)}, u32[]{:S(2)}, u32[]{:S(2)}) collective-permute-start(bf16[512,512]{1,0:T(8,128)(2,1)} %collective-permute-done.16.refs_2_), channel_id=1, source_target_pairs={{0,16},{1,9},{2,18},{3,11},{4,20},{5,13},{6,22},{7,15},{8,24},{9,1... | collective-permute-start | bytes 1572872 | tf_op jit(solution)/shard_map/ppermute | solution.py:506
  59.3 0.8 dynamic_slice.3
  60.1 0.8 copy.5.index_ref
  60.9 8.5 %shard_map.37.picked_ref = bf16[256,512]{1,0:T(8,128)(2,1)} custom-call(s32[256,1]{1,0:T(8,128)} %copy.5.index_ref, bf16[512,2048]{1,0:T(8,128)(2,1)} %refs_0_.3, bf16[512,2048]{1,0:T(8,128)(2,1)} %copy-done.1, bf16[512,512]{1,0:T(8,128)(2,1)} %copy-done.2, bf16[512,512]{1,0:T(8,128)(2,1)} %copy-done.9, bf16[512,512]{1,0:T(8,128)(2,1)} %copy-done.5, ...), custom_call_target="tpu_custom_call" | custom-call | tf_op jit(solution)/shard_map/pallas_call | solution.py:409
  69.5 2.3 %collective-permute-done.22.refs_6_ = bf16[512,512]{1,0:T(8,128)(2,1)} collective-permute-done((bf16[512,512]{1,0:T(8,128)(2,1)}, bf16[512,512]{1,0:T(8,128)(2,1)}, u32[]{:S(2)}, u32[]{:S(2)}) %collective-permute-start.22) | collective-permute-done | bytes 524320 | tf_op jit(solution)/shard_map/ppermute | solution.py:506
  73.0 2.3 %collective-permute-done.23.refs_5_ = bf16[512,512]{1,0:T(8,128)(2,1)S(1)} collective-permute-done((bf16[512,512]{1,0:T(8,128)(2,1)}, bf16[512,512]{1,0:T(8,128)(2,1)S(1)}, u32[]{:S(2)}, u32[]{:S(2)}) %collective-permute-start.23) | collective-permute-done | bytes 524320 | tf_op jit(solution)/shard_map/ppermute | solution.py:452
  76.1 34.5 %shard_map.38 = f32[256,128,128]{2,1,0:T(8,128)} custom-call(s32[256,1]{1,0:T(8,128)} %copy.5.index_ref, bf16[256,512]{1,0:T(8,128)(2,1)} %shard_map.37.picked_ref, bf16[65,128,256]{2,1,0:T(8,128)(2,1)} %constant.14.clone.far_tables_ref, bf16[512,2048]{1,0:T(8,128)(2,1)} %refs_0_.3, bf16[512,2048]{1,0:T(8,128)(2,1)} %copy-done.1, ...), custom_call_target="tpu_custom_call" | custom-call | tf_op jit(solution)/shard_map/pallas_call | solution.py:430
  (65 shorter events, 5.1 us)
Async XLA Ops:
  1.4 15.8 %collective-permute-start.1 = (bf16[512,512]{1,0:T(8,128)(2,1)S(1)}, bf16[512,512]{1,0:T(8,128)(2,1)S(1)}, u32[]{:S(2)}, u32[]{:S(2)}) collective-permute-start(bf16[512,512]{1,0:T(8,128)(2,1)S(1)} %get-tuple-element.66), channel_id=1, source_target_pairs={{0,8},{1,17},{2,10},{3,19},{4,12},{5,21},{6,14},{7,23},{8,0},{9,25... | collective-permute-start | bytes 1572872 | tf_op jit(solution)/shard_map/ppermute | solution.py:506
  4.4 50.1 %collective-permute-start = (bf16[512,2048]{1,0:T(8,128)(2,1)S(1)}, bf16[512,2048]{1,0:T(8,128)(2,1)S(1)}, u32[]{:S(2)}, u32[]{:S(2)}) collective-permute-start(bf16[512,2048]{1,0:T(8,128)(2,1)S(1)} %copy-done), channel_id=1, source_target_pairs={{0,4},{4,0},{8,12},{12,8},{16,20},{20,16},{24,28},{28,24},{1,5},{5... | collective-permute-start | bytes 6291464 | tf_op jit(solution)/shard_map/ppermute | solution.py:452
  4.4 24.0 %collective-permute-start.4 = (bf16[512,512]{1,0:T(8,128)(2,1)S(1)}, bf16[512,512]{1,0:T(8,128)(2,1)S(1)}, u32[]{:S(2)}, u32[]{:S(2)}) collective-permute-start(bf16[512,512]{1,0:T(8,128)(2,1)S(1)} %get-tuple-element.65), channel_id=1, source_target_pairs={{0,8},{1,17},{2,10},{3,19},{4,12},{5,21},{6,14},{7,23},{8,0},{9,25... | collective-permute-start | bytes 1572872 | tf_op jit(solution)/shard_map/ppermute | solution.py:506
  17.2 13.4 %collective-permute-start.5 = (bf16[512,512]{1,0:T(8,128)(2,1)S(1)}, bf16[512,512]{1,0:T(8,128)(2,1)S(1)}, u32[]{:S(2)}, u32[]{:S(2)}) collective-permute-start(bf16[512,512]{1,0:T(8,128)(2,1)S(1)} %collective-permute-done.1.refs_2_.refs_8_), channel_id=1, source_target_pairs={{0,1},{1,0},{2,3},{3,2},{4,5},{5,4},{6,7},{7,6},{8,9},{9,8},{10,11... | collective-permute-start | bytes 1572872 | tf_op jit(solution)/shard_map/ppermute | solution.py:506
  19.3 12.8 %collective-permute-start.3 = (bf16[512,512]{1,0:T(8,128)(2,1)S(1)}, bf16[512,512]{1,0:T(8,128)(2,1)S(1)}, u32[]{:S(2)}, u32[]{:S(2)}) collective-permute-start(bf16[512,512]{1,0:T(8,128)(2,1)S(1)} %collective-permute-done.1.refs_2_.refs_8_), channel_id=1, source_target_pairs={{0,16},{1,9},{2,18},{3,11},{4,20},{5,13},{6,22},{7,15},{8,24},{9,1... | collective-permute-start | bytes 1572872 | tf_op jit(solution)/shard_map/ppermute | solution.py:506
  20.9 17.9 %collective-permute-start.10 = (bf16[512,512]{1,0:T(8,128)(2,1)S(1)}, bf16[512,512]{1,0:T(8,128)(2,1)S(1)}, u32[]{:S(2)}, u32[]{:S(2)}) collective-permute-start(bf16[512,512]{1,0:T(8,128)(2,1)S(1)} %slice.18), channel_id=1, source_target_pairs={{0,8},{1,17},{2,10},{3,19},{4,12},{5,21},{6,14},{7,23},{8,0},{9,25... | collective-permute-start | bytes 1572872 | tf_op jit(solution)/shard_map/ppermute | solution.py:506
  28.4 12.3 %collective-permute-start.11 = (bf16[512,512]{1,0:T(8,128)(2,1)S(1)}, bf16[512,512]{1,0:T(8,128)(2,1)S(1)}, u32[]{:S(2)}, u32[]{:S(2)}) collective-permute-start(bf16[512,512]{1,0:T(8,128)(2,1)S(1)} %collective-permute-done.4.refs_8_.refs_14_), channel_id=1, source_target_pairs={{0,1},{1,0},{2,3},{3,2},{4,5},{5,4},{6,7},{7,6},{8,9},{9,8},{10,11... | collective-permute-start | bytes 1572872 | tf_op jit(solution)/shard_map/ppermute | solution.py:506
  30.6 11.6 %collective-permute-start.9 = (bf16[512,512]{1,0:T(8,128)(2,1)S(1)}, bf16[512,512]{1,0:T(8,128)(2,1)S(1)}, u32[]{:S(2)}, u32[]{:S(2)}) collective-permute-start(bf16[512,512]{1,0:T(8,128)(2,1)S(1)} %collective-permute-done.4.refs_8_.refs_14_), channel_id=1, source_target_pairs={{0,16},{1,9},{2,18},{3,11},{4,20},{5,13},{6,22},{7,15},{8,24},{9,1... | collective-permute-start | bytes 1572872 | tf_op jit(solution)/shard_map/ppermute | solution.py:506
  32.2 19.9 %collective-permute-start.2 = (bf16[512,512]{1,0:T(8,128)(2,1)S(1)}, bf16[512,512]{1,0:T(8,128)(2,1)S(1)}, u32[]{:S(2)}, u32[]{:S(2)}) collective-permute-start(bf16[512,512]{1,0:T(8,128)(2,1)S(1)} %collective-permute-done.1.refs_2_.refs_8_), channel_id=1, source_target_pairs={{0,4},{4,0},{8,12},{12,8},{16,20},{20,16},{24,28},{28,24},{1,5},{5... | collective-permute-start | bytes 1572872 | tf_op jit(solution)/shard_map/ppermute | solution.py:452
  38.8 13.2 %collective-permute-start.16 = (bf16[512,512]{1,0:T(8,128)(2,1)S(1)}, bf16[512,512]{1,0:T(8,128)(2,1)}, u32[]{:S(2)}, u32[]{:S(2)}) collective-permute-start(bf16[512,512]{1,0:T(8,128)(2,1)S(1)} %slice.19), channel_id=1, source_target_pairs={{0,8},{1,17},{2,10},{3,19},{4,12},{5,21},{6,14},{7,23},{8,0},{9,25... | collective-permute-start | bytes 1572872 | tf_op jit(solution)/shard_map/ppermute | solution.py:506
  40.7 12.5 %collective-permute-start.17 = (bf16[512,512]{1,0:T(8,128)(2,1)S(1)}, bf16[512,512]{1,0:T(8,128)(2,1)}, u32[]{:S(2)}, u32[]{:S(2)}) collective-permute-start(bf16[512,512]{1,0:T(8,128)(2,1)S(1)} %collective-permute-done.10.refs_14_.refs_20_), channel_id=1, source_target_pairs={{0,1},{1,0},{2,3},{3,2},{4,5},{5,4},{6,7},{7,6},{8,9},{9,8},{10,11... | collective-permute-start | bytes 1572872 | tf_op jit(solution)/shard_map/ppermute | solution.py:506
  42.2 12.3 %collective-permute-start.15 = (bf16[512,512]{1,0:T(8,128)(2,1)S(1)}, bf16[512,512]{1,0:T(8,128)(2,1)}, u32[]{:S(2)}, u32[]{:S(2)}) collective-permute-start(bf16[512,512]{1,0:T(8,128)(2,1)S(1)} %collective-permute-done.10.refs_14_.refs_20_), channel_id=1, source_target_pairs={{0,16},{1,9},{2,18},{3,11},{4,20},{5,13},{6,22},{7,15},{8,24},{9,1... | collective-permute-start | bytes 1572872 | tf_op jit(solution)/shard_map/ppermute | solution.py:506
  52.0 4.4 %collective-permute-start.8 = (bf16[512,512]{1,0:T(8,128)(2,1)S(1)}, bf16[512,512]{1,0:T(8,128)(2,1)S(1)}, u32[]{:S(2)}, u32[]{:S(2)}) collective-permute-start(bf16[512,512]{1,0:T(8,128)(2,1)S(1)} %collective-permute-done.4.refs_8_.refs_14_), channel_id=1, source_target_pairs={{0,4},{4,0},{8,12},{12,8},{16,20},{20,16},{24,28},{28,24},{1,5},{5... | collective-permute-start | bytes 1572872 | tf_op jit(solution)/shard_map/ppermute | solution.py:452
  52.1 4.4 %collective-permute-start.6 = (bf16[512,512]{1,0:T(8,128)(2,1)S(1)}, bf16[512,512]{1,0:T(8,128)(2,1)S(1)}, u32[]{:S(2)}, u32[]{:S(2)}) collective-permute-start(bf16[512,512]{1,0:T(8,128)(2,1)S(1)} %collective-permute-done.3.refs_4_.refs_10_), channel_id=1, source_target_pairs={{0,4},{4,0},{8,12},{12,8},{16,20},{20,16},{24,28},{28,24},{1,5},{5... | collective-permute-start | bytes 1572872 | tf_op jit(solution)/shard_map/ppermute | solution.py:452
  53.2 3.8 %collective-permute-start.7 = (bf16[512,512]{1,0:T(8,128)(2,1)S(1)}, bf16[512,512]{1,0:T(8,128)(2,1)S(1)}, u32[]{:S(2)}, u32[]{:S(2)}) collective-permute-start(bf16[512,512]{1,0:T(8,128)(2,1)S(1)} %collective-permute-done.5.refs_6_.refs_12_), channel_id=1, source_target_pairs={{0,4},{4,0},{8,12},{12,8},{16,20},{20,16},{24,28},{28,24},{1,5},{5... | collective-permute-start | bytes 1572872 | tf_op jit(solution)/shard_map/ppermute | solution.py:452
  54.5 2.6 %collective-permute-start.12 = (bf16[512,512]{1,0:T(8,128)(2,1)S(1)}, bf16[512,512]{1,0:T(8,128)(2,1)S(1)}, u32[]{:S(2)}, u32[]{:S(2)}) collective-permute-start(bf16[512,512]{1,0:T(8,128)(2,1)S(1)} %collective-permute-done.9.refs_10_.refs_16_), channel_id=1, source_target_pairs={{0,4},{4,0},{8,12},{12,8},{16,20},{20,16},{24,28},{28,24},{1,5},{5... | collective-permute-start | bytes 1572872 | tf_op jit(solution)/shard_map/ppermute | solution.py:452
  56.4 4.5 %collective-permute-start.14 = (bf16[512,512]{1,0:T(8,128)(2,1)S(1)}, bf16[512,512]{1,0:T(8,128)(2,1)}, u32[]{:S(2)}, u32[]{:S(2)}) collective-permute-start(bf16[512,512]{1,0:T(8,128)(2,1)S(1)} %collective-permute-done.10.refs_14_.refs_20_), channel_id=1, source_target_pairs={{0,4},{4,0},{8,12},{12,8},{16,20},{20,16},{24,28},{28,24},{1,5},{5... | collective-permute-start | bytes 1572872 | tf_op jit(solution)/shard_map/ppermute | solution.py:452
  56.5 4.4 %collective-permute-start.18 = (bf16[512,512]{1,0:T(8,128)(2,1)}, bf16[512,512]{1,0:T(8,128)(2,1)}, u32[]{:S(2)}, u32[]{:S(2)}) collective-permute-start(bf16[512,512]{1,0:T(8,128)(2,1)} %collective-permute-done.15.refs_16_.refs_22_), channel_id=1, source_target_pairs={{0,4},{4,0},{8,12},{12,8},{16,20},{20,16},{24,28},{28,24},{1,5},{5... | collective-permute-start | bytes 1572872 | tf_op jit(solution)/shard_map/ppermute | solution.py:452
  57.0 3.9 %collective-permute-start.19 = (bf16[512,512]{1,0:T(8,128)(2,1)}, bf16[512,512]{1,0:T(8,128)(2,1)}, u32[]{:S(2)}, u32[]{:S(2)}) collective-permute-start(bf16[512,512]{1,0:T(8,128)(2,1)} %collective-permute-done.17.refs_18_.refs_24_), channel_id=1, source_target_pairs={{0,4},{4,0},{8,12},{12,8},{16,20},{20,16},{24,28},{28,24},{1,5},{5... | collective-permute-start | bytes 1572872 | tf_op jit(solution)/shard_map/ppermute | solution.py:452
  57.2 14.6 %collective-permute-start.22 = (bf16[512,512]{1,0:T(8,128)(2,1)}, bf16[512,512]{1,0:T(8,128)(2,1)}, u32[]{:S(2)}, u32[]{:S(2)}) collective-permute-start(bf16[512,512]{1,0:T(8,128)(2,1)} %collective-permute-done.16.refs_2_), channel_id=1, source_target_pairs={{0,1},{1,0},{2,3},{3,2},{4,5},{5,4},{6,7},{7,6},{8,9},{9,8},{10,11... | collective-permute-start | bytes 1572872 | tf_op jit(solution)/shard_map/ppermute | solution.py:506
  57.9 14.5 %collective-permute-start.21 = (bf16[512,512]{1,0:T(8,128)(2,1)}, bf16[512,512]{1,0:T(8,128)(2,1)}, u32[]{:S(2)}, u32[]{:S(2)}) collective-permute-start(bf16[512,512]{1,0:T(8,128)(2,1)} %collective-permute-done.16.refs_2_), channel_id=1, source_target_pairs={{0,16},{1,9},{2,18},{3,11},{4,20},{5,13},{6,22},{7,15},{8,24},{9,1... | collective-permute-start | bytes 1572872 | tf_op jit(solution)/shard_map/ppermute | solution.py:506
  60.9 12.1 %collective-permute-start.20 = (bf16[512,512]{1,0:T(8,128)(2,1)}, bf16[512,512]{1,0:T(8,128)(2,1)}, u32[]{:S(2)}, u32[]{:S(2)}) collective-permute-start(bf16[512,512]{1,0:T(8,128)(2,1)} %collective-permute-done.16.refs_2_), channel_id=1, source_target_pairs={{0,4},{4,0},{8,12},{12,8},{16,20},{20,16},{24,28},{28,24},{1,5},{5... | collective-permute-start | bytes 1572872 | tf_op jit(solution)/shard_map/ppermute | solution.py:452
  72.5 2.8 %collective-permute-start.23 = (bf16[512,512]{1,0:T(8,128)(2,1)}, bf16[512,512]{1,0:T(8,128)(2,1)S(1)}, u32[]{:S(2)}, u32[]{:S(2)}) collective-permute-start(bf16[512,512]{1,0:T(8,128)(2,1)} %collective-permute-done.21.refs_4_), channel_id=1, source_target_pairs={{0,4},{4,0},{8,12},{12,8},{16,20},{20,16},{24,28},{28,24},{1,5},{5... | collective-permute-start | bytes 1572872 | tf_op jit(solution)/shard_map/ppermute | solution.py:452
  72.5 3.0 %collective-permute-start.24 = (bf16[512,512]{1,0:T(8,128)(2,1)}, bf16[512,512]{1,0:T(8,128)(2,1)}, u32[]{:S(2)}, u32[]{:S(2)}) collective-permute-start(bf16[512,512]{1,0:T(8,128)(2,1)} %collective-permute-done.22.refs_6_), channel_id=1, source_target_pairs={{0,4},{4,0},{8,12},{12,8},{16,20},{20,16},{24,28},{28,24},{1,5},{5... | collective-permute-start | bytes 1572872 | tf_op jit(solution)/shard_map/ppermute | solution.py:452
  (17 other events, 207.3 us)

commit v4 on v3

--- a/solution.py
+++ b/solution.py
@@ -492,7 +492,7 @@
 
 
 CORE, NEAR, FAR = 1, 2, 4
-SCRIPT = ("F0", "F1", "B", "P0", "F2", "P1", "F3", "S0", "P2", "S1", "W", "X3", "V2", "P3", "S2", "K012:0", "S3")
+SCRIPT = ("F0", "F1", "B", "P0", "F2", "P1", "F3", "S0", "P2", "W", "S1", "X3", "V2", "P3", "S2", "K012:0", "S3")
 PIECE_ROWS = (4, 4, 4, 4)
 
 

time: 111 us -> 111 us (level)
  local copies, waits for them, and re-layouts: 5.09 us -> 3.79 us
  waiting for transfers between devices: 40.8 us -> 42 us
    unnamed x32 -> x34, local copies, waits for them, and re-layouts: 2.04 us -> 0.71 us
    ppermute x12, waiting for transfers between devices: 38.3 us -> 39.4 us  [exchange(): return lax.ppermute(array, ('grid', 'pts'), pairs)]
  transfers between devices with their start and end apart: 25 -> 25, of which waited for: 11 -> 11; matrix products, arithmetic and copies ran while one was open for 1% -> 3% of each run, Pallas kernels for 8% -> 8%
where the time goes in v4:
time: 111 us; the launch traced here: 110 us
  Pallas kernels  43 us (39%)
  waiting for transfers between devices  42 us (38%)
  starting transfers between devices  21.3 us (19%)
  local copies, waits for them, and re-layouts  3.79 us (3%)
    ppermute x12, waiting for transfers between devices, exchange(): return lax.ppermute(array, ('grid', 'pts'), pairs)  39.4 us
    pallas_call x1, Pallas kernels, screen_sheets(): pl.pallas_call(functools.partial(sheet_kernel, plan, pick_first), in_spec...  34.5 us
    ppermute x12, starting transfers between devices, exchange(): return lax.ppermute(array, ('grid', 'pts'), pairs)  18.6 us
    pallas_call x1, Pallas kernels, pick_cells(): pl.pallas_call(functools.partial(pick_kernel, plan), in_specs=[VMEM_SPEC]...  8.55 us
    ppermute x13, starting transfers between devices, swap(): return lax.ppermute(array, 'grid', [(i, i ^ mask) for i in range(count)])  2.66 us
    ppermute x13, waiting for transfers between devices, swap(): return lax.ppermute(array, 'grid', [(i, i ^ mask) for i in range(count)])  2.51 us
  transfers between devices with their start and end apart: 25, of which 11 were waited for; matrix products, arithmetic and copies ran while one was open for 3% of the time, Pallas kernels for 8%

profile of v4, /device:TPU:0, one launch (start us, length us, event | category | flops | bytes accessed | tf_op | source)
XLA Modules:
  0.0 110.4 jit_solution(13420896862252596773)
XLA Ops:
  0.5 1.4 %fusion = (bf16[512,512]{1,0:T(8,128)(2,1)S(1)}, bf16[512,512]{1,0:T(8,128)(2,1)S(1)}) fusion(bf16[512,2048]{1,0:T(8,128)(2,1)} %refs_0_.3), kind=kLoop, calls=%fused_computation | loop fusion | bytes 2097152 | tf_op jit(solution)/shard_map/slice | solution.py:516
  1.9 2.5 %collective-permute-start.1 = (bf16[512,512]{1,0:T(8,128)(2,1)S(1)}, bf16[512,512]{1,0:T(8,128)(2,1)S(1)}, u32[]{:S(2)}, u32[]{:S(2)}) collective-permute-start(bf16[512,512]{1,0:T(8,128)(2,1)S(1)} %get-tuple-element.66), channel_id=1, source_target_pairs={{0,8},{1,17},{2,10},{3,19},{4,12},{5,21},{6,14},{7,23},{8,0},{9,25... | collective-permute-start | bytes 1572872 | tf_op jit(solution)/shard_map/ppermute | solution.py:506
  4.5 12.7 %collective-permute-done.1.refs_2_.refs_8_ = bf16[512,512]{1,0:T(8,128)(2,1)S(1)} collective-permute-done((bf16[512,512]{1,0:T(8,128)(2,1)S(1)}, bf16[512,512]{1,0:T(8,128)(2,1)S(1)}, u32[]{:S(2)}, u32[]{:S(2)}) %collective-permute-start.1) | collective-permute-done | bytes 524320 | tf_op jit(solution)/shard_map/ppermute | solution.py:506
  17.2 2.1 %collective-permute-start.5 = (bf16[512,512]{1,0:T(8,128)(2,1)S(1)}, bf16[512,512]{1,0:T(8,128)(2,1)S(1)}, u32[]{:S(2)}, u32[]{:S(2)}) collective-permute-start(bf16[512,512]{1,0:T(8,128)(2,1)S(1)} %collective-permute-done.1.refs_2_.refs_8_), channel_id=1, source_target_pairs={{0,1},{1,0},{2,3},{3,2},{4,5},{5,4},{6,7},{7,6},{8,9},{9,8},{10,11... | collective-permute-start | bytes 1572872 | tf_op jit(solution)/shard_map/ppermute | solution.py:506
  19.3 1.5 %collective-permute-start.3 = (bf16[512,512]{1,0:T(8,128)(2,1)S(1)}, bf16[512,512]{1,0:T(8,128)(2,1)S(1)}, u32[]{:S(2)}, u32[]{:S(2)}) collective-permute-start(bf16[512,512]{1,0:T(8,128)(2,1)S(1)} %collective-permute-done.1.refs_2_.refs_8_), channel_id=1, source_target_pairs={{0,16},{1,9},{2,18},{3,11},{4,20},{5,13},{6,22},{7,15},{8,24},{9,1... | collective-permute-start | bytes 1572872 | tf_op jit(solution)/shard_map/ppermute | solution.py:506
  20.8 1.6 %collective-permute-start.10 = (bf16[512,512]{1,0:T(8,128)(2,1)S(1)}, bf16[512,512]{1,0:T(8,128)(2,1)S(1)}, u32[]{:S(2)}, u32[]{:S(2)}) collective-permute-start(bf16[512,512]{1,0:T(8,128)(2,1)S(1)} %slice.18), channel_id=1, source_target_pairs={{0,8},{1,17},{2,10},{3,19},{4,12},{5,21},{6,14},{7,23},{8,0},{9,25... | collective-permute-start | bytes 1572872 | tf_op jit(solution)/shard_map/ppermute | solution.py:506
  22.4 6.0 %collective-permute-done.4.refs_8_.refs_14_ = bf16[512,512]{1,0:T(8,128)(2,1)S(1)} collective-permute-done((bf16[512,512]{1,0:T(8,128)(2,1)S(1)}, bf16[512,512]{1,0:T(8,128)(2,1)S(1)}, u32[]{:S(2)}, u32[]{:S(2)}) %collective-permute-start.4) | collective-permute-done | bytes 524320 | tf_op jit(solution)/shard_map/ppermute | solution.py:506
  28.4 2.1 %collective-permute-start.11 = (bf16[512,512]{1,0:T(8,128)(2,1)S(1)}, bf16[512,512]{1,0:T(8,128)(2,1)S(1)}, u32[]{:S(2)}, u32[]{:S(2)}) collective-permute-start(bf16[512,512]{1,0:T(8,128)(2,1)S(1)} %collective-permute-done.4.refs_8_.refs_14_), channel_id=1, source_target_pairs={{0,1},{1,0},{2,3},{3,2},{4,5},{5,4},{6,7},{7,6},{8,9},{9,8},{10,11... | collective-permute-start | bytes 1572872 | tf_op jit(solution)/shard_map/ppermute | solution.py:506
  30.5 1.5 %collective-permute-start.9 = (bf16[512,512]{1,0:T(8,128)(2,1)S(1)}, bf16[512,512]{1,0:T(8,128)(2,1)S(1)}, u32[]{:S(2)}, u32[]{:S(2)}) collective-permute-start(bf16[512,512]{1,0:T(8,128)(2,1)S(1)} %collective-permute-done.4.refs_8_.refs_14_), channel_id=1, source_target_pairs={{0,16},{1,9},{2,18},{3,11},{4,20},{5,13},{6,22},{7,15},{8,24},{9,1... | collective-permute-start | bytes 1572872 | tf_op jit(solution)/shard_map/ppermute | solution.py:506
  32.1 1.6 %collective-permute-start.16 = (bf16[512,512]{1,0:T(8,128)(2,1)S(1)}, bf16[512,512]{1,0:T(8,128)(2,1)}, u32[]{:S(2)}, u32[]{:S(2)}) collective-permute-start(bf16[512,512]{1,0:T(8,128)(2,1)S(1)} %slice.19), channel_id=1, source_target_pairs={{0,8},{1,17},{2,10},{3,19},{4,12},{5,21},{6,14},{7,23},{8,0},{9,25... | collective-permute-start | bytes 1572872 | tf_op jit(solution)/shard_map/ppermute | solution.py:506
  33.7 6.0 %collective-permute-done.10.refs_14_.refs_20_ = bf16[512,512]{1,0:T(8,128)(2,1)S(1)} collective-permute-done((bf16[512,512]{1,0:T(8,128)(2,1)S(1)}, bf16[512,512]{1,0:T(8,128)(2,1)S(1)}, u32[]{:S(2)}, u32[]{:S(2)}) %collective-permute-start.10) | collective-permute-done | bytes 524320 | tf_op jit(solution)/shard_map/ppermute | solution.py:506
  39.7 2.0 %collective-permute-done.11.refs_12_.refs_18_ = bf16[512,512]{1,0:T(8,128)(2,1)S(1)} collective-permute-done((bf16[512,512]{1,0:T(8,128)(2,1)S(1)}, bf16[512,512]{1,0:T(8,128)(2,1)S(1)}, u32[]{:S(2)}, u32[]{:S(2)}) %collective-permute-start.11) | collective-permute-done | bytes 524320 | tf_op jit(solution)/shard_map/ppermute | solution.py:506
  41.7 1.6 %collective-permute-start.17 = (bf16[512,512]{1,0:T(8,128)(2,1)S(1)}, bf16[512,512]{1,0:T(8,128)(2,1)S(1)}, u32[]{:S(2)}, u32[]{:S(2)}) collective-permute-start(bf16[512,512]{1,0:T(8,128)(2,1)S(1)} %collective-permute-done.10.refs_14_.refs_20_), channel_id=1, source_target_pairs={{0,1},{1,0},{2,3},{3,2},{4,5},{5,4},{6,7},{7,6},{8,9},{9,8},{10,11... | collective-permute-start | bytes 1572872 | tf_op jit(solution)/shard_map/ppermute | solution.py:506
  43.3 1.5 %collective-permute-start.15 = (bf16[512,512]{1,0:T(8,128)(2,1)S(1)}, bf16[512,512]{1,0:T(8,128)(2,1)S(1)}, u32[]{:S(2)}, u32[]{:S(2)}) collective-permute-start(bf16[512,512]{1,0:T(8,128)(2,1)S(1)} %collective-permute-done.10.refs_14_.refs_20_), channel_id=1, source_target_pairs={{0,16},{1,9},{2,18},{3,11},{4,20},{5,13},{6,22},{7,15},{8,24},{9,1... | collective-permute-start | bytes 1572872 | tf_op jit(solution)/shard_map/ppermute | solution.py:506
  44.9 5.8 %collective-permute-done.16.refs_2_ = bf16[512,512]{1,0:T(8,128)(2,1)} collective-permute-done((bf16[512,512]{1,0:T(8,128)(2,1)S(1)}, bf16[512,512]{1,0:T(8,128)(2,1)}, u32[]{:S(2)}, u32[]{:S(2)}) %collective-permute-start.16) | collective-permute-done | bytes 524320 | tf_op jit(solution)/shard_map/ppermute | solution.py:506
  51.3 3.1 %collective-permute-done.17.refs_18_.refs_24_ = bf16[512,512]{1,0:T(8,128)(2,1)S(1)} collective-permute-done((bf16[512,512]{1,0:T(8,128)(2,1)S(1)}, bf16[512,512]{1,0:T(8,128)(2,1)S(1)}, u32[]{:S(2)}, u32[]{:S(2)}) %collective-permute-start.17) | collective-permute-done | bytes 524320 | tf_op jit(solution)/shard_map/ppermute | solution.py:506
  54.4 1.5 %collective-permute-done.15.refs_16_.refs_22_ = bf16[512,512]{1,0:T(8,128)(2,1)S(1)} collective-permute-done((bf16[512,512]{1,0:T(8,128)(2,1)S(1)}, bf16[512,512]{1,0:T(8,128)(2,1)S(1)}, u32[]{:S(2)}, u32[]{:S(2)}) %collective-permute-start.15) | collective-permute-done | bytes 524320 | tf_op jit(solution)/shard_map/ppermute | solution.py:506
  57.0 1.0 collective-permute-start.22
  58.0 1.6 %collective-permute-start.21 = (bf16[512,512]{1,0:T(8,128)(2,1)}, bf16[512,512]{1,0:T(8,128)(2,1)}, u32[]{:S(2)}, u32[]{:S(2)}) collective-permute-start(bf16[512,512]{1,0:T(8,128)(2,1)} %collective-permute-done.16.refs_2_), channel_id=1, source_target_pairs={{0,16},{1,9},{2,18},{3,11},{4,20},{5,13},{6,22},{7,15},{8,24},{9,1... | collective-permute-start | bytes 1572872 | tf_op jit(solution)/shard_map/ppermute | solution.py:506
  60.4 0.8 copy.5.index_ref
  61.3 8.6 %shard_map.37.picked_ref = bf16[256,512]{1,0:T(8,128)(2,1)} custom-call(s32[256,1]{1,0:T(8,128)} %copy.5.index_ref, bf16[512,2048]{1,0:T(8,128)(2,1)} %refs_0_.3, bf16[512,2048]{1,0:T(8,128)(2,1)} %collective-permute-done.refs_1_, bf16[512,512]{1,0:T(8,128)(2,1)} %copy-done.1, bf16[512,512]{1,0:T(8,128)(2,1)} %copy-done.8, bf16[512,512]{1,0:T(8,128)(2,1)} %copy-done.4, ...), custom_call_target="tpu_custom_call" | custom-call | tf_op jit(solution)/shard_map/pallas_call | solution.py:409
  69.8 1.5 %collective-permute-done.22.refs_6_ = bf16[512,512]{1,0:T(8,128)(2,1)} collective-permute-done((bf16[512,512]{1,0:T(8,128)(2,1)}, bf16[512,512]{1,0:T(8,128)(2,1)}, u32[]{:S(2)}, u32[]{:S(2)}) %collective-permute-start.22) | collective-permute-done | bytes 524320 | tf_op jit(solution)/shard_map/ppermute | solution.py:506
  72.6 2.3 %collective-permute-done.23.refs_5_ = bf16[512,512]{1,0:T(8,128)(2,1)S(1)} collective-permute-done((bf16[512,512]{1,0:T(8,128)(2,1)}, bf16[512,512]{1,0:T(8,128)(2,1)S(1)}, u32[]{:S(2)}, u32[]{:S(2)}) %collective-permute-start.23) | collective-permute-done | bytes 524320 | tf_op jit(solution)/shard_map/ppermute | solution.py:452
  75.7 34.5 %shard_map.38 = f32[256,128,128]{2,1,0:T(8,128)} custom-call(s32[256,1]{1,0:T(8,128)} %copy.5.index_ref, bf16[256,512]{1,0:T(8,128)(2,1)} %shard_map.37.picked_ref, bf16[65,128,256]{2,1,0:T(8,128)(2,1)} %constant.14.clone.far_tables_ref, bf16[512,2048]{1,0:T(8,128)(2,1)} %refs_0_.3, bf16[512,2048]{1,0:T(8,128)(2,1)} %collective-permute-done.refs_1_, ...), custom_call_target="tpu_custom_call" | custom-call | tf_op jit(solution)/shard_map/pallas_call | solution.py:430
  (67 shorter events, 5.2 us)
Async XLA Ops:
  0.0 43.3 %collective-permute-start = (bf16[512,2048]{1,0:T(8,128)(2,1)}, bf16[512,2048]{1,0:T(8,128)(2,1)}, u32[]{:S(2)}, u32[]{:S(2)}) collective-permute-start(bf16[512,2048]{1,0:T(8,128)(2,1)} %refs_0_.3), channel_id=1, source_target_pairs={{0,4},{4,0},{8,12},{12,8},{16,20},{20,16},{24,28},{28,24},{1,5},{5... | collective-permute-start | bytes 6291464 | tf_op jit(solution)/shard_map/ppermute | solution.py:452
  1.9 15.3 %collective-permute-start.1 = (bf16[512,512]{1,0:T(8,128)(2,1)S(1)}, bf16[512,512]{1,0:T(8,128)(2,1)S(1)}, u32[]{:S(2)}, u32[]{:S(2)}) collective-permute-start(bf16[512,512]{1,0:T(8,128)(2,1)S(1)} %get-tuple-element.66), channel_id=1, source_target_pairs={{0,8},{1,17},{2,10},{3,19},{4,12},{5,21},{6,14},{7,23},{8,0},{9,25... | collective-permute-start | bytes 1572872 | tf_op jit(solution)/shard_map/ppermute | solution.py:506
  4.4 24.0 %collective-permute-start.4 = (bf16[512,512]{1,0:T(8,128)(2,1)S(1)}, bf16[512,512]{1,0:T(8,128)(2,1)S(1)}, u32[]{:S(2)}, u32[]{:S(2)}) collective-permute-start(bf16[512,512]{1,0:T(8,128)(2,1)S(1)} %get-tuple-element.65), channel_id=1, source_target_pairs={{0,8},{1,17},{2,10},{3,19},{4,12},{5,21},{6,14},{7,23},{8,0},{9,25... | collective-permute-start | bytes 1572872 | tf_op jit(solution)/shard_map/ppermute | solution.py:506
  17.2 13.3 %collective-permute-start.5 = (bf16[512,512]{1,0:T(8,128)(2,1)S(1)}, bf16[512,512]{1,0:T(8,128)(2,1)S(1)}, u32[]{:S(2)}, u32[]{:S(2)}) collective-permute-start(bf16[512,512]{1,0:T(8,128)(2,1)S(1)} %collective-permute-done.1.refs_2_.refs_8_), channel_id=1, source_target_pairs={{0,1},{1,0},{2,3},{3,2},{4,5},{5,4},{6,7},{7,6},{8,9},{9,8},{10,11... | collective-permute-start | bytes 1572872 | tf_op jit(solution)/shard_map/ppermute | solution.py:506
  19.3 12.8 %collective-permute-start.3 = (bf16[512,512]{1,0:T(8,128)(2,1)S(1)}, bf16[512,512]{1,0:T(8,128)(2,1)S(1)}, u32[]{:S(2)}, u32[]{:S(2)}) collective-permute-start(bf16[512,512]{1,0:T(8,128)(2,1)S(1)} %collective-permute-done.1.refs_2_.refs_8_), channel_id=1, source_target_pairs={{0,16},{1,9},{2,18},{3,11},{4,20},{5,13},{6,22},{7,15},{8,24},{9,1... | collective-permute-start | bytes 1572872 | tf_op jit(solution)/shard_map/ppermute | solution.py:506
  20.8 18.8 %collective-permute-start.10 = (bf16[512,512]{1,0:T(8,128)(2,1)S(1)}, bf16[512,512]{1,0:T(8,128)(2,1)S(1)}, u32[]{:S(2)}, u32[]{:S(2)}) collective-permute-start(bf16[512,512]{1,0:T(8,128)(2,1)S(1)} %slice.18), channel_id=1, source_target_pairs={{0,8},{1,17},{2,10},{3,19},{4,12},{5,21},{6,14},{7,23},{8,0},{9,25... | collective-permute-start | bytes 1572872 | tf_op jit(solution)/shard_map/ppermute | solution.py:506
  28.4 13.3 %collective-permute-start.11 = (bf16[512,512]{1,0:T(8,128)(2,1)S(1)}, bf16[512,512]{1,0:T(8,128)(2,1)S(1)}, u32[]{:S(2)}, u32[]{:S(2)}) collective-permute-start(bf16[512,512]{1,0:T(8,128)(2,1)S(1)} %collective-permute-done.4.refs_8_.refs_14_), channel_id=1, source_target_pairs={{0,1},{1,0},{2,3},{3,2},{4,5},{5,4},{6,7},{7,6},{8,9},{9,8},{10,11... | collective-permute-start | bytes 1572872 | tf_op jit(solution)/shard_map/ppermute | solution.py:506
  30.5 14.3 %collective-permute-start.9 = (bf16[512,512]{1,0:T(8,128)(2,1)S(1)}, bf16[512,512]{1,0:T(8,128)(2,1)S(1)}, u32[]{:S(2)}, u32[]{:S(2)}) collective-permute-start(bf16[512,512]{1,0:T(8,128)(2,1)S(1)} %collective-permute-done.4.refs_8_.refs_14_), channel_id=1, source_target_pairs={{0,16},{1,9},{2,18},{3,11},{4,20},{5,13},{6,22},{7,15},{8,24},{9,1... | collective-permute-start | bytes 1572872 | tf_op jit(solution)/shard_map/ppermute | solution.py:506
  32.1 18.6 %collective-permute-start.16 = (bf16[512,512]{1,0:T(8,128)(2,1)S(1)}, bf16[512,512]{1,0:T(8,128)(2,1)}, u32[]{:S(2)}, u32[]{:S(2)}) collective-permute-start(bf16[512,512]{1,0:T(8,128)(2,1)S(1)} %slice.19), channel_id=1, source_target_pairs={{0,8},{1,17},{2,10},{3,19},{4,12},{5,21},{6,14},{7,23},{8,0},{9,25... | collective-permute-start | bytes 1572872 | tf_op jit(solution)/shard_map/ppermute | solution.py:506
  39.7 11.0 %collective-permute-start.2 = (bf16[512,512]{1,0:T(8,128)(2,1)S(1)}, bf16[512,512]{1,0:T(8,128)(2,1)S(1)}, u32[]{:S(2)}, u32[]{:S(2)}) collective-permute-start(bf16[512,512]{1,0:T(8,128)(2,1)S(1)} %collective-permute-done.1.refs_2_.refs_8_), channel_id=1, source_target_pairs={{0,4},{4,0},{8,12},{12,8},{16,20},{20,16},{24,28},{28,24},{1,5},{5... | collective-permute-start | bytes 1572872 | tf_op jit(solution)/shard_map/ppermute | solution.py:452
  41.7 12.6 %collective-permute-start.17 = (bf16[512,512]{1,0:T(8,128)(2,1)S(1)}, bf16[512,512]{1,0:T(8,128)(2,1)S(1)}, u32[]{:S(2)}, u32[]{:S(2)}) collective-permute-start(bf16[512,512]{1,0:T(8,128)(2,1)S(1)} %collective-permute-done.10.refs_14_.refs_20_), channel_id=1, source_target_pairs={{0,1},{1,0},{2,3},{3,2},{4,5},{5,4},{6,7},{7,6},{8,9},{9,8},{10,11... | collective-permute-start | bytes 1572872 | tf_op jit(solution)/shard_map/ppermute | solution.py:506
  43.3 12.5 %collective-permute-start.15 = (bf16[512,512]{1,0:T(8,128)(2,1)S(1)}, bf16[512,512]{1,0:T(8,128)(2,1)S(1)}, u32[]{:S(2)}, u32[]{:S(2)}) collective-permute-start(bf16[512,512]{1,0:T(8,128)(2,1)S(1)} %collective-permute-done.10.refs_14_.refs_20_), channel_id=1, source_target_pairs={{0,16},{1,9},{2,18},{3,11},{4,20},{5,13},{6,22},{7,15},{8,24},{9,1... | collective-permute-start | bytes 1572872 | tf_op jit(solution)/shard_map/ppermute | solution.py:506
  44.8 11.0 %collective-permute-start.8 = (bf16[512,512]{1,0:T(8,128)(2,1)S(1)}, bf16[512,512]{1,0:T(8,128)(2,1)S(1)}, u32[]{:S(2)}, u32[]{:S(2)}) collective-permute-start(bf16[512,512]{1,0:T(8,128)(2,1)S(1)} %collective-permute-done.4.refs_8_.refs_14_), channel_id=1, source_target_pairs={{0,4},{4,0},{8,12},{12,8},{16,20},{20,16},{24,28},{28,24},{1,5},{5... | collective-permute-start | bytes 1572872 | tf_op jit(solution)/shard_map/ppermute | solution.py:452
  50.7 5.7 %collective-permute-start.6 = (bf16[512,512]{1,0:T(8,128)(2,1)S(1)}, bf16[512,512]{1,0:T(8,128)(2,1)S(1)}, u32[]{:S(2)}, u32[]{:S(2)}) collective-permute-start(bf16[512,512]{1,0:T(8,128)(2,1)S(1)} %collective-permute-done.3.refs_4_.refs_10_), channel_id=1, source_target_pairs={{0,4},{4,0},{8,12},{12,8},{16,20},{20,16},{24,28},{28,24},{1,5},{5... | collective-permute-start | bytes 1572872 | tf_op jit(solution)/shard_map/ppermute | solution.py:452
  50.7 5.8 %collective-permute-start.7 = (bf16[512,512]{1,0:T(8,128)(2,1)S(1)}, bf16[512,512]{1,0:T(8,128)(2,1)S(1)}, u32[]{:S(2)}, u32[]{:S(2)}) collective-permute-start(bf16[512,512]{1,0:T(8,128)(2,1)S(1)} %collective-permute-done.5.refs_6_.refs_12_), channel_id=1, source_target_pairs={{0,4},{4,0},{8,12},{12,8},{16,20},{20,16},{24,28},{28,24},{1,5},{5... | collective-permute-start | bytes 1572872 | tf_op jit(solution)/shard_map/ppermute | solution.py:452
  54.4 2.6 %collective-permute-start.12 = (bf16[512,512]{1,0:T(8,128)(2,1)S(1)}, bf16[512,512]{1,0:T(8,128)(2,1)S(1)}, u32[]{:S(2)}, u32[]{:S(2)}) collective-permute-start(bf16[512,512]{1,0:T(8,128)(2,1)S(1)} %collective-permute-done.9.refs_10_.refs_16_), channel_id=1, source_target_pairs={{0,4},{4,0},{8,12},{12,8},{16,20},{20,16},{24,28},{28,24},{1,5},{5... | collective-permute-start | bytes 1572872 | tf_op jit(solution)/shard_map/ppermute | solution.py:452
  55.9 5.4 %collective-permute-start.14 = (bf16[512,512]{1,0:T(8,128)(2,1)S(1)}, bf16[512,512]{1,0:T(8,128)(2,1)}, u32[]{:S(2)}, u32[]{:S(2)}) collective-permute-start(bf16[512,512]{1,0:T(8,128)(2,1)S(1)} %collective-permute-done.10.refs_14_.refs_20_), channel_id=1, source_target_pairs={{0,4},{4,0},{8,12},{12,8},{16,20},{20,16},{24,28},{28,24},{1,5},{5... | collective-permute-start | bytes 1572872 | tf_op jit(solution)/shard_map/ppermute | solution.py:452
  56.4 4.8 %collective-permute-start.18 = (bf16[512,512]{1,0:T(8,128)(2,1)S(1)}, bf16[512,512]{1,0:T(8,128)(2,1)}, u32[]{:S(2)}, u32[]{:S(2)}) collective-permute-start(bf16[512,512]{1,0:T(8,128)(2,1)S(1)} %collective-permute-done.15.refs_16_.refs_22_), channel_id=1, source_target_pairs={{0,4},{4,0},{8,12},{12,8},{16,20},{20,16},{24,28},{28,24},{1,5},{5... | collective-permute-start | bytes 1572872 | tf_op jit(solution)/shard_map/ppermute | solution.py:452
  56.5 4.7 %collective-permute-start.19 = (bf16[512,512]{1,0:T(8,128)(2,1)S(1)}, bf16[512,512]{1,0:T(8,128)(2,1)}, u32[]{:S(2)}, u32[]{:S(2)}) collective-permute-start(bf16[512,512]{1,0:T(8,128)(2,1)S(1)} %collective-permute-done.17.refs_18_.refs_24_), channel_id=1, source_target_pairs={{0,4},{4,0},{8,12},{12,8},{16,20},{20,16},{24,28},{28,24},{1,5},{5... | collective-permute-start | bytes 1572872 | tf_op jit(solution)/shard_map/ppermute | solution.py:452
  57.0 14.3 %collective-permute-start.22 = (bf16[512,512]{1,0:T(8,128)(2,1)}, bf16[512,512]{1,0:T(8,128)(2,1)}, u32[]{:S(2)}, u32[]{:S(2)}) collective-permute-start(bf16[512,512]{1,0:T(8,128)(2,1)} %collective-permute-done.16.refs_2_), channel_id=1, source_target_pairs={{0,1},{1,0},{2,3},{3,2},{4,5},{5,4},{6,7},{7,6},{8,9},{9,8},{10,11... | collective-permute-start | bytes 1572872 | tf_op jit(solution)/shard_map/ppermute | solution.py:506
  58.0 14.1 %collective-permute-start.21 = (bf16[512,512]{1,0:T(8,128)(2,1)}, bf16[512,512]{1,0:T(8,128)(2,1)}, u32[]{:S(2)}, u32[]{:S(2)}) collective-permute-start(bf16[512,512]{1,0:T(8,128)(2,1)} %collective-permute-done.16.refs_2_), channel_id=1, source_target_pairs={{0,16},{1,9},{2,18},{3,11},{4,20},{5,13},{6,22},{7,15},{8,24},{9,1... | collective-permute-start | bytes 1572872 | tf_op jit(solution)/shard_map/ppermute | solution.py:506
  61.2 11.4 %collective-permute-start.20 = (bf16[512,512]{1,0:T(8,128)(2,1)}, bf16[512,512]{1,0:T(8,128)(2,1)}, u32[]{:S(2)}, u32[]{:S(2)}) collective-permute-start(bf16[512,512]{1,0:T(8,128)(2,1)} %collective-permute-done.16.refs_2_), channel_id=1, source_target_pairs={{0,4},{4,0},{8,12},{12,8},{16,20},{20,16},{24,28},{28,24},{1,5},{5... | collective-permute-start | bytes 1572872 | tf_op jit(solution)/shard_map/ppermute | solution.py:452
  72.1 2.8 %collective-permute-start.23 = (bf16[512,512]{1,0:T(8,128)(2,1)}, bf16[512,512]{1,0:T(8,128)(2,1)S(1)}, u32[]{:S(2)}, u32[]{:S(2)}) collective-permute-start(bf16[512,512]{1,0:T(8,128)(2,1)} %collective-permute-done.21.refs_4_), channel_id=1, source_target_pairs={{0,4},{4,0},{8,12},{12,8},{16,20},{20,16},{24,28},{28,24},{1,5},{5... | collective-permute-start | bytes 1572872 | tf_op jit(solution)/shard_map/ppermute | solution.py:452
  72.1 3.0 %collective-permute-start.24 = (bf16[512,512]{1,0:T(8,128)(2,1)}, bf16[512,512]{1,0:T(8,128)(2,1)}, u32[]{:S(2)}, u32[]{:S(2)}) collective-permute-start(bf16[512,512]{1,0:T(8,128)(2,1)} %collective-permute-done.22.refs_6_), channel_id=1, source_target_pairs={{0,4},{4,0},{8,12},{12,8},{16,20},{20,16},{24,28},{28,24},{1,5},{5... | collective-permute-start | bytes 1572872 | tf_op jit(solution)/shard_map/ppermute | solution.py:452
  (18 other events, 222.7 us)

commit v5 on v4

--- a/solution.py
+++ b/solution.py
@@ -525,8 +525,11 @@
         core[p] = [order.start(swap, first[p], CORE)]
 
     def share(p):
-        order.wait(*far[p])
-        core[p] += [order.start(swap, array, CORE) for array in far[p]]
+        if p < len(PIECE_ROWS) - 1:
+            order.wait(*far[p])
+        for array in far[p]:
+            order.wait(array)
+            core[p].append(order.start(swap, array, CORE))
 
     def step(p):
         order.wait(*core[p])

time: 111 us -> 136 us (1.23)
  waiting for transfers between devices: 42 us -> 66.9 us
    ppermute x12, waiting for transfers between devices: 39.4 us -> 64.8 us  [exchange(): return lax.ppermute(array, ('grid', 'pts'), pairs)]
    ppermute x12, starting transfers between devices: 18.6 us -> 20 us  [exchange(): return lax.ppermute(array, ('grid', 'pts'), pairs)]
  transfers between devices with their start and end apart: 25 -> 25, of which waited for: 11 -> 10; matrix products, arithmetic and copies ran while one was open for 3% -> 1% of each run, Pallas kernels for 8% -> 6%
where the time goes in v5:
time: 136 us
  waiting for transfers between devices  66.9 us (49%)
  Pallas kernels  43.1 us (32%)
  starting transfers between devices  22.2 us (16%)
  local copies, waits for them, and re-layouts  3.76 us (3%)
    ppermute x12, waiting for transfers between devices, exchange(): return lax.ppermute(array, ('grid', 'pts'), pairs)  64.8 us
    pallas_call x1, Pallas kernels, screen_sheets(): pl.pallas_call(functools.partial(sheet_kernel, plan, pick_first), in_spec...  34.5 us
    ppermute x12, starting transfers between devices, exchange(): return lax.ppermute(array, ('grid', 'pts'), pairs)  20 us
    pallas_call x1, Pallas kernels, pick_cells(): pl.pallas_call(functools.partial(pick_kernel, plan), in_specs=[VMEM_SPEC]...  8.53 us
  transfers between devices with their start and end apart: 25, of which 10 were waited for; matrix products, arithmetic and copies ran while one was open for 1% of the time, Pallas kernels for 6%

profile of v5, /device:TPU:0, one launch (start us, length us, event | category | flops | bytes accessed | tf_op | source)
XLA Modules:
  0.0 136.2 jit_solution(8196505283489300576)
XLA Ops:
  0.0 1.4 %fusion = (bf16[512,512]{1,0:T(8,128)(2,1)S(1)}, bf16[512,512]{1,0:T(8,128)(2,1)S(1)}) fusion(bf16[512,2048]{1,0:T(8,128)(2,1)} %refs_0_.3), kind=kLoop, calls=%fused_computation | loop fusion | bytes 2097152 | tf_op jit(solution)/shard_map/slice | solution.py:516
  1.4 3.0 %collective-permute-start.1 = (bf16[512,512]{1,0:T(8,128)(2,1)S(1)}, bf16[512,512]{1,0:T(8,128)(2,1)S(1)}, u32[]{:S(2)}, u32[]{:S(2)}) collective-permute-start(bf16[512,512]{1,0:T(8,128)(2,1)S(1)} %get-tuple-element.20), channel_id=1, source_target_pairs={{0,8},{1,17},{2,10},{3,19},{4,12},{5,21},{6,14},{7,23},{8,0},{9,25... | collective-permute-start | bytes 1572872 | tf_op jit(solution)/shard_map/ppermute | solution.py:506
  4.5 12.7 %collective-permute-done.1.refs_2_.refs_8_ = bf16[512,512]{1,0:T(8,128)(2,1)S(1)} collective-permute-done((bf16[512,512]{1,0:T(8,128)(2,1)S(1)}, bf16[512,512]{1,0:T(8,128)(2,1)S(1)}, u32[]{:S(2)}, u32[]{:S(2)}) %collective-permute-start.1) | collective-permute-done | bytes 524320 | tf_op jit(solution)/shard_map/ppermute | solution.py:506
  17.2 2.1 %collective-permute-start.13 = (bf16[512,512]{1,0:T(8,128)(2,1)S(1)}, bf16[512,512]{1,0:T(8,128)(2,1)S(1)}, u32[]{:S(2)}, u32[]{:S(2)}) collective-permute-start(bf16[512,512]{1,0:T(8,128)(2,1)S(1)} %slice.18), channel_id=1, source_target_pairs={{0,8},{1,17},{2,10},{3,19},{4,12},{5,21},{6,14},{7,23},{8,0},{9,25... | collective-permute-start | bytes 1572872 | tf_op jit(solution)/shard_map/ppermute | solution.py:506
  19.4 9.1 %collective-permute-done.7.refs_8_.refs_14_ = bf16[512,512]{1,0:T(8,128)(2,1)S(1)} collective-permute-done((bf16[512,512]{1,0:T(8,128)(2,1)S(1)}, bf16[512,512]{1,0:T(8,128)(2,1)S(1)}, u32[]{:S(2)}, u32[]{:S(2)}) %collective-permute-start.7) | collective-permute-done | bytes 524320 | tf_op jit(solution)/shard_map/ppermute | solution.py:506
  28.5 2.1 %collective-permute-start.19 = (bf16[512,512]{1,0:T(8,128)(2,1)S(1)}, bf16[512,512]{1,0:T(8,128)(2,1)}, u32[]{:S(2)}, u32[]{:S(2)}) collective-permute-start(bf16[512,512]{1,0:T(8,128)(2,1)S(1)} %slice.19), channel_id=1, source_target_pairs={{0,8},{1,17},{2,10},{3,19},{4,12},{5,21},{6,14},{7,23},{8,0},{9,25... | collective-permute-start | bytes 1572872 | tf_op jit(solution)/shard_map/ppermute | solution.py:506
  30.6 1.6 %collective-permute-start.5 = (bf16[512,512]{1,0:T(8,128)(2,1)S(1)}, bf16[512,512]{1,0:T(8,128)(2,1)S(1)}, u32[]{:S(2)}, u32[]{:S(2)}) collective-permute-start(bf16[512,512]{1,0:T(8,128)(2,1)S(1)} %collective-permute-done.1.refs_2_.refs_8_), channel_id=1, source_target_pairs={{0,1},{1,0},{2,3},{3,2},{4,5},{5,4},{6,7},{7,6},{8,9},{9,8},{10,11... | collective-permute-start | bytes 1572872 | tf_op jit(solution)/shard_map/ppermute | solution.py:506
  32.7 7.0 %collective-permute-done.13.refs_14_.refs_20_ = bf16[512,512]{1,0:T(8,128)(2,1)S(1)} collective-permute-done((bf16[512,512]{1,0:T(8,128)(2,1)S(1)}, bf16[512,512]{1,0:T(8,128)(2,1)S(1)}, u32[]{:S(2)}, u32[]{:S(2)}) %collective-permute-start.13) | collective-permute-done | bytes 524320 | tf_op jit(solution)/shard_map/ppermute | solution.py:506
  39.7 2.1 %collective-permute-start.11 = (bf16[512,512]{1,0:T(8,128)(2,1)S(1)}, bf16[512,512]{1,0:T(8,128)(2,1)S(1)}, u32[]{:S(2)}, u32[]{:S(2)}) collective-permute-start(bf16[512,512]{1,0:T(8,128)(2,1)S(1)} %collective-permute-done.7.refs_8_.refs_14_), channel_id=1, source_target_pairs={{0,1},{1,0},{2,3},{3,2},{4,5},{5,4},{6,7},{7,6},{8,9},{9,8},{10,11... | collective-permute-start | bytes 1572872 | tf_op jit(solution)/shard_map/ppermute | solution.py:506
  41.8 8.4 %collective-permute-done.19.refs_2_ = bf16[512,512]{1,0:T(8,128)(2,1)} collective-permute-done((bf16[512,512]{1,0:T(8,128)(2,1)S(1)}, bf16[512,512]{1,0:T(8,128)(2,1)}, u32[]{:S(2)}, u32[]{:S(2)}) %collective-permute-start.19) | collective-permute-done | bytes 524320 | tf_op jit(solution)/shard_map/ppermute | solution.py:506
  50.2 1.8 %collective-permute-start.9 = (bf16[512,512]{1,0:T(8,128)(2,1)S(1)}, bf16[512,512]{1,0:T(8,128)(2,1)S(1)}, u32[]{:S(2)}, u32[]{:S(2)}) collective-permute-start(bf16[512,512]{1,0:T(8,128)(2,1)S(1)} %collective-permute-done.7.refs_8_.refs_14_), channel_id=1, source_target_pairs={{0,16},{1,9},{2,18},{3,11},{4,20},{5,13},{6,22},{7,15},{8,24},{9,1... | collective-permute-start | bytes 1572872 | tf_op jit(solution)/shard_map/ppermute | solution.py:506
  52.2 1.6 %collective-permute-start.17 = (bf16[512,512]{1,0:T(8,128)(2,1)S(1)}, bf16[512,512]{1,0:T(8,128)(2,1)S(1)}, u32[]{:S(2)}, u32[]{:S(2)}) collective-permute-start(bf16[512,512]{1,0:T(8,128)(2,1)S(1)} %collective-permute-done.13.refs_14_.refs_20_), channel_id=1, source_target_pairs={{0,1},{1,0},{2,3},{3,2},{4,5},{5,4},{6,7},{7,6},{8,9},{9,8},{10,11... | collective-permute-start | bytes 1572872 | tf_op jit(solution)/shard_map/ppermute | solution.py:506
  53.8 1.5 %collective-permute-start.15 = (bf16[512,512]{1,0:T(8,128)(2,1)S(1)}, bf16[512,512]{1,0:T(8,128)(2,1)}, u32[]{:S(2)}, u32[]{:S(2)}) collective-permute-start(bf16[512,512]{1,0:T(8,128)(2,1)S(1)} %collective-permute-done.13.refs_14_.refs_20_), channel_id=1, source_target_pairs={{0,16},{1,9},{2,18},{3,11},{4,20},{5,13},{6,22},{7,15},{8,24},{9,1... | collective-permute-start | bytes 1572872 | tf_op jit(solution)/shard_map/ppermute | solution.py:506
  55.3 9.6 %collective-permute-done.9.refs_10_.refs_16_ = bf16[512,512]{1,0:T(8,128)(2,1)S(1)} collective-permute-done((bf16[512,512]{1,0:T(8,128)(2,1)S(1)}, bf16[512,512]{1,0:T(8,128)(2,1)S(1)}, u32[]{:S(2)}, u32[]{:S(2)}) %collective-permute-start.9) | collective-permute-done | bytes 524320 | tf_op jit(solution)/shard_map/ppermute | solution.py:506
  65.0 1.9 %collective-permute-start.23 = (bf16[512,512]{1,0:T(8,128)(2,1)}, bf16[512,512]{1,0:T(8,128)(2,1)}, u32[]{:S(2)}, u32[]{:S(2)}) collective-permute-start(bf16[512,512]{1,0:T(8,128)(2,1)} %collective-permute-done.19.refs_2_), channel_id=1, source_target_pairs={{0,1},{1,0},{2,3},{3,2},{4,5},{5,4},{6,7},{7,6},{8,9},{9,8},{10,11... | collective-permute-start | bytes 1572872 | tf_op jit(solution)/shard_map/ppermute | solution.py:506
  66.9 1.5 %collective-permute-start.21 = (bf16[512,512]{1,0:T(8,128)(2,1)}, bf16[512,512]{1,0:T(8,128)(2,1)}, u32[]{:S(2)}, u32[]{:S(2)}) collective-permute-start(bf16[512,512]{1,0:T(8,128)(2,1)} %collective-permute-done.19.refs_2_), channel_id=1, source_target_pairs={{0,16},{1,9},{2,18},{3,11},{4,20},{5,13},{6,22},{7,15},{8,24},{9,1... | collective-permute-start | bytes 1572872 | tf_op jit(solution)/shard_map/ppermute | solution.py:506
  68.4 7.9 %collective-permute-done.15.refs_16_.refs_22_ = bf16[512,512]{1,0:T(8,128)(2,1)} collective-permute-done((bf16[512,512]{1,0:T(8,128)(2,1)S(1)}, bf16[512,512]{1,0:T(8,128)(2,1)}, u32[]{:S(2)}, u32[]{:S(2)}) %collective-permute-start.15) | collective-permute-done | bytes 524320 | tf_op jit(solution)/shard_map/ppermute | solution.py:506
  76.9 2.9 %collective-permute-done.23.refs_6_ = bf16[512,512]{1,0:T(8,128)(2,1)} collective-permute-done((bf16[512,512]{1,0:T(8,128)(2,1)}, bf16[512,512]{1,0:T(8,128)(2,1)}, u32[]{:S(2)}, u32[]{:S(2)}) %collective-permute-start.23) | collective-permute-done | bytes 524320 | tf_op jit(solution)/shard_map/ppermute | solution.py:506
  79.8 7.3 %collective-permute-done.21.refs_4_ = bf16[512,512]{1,0:T(8,128)(2,1)} collective-permute-done((bf16[512,512]{1,0:T(8,128)(2,1)}, bf16[512,512]{1,0:T(8,128)(2,1)}, u32[]{:S(2)}, u32[]{:S(2)}) %collective-permute-start.21) | collective-permute-done | bytes 524320 | tf_op jit(solution)/shard_map/ppermute | solution.py:506
  89.2 1.4 collective-permute-done.18.refs_19_.refs_25_
  91.3 0.8 dynamic_slice.3
  92.1 0.8 copy.5.index_ref
  92.9 8.5 %shard_map.37.picked_ref = bf16[256,512]{1,0:T(8,128)(2,1)} custom-call(s32[256,1]{1,0:T(8,128)} %copy.5.index_ref, bf16[512,2048]{1,0:T(8,128)(2,1)} %refs_0_.3, bf16[512,2048]{1,0:T(8,128)(2,1)} %collective-permute-done.refs_1_, bf16[512,512]{1,0:T(8,128)(2,1)} %copy-done.1, bf16[512,512]{1,0:T(8,128)(2,1)} %copy-done.6, bf16[512,512]{1,0:T(8,128)(2,1)} %copy-done.5, ...), custom_call_target="tpu_custom_call" | custom-call | tf_op jit(solution)/shard_map/pallas_call | solution.py:409
  101.5 34.5 %shard_map.38 = f32[256,128,128]{2,1,0:T(8,128)} custom-call(s32[256,1]{1,0:T(8,128)} %copy.5.index_ref, bf16[256,512]{1,0:T(8,128)(2,1)} %shard_map.37.picked_ref, bf16[65,128,256]{2,1,0:T(8,128)(2,1)} %constant.14.clone.far_tables_ref, bf16[512,2048]{1,0:T(8,128)(2,1)} %refs_0_.3, bf16[512,2048]{1,0:T(8,128)(2,1)} %collective-permute-done.refs_1_, ...), custom_call_target="tpu_custom_call" | custom-call | tf_op jit(solution)/shard_map/pallas_call | solution.py:430
  (67 shorter events, 4.3 us)
Async XLA Ops:
  1.4 15.8 %collective-permute-start.1 = (bf16[512,512]{1,0:T(8,128)(2,1)S(1)}, bf16[512,512]{1,0:T(8,128)(2,1)S(1)}, u32[]{:S(2)}, u32[]{:S(2)}) collective-permute-start(bf16[512,512]{1,0:T(8,128)(2,1)S(1)} %get-tuple-element.20), channel_id=1, source_target_pairs={{0,8},{1,17},{2,10},{3,19},{4,12},{5,21},{6,14},{7,23},{8,0},{9,25... | collective-permute-start | bytes 1572872 | tf_op jit(solution)/shard_map/ppermute | solution.py:506
  4.4 24.0 %collective-permute-start.7 = (bf16[512,512]{1,0:T(8,128)(2,1)S(1)}, bf16[512,512]{1,0:T(8,128)(2,1)S(1)}, u32[]{:S(2)}, u32[]{:S(2)}) collective-permute-start(bf16[512,512]{1,0:T(8,128)(2,1)S(1)} %get-tuple-element.19), channel_id=1, source_target_pairs={{0,8},{1,17},{2,10},{3,19},{4,12},{5,21},{6,14},{7,23},{8,0},{9,25... | collective-permute-start | bytes 1572872 | tf_op jit(solution)/shard_map/ppermute | solution.py:506
  17.2 22.4 %collective-permute-start.13 = (bf16[512,512]{1,0:T(8,128)(2,1)S(1)}, bf16[512,512]{1,0:T(8,128)(2,1)S(1)}, u32[]{:S(2)}, u32[]{:S(2)}) collective-permute-start(bf16[512,512]{1,0:T(8,128)(2,1)S(1)} %slice.18), channel_id=1, source_target_pairs={{0,8},{1,17},{2,10},{3,19},{4,12},{5,21},{6,14},{7,23},{8,0},{9,25... | collective-permute-start | bytes 1572872 | tf_op jit(solution)/shard_map/ppermute | solution.py:506
  28.5 21.7 %collective-permute-start.19 = (bf16[512,512]{1,0:T(8,128)(2,1)S(1)}, bf16[512,512]{1,0:T(8,128)(2,1)}, u32[]{:S(2)}, u32[]{:S(2)}) collective-permute-start(bf16[512,512]{1,0:T(8,128)(2,1)S(1)} %slice.19), channel_id=1, source_target_pairs={{0,8},{1,17},{2,10},{3,19},{4,12},{5,21},{6,14},{7,23},{8,0},{9,25... | collective-permute-start | bytes 1572872 | tf_op jit(solution)/shard_map/ppermute | solution.py:506
  30.6 19.6 %collective-permute-start.5 = (bf16[512,512]{1,0:T(8,128)(2,1)S(1)}, bf16[512,512]{1,0:T(8,128)(2,1)S(1)}, u32[]{:S(2)}, u32[]{:S(2)}) collective-permute-start(bf16[512,512]{1,0:T(8,128)(2,1)S(1)} %collective-permute-done.1.refs_2_.refs_8_), channel_id=1, source_target_pairs={{0,1},{1,0},{2,3},{3,2},{4,5},{5,4},{6,7},{7,6},{8,9},{9,8},{10,11... | collective-permute-start | bytes 1572872 | tf_op jit(solution)/shard_map/ppermute | solution.py:506
  32.2 19.8 %collective-permute-start.3 = (bf16[512,512]{1,0:T(8,128)(2,1)S(1)}, bf16[512,512]{1,0:T(8,128)(2,1)S(1)}, u32[]{:S(2)}, u32[]{:S(2)}) collective-permute-start(bf16[512,512]{1,0:T(8,128)(2,1)S(1)} %collective-permute-done.1.refs_2_.refs_8_), channel_id=1, source_target_pairs={{0,16},{1,9},{2,18},{3,11},{4,20},{5,13},{6,22},{7,15},{8,24},{9,1... | collective-permute-start | bytes 1572872 | tf_op jit(solution)/shard_map/ppermute | solution.py:506
  32.7 19.5 %collective-permute-start.2 = (bf16[512,512]{1,0:T(8,128)(2,1)S(1)}, bf16[512,512]{1,0:T(8,128)(2,1)S(1)}, u32[]{:S(2)}, u32[]{:S(2)}) collective-permute-start(bf16[512,512]{1,0:T(8,128)(2,1)S(1)} %collective-permute-done.1.refs_2_.refs_8_), channel_id=1, source_target_pairs={{0,4},{4,0},{8,12},{12,8},{16,20},{20,16},{24,28},{28,24},{1,5},{5... | collective-permute-start | bytes 1572872 | tf_op jit(solution)/shard_map/ppermute | solution.py:452
  39.7 14.1 %collective-permute-start.11 = (bf16[512,512]{1,0:T(8,128)(2,1)S(1)}, bf16[512,512]{1,0:T(8,128)(2,1)S(1)}, u32[]{:S(2)}, u32[]{:S(2)}) collective-permute-start(bf16[512,512]{1,0:T(8,128)(2,1)S(1)} %collective-permute-done.7.refs_8_.refs_14_), channel_id=1, source_target_pairs={{0,1},{1,0},{2,3},{3,2},{4,5},{5,4},{6,7},{7,6},{8,9},{9,8},{10,11... | collective-permute-start | bytes 1572872 | tf_op jit(solution)/shard_map/ppermute | solution.py:506
  50.2 42.7 %collective-permute-start = (bf16[512,2048]{1,0:T(8,128)(2,1)S(1)}, bf16[512,2048]{1,0:T(8,128)(2,1)}, u32[]{:S(2)}, u32[]{:S(2)}) collective-permute-start(bf16[512,2048]{1,0:T(8,128)(2,1)S(1)} %copy-done), channel_id=1, source_target_pairs={{0,4},{4,0},{8,12},{12,8},{16,20},{20,16},{24,28},{28,24},{1,5},{5... | collective-permute-start | bytes 6291464 | tf_op jit(solution)/shard_map/ppermute | solution.py:452
  50.2 14.8 %collective-permute-start.9 = (bf16[512,512]{1,0:T(8,128)(2,1)S(1)}, bf16[512,512]{1,0:T(8,128)(2,1)S(1)}, u32[]{:S(2)}, u32[]{:S(2)}) collective-permute-start(bf16[512,512]{1,0:T(8,128)(2,1)S(1)} %collective-permute-done.7.refs_8_.refs_14_), channel_id=1, source_target_pairs={{0,16},{1,9},{2,18},{3,11},{4,20},{5,13},{6,22},{7,15},{8,24},{9,1... | collective-permute-start | bytes 1572872 | tf_op jit(solution)/shard_map/ppermute | solution.py:506
  52.0 13.0 %collective-permute-start.8 = (bf16[512,512]{1,0:T(8,128)(2,1)S(1)}, bf16[512,512]{1,0:T(8,128)(2,1)S(1)}, u32[]{:S(2)}, u32[]{:S(2)}) collective-permute-start(bf16[512,512]{1,0:T(8,128)(2,1)S(1)} %collective-permute-done.7.refs_8_.refs_14_), channel_id=1, source_target_pairs={{0,4},{4,0},{8,12},{12,8},{16,20},{20,16},{24,28},{28,24},{1,5},{5... | collective-permute-start | bytes 1572872 | tf_op jit(solution)/shard_map/ppermute | solution.py:452
  52.2 14.7 %collective-permute-start.17 = (bf16[512,512]{1,0:T(8,128)(2,1)S(1)}, bf16[512,512]{1,0:T(8,128)(2,1)S(1)}, u32[]{:S(2)}, u32[]{:S(2)}) collective-permute-start(bf16[512,512]{1,0:T(8,128)(2,1)S(1)} %collective-permute-done.13.refs_14_.refs_20_), channel_id=1, source_target_pairs={{0,1},{1,0},{2,3},{3,2},{4,5},{5,4},{6,7},{7,6},{8,9},{9,8},{10,11... | collective-permute-start | bytes 1572872 | tf_op jit(solution)/shard_map/ppermute | solution.py:506
  53.8 22.5 %collective-permute-start.15 = (bf16[512,512]{1,0:T(8,128)(2,1)S(1)}, bf16[512,512]{1,0:T(8,128)(2,1)}, u32[]{:S(2)}, u32[]{:S(2)}) collective-permute-start(bf16[512,512]{1,0:T(8,128)(2,1)S(1)} %collective-permute-done.13.refs_14_.refs_20_), channel_id=1, source_target_pairs={{0,16},{1,9},{2,18},{3,11},{4,20},{5,13},{6,22},{7,15},{8,24},{9,1... | collective-permute-start | bytes 1572872 | tf_op jit(solution)/shard_map/ppermute | solution.py:506
  65.0 11.3 %collective-permute-start.14 = (bf16[512,512]{1,0:T(8,128)(2,1)S(1)}, bf16[512,512]{1,0:T(8,128)(2,1)S(1)}, u32[]{:S(2)}, u32[]{:S(2)}) collective-permute-start(bf16[512,512]{1,0:T(8,128)(2,1)S(1)} %collective-permute-done.13.refs_14_.refs_20_), channel_id=1, source_target_pairs={{0,4},{4,0},{8,12},{12,8},{16,20},{20,16},{24,28},{28,24},{1,5},{5... | collective-permute-start | bytes 1572872 | tf_op jit(solution)/shard_map/ppermute | solution.py:452
  65.0 14.8 %collective-permute-start.23 = (bf16[512,512]{1,0:T(8,128)(2,1)}, bf16[512,512]{1,0:T(8,128)(2,1)}, u32[]{:S(2)}, u32[]{:S(2)}) collective-permute-start(bf16[512,512]{1,0:T(8,128)(2,1)} %collective-permute-done.19.refs_2_), channel_id=1, source_target_pairs={{0,1},{1,0},{2,3},{3,2},{4,5},{5,4},{6,7},{7,6},{8,9},{9,8},{10,11... | collective-permute-start | bytes 1572872 | tf_op jit(solution)/shard_map/ppermute | solution.py:506
  66.9 20.2 %collective-permute-start.21 = (bf16[512,512]{1,0:T(8,128)(2,1)}, bf16[512,512]{1,0:T(8,128)(2,1)}, u32[]{:S(2)}, u32[]{:S(2)}) collective-permute-start(bf16[512,512]{1,0:T(8,128)(2,1)} %collective-permute-done.19.refs_2_), channel_id=1, source_target_pairs={{0,16},{1,9},{2,18},{3,11},{4,20},{5,13},{6,22},{7,15},{8,24},{9,1... | collective-permute-start | bytes 1572872 | tf_op jit(solution)/shard_map/ppermute | solution.py:506
  76.3 10.8 %collective-permute-start.6 = (bf16[512,512]{1,0:T(8,128)(2,1)S(1)}, bf16[512,512]{1,0:T(8,128)(2,1)S(1)}, u32[]{:S(2)}, u32[]{:S(2)}) collective-permute-start(bf16[512,512]{1,0:T(8,128)(2,1)S(1)} %collective-permute-done.5.refs_6_.refs_12_), channel_id=1, source_target_pairs={{0,4},{4,0},{8,12},{12,8},{16,20},{20,16},{24,28},{28,24},{1,5},{5... | collective-permute-start | bytes 1572872 | tf_op jit(solution)/shard_map/ppermute | solution.py:452
  76.3 11.4 %collective-permute-start.4 = (bf16[512,512]{1,0:T(8,128)(2,1)S(1)}, bf16[512,512]{1,0:T(8,128)(2,1)S(1)}, u32[]{:S(2)}, u32[]{:S(2)}) collective-permute-start(bf16[512,512]{1,0:T(8,128)(2,1)S(1)} %collective-permute-done.3.refs_4_.refs_10_), channel_id=1, source_target_pairs={{0,4},{4,0},{8,12},{12,8},{16,20},{20,16},{24,28},{28,24},{1,5},{5... | collective-permute-start | bytes 1572872 | tf_op jit(solution)/shard_map/ppermute | solution.py:452
  79.8 8.0 %collective-permute-start.12 = (bf16[512,512]{1,0:T(8,128)(2,1)S(1)}, bf16[512,512]{1,0:T(8,128)(2,1)S(1)}, u32[]{:S(2)}, u32[]{:S(2)}) collective-permute-start(bf16[512,512]{1,0:T(8,128)(2,1)S(1)} %collective-permute-done.11.refs_12_.refs_18_), channel_id=1, source_target_pairs={{0,4},{4,0},{8,12},{12,8},{16,20},{20,16},{24,28},{28,24},{1,5},{5... | collective-permute-start | bytes 1572872 | tf_op jit(solution)/shard_map/ppermute | solution.py:452
  87.1 3.4 %collective-permute-start.18 = (bf16[512,512]{1,0:T(8,128)(2,1)S(1)}, bf16[512,512]{1,0:T(8,128)(2,1)S(1)}, u32[]{:S(2)}, u32[]{:S(2)}) collective-permute-start(bf16[512,512]{1,0:T(8,128)(2,1)S(1)} %collective-permute-done.17.refs_18_.refs_24_), channel_id=1, source_target_pairs={{0,4},{4,0},{8,12},{12,8},{16,20},{20,16},{24,28},{28,24},{1,5},{5... | collective-permute-start | bytes 1572872 | tf_op jit(solution)/shard_map/ppermute | solution.py:452
  87.7 5.2 %collective-permute-start.16 = (bf16[512,512]{1,0:T(8,128)(2,1)}, bf16[512,512]{1,0:T(8,128)(2,1)}, u32[]{:S(2)}, u32[]{:S(2)}) collective-permute-start(bf16[512,512]{1,0:T(8,128)(2,1)} %collective-permute-done.15.refs_16_.refs_22_), channel_id=1, source_target_pairs={{0,4},{4,0},{8,12},{12,8},{16,20},{20,16},{24,28},{28,24},{1,5},{5... | collective-permute-start | bytes 1572872 | tf_op jit(solution)/shard_map/ppermute | solution.py:452
  87.8 13.6 %collective-permute-start.20 = (bf16[512,512]{1,0:T(8,128)(2,1)}, bf16[512,512]{1,0:T(8,128)(2,1)}, u32[]{:S(2)}, u32[]{:S(2)}) collective-permute-start(bf16[512,512]{1,0:T(8,128)(2,1)} %collective-permute-done.19.refs_2_), channel_id=1, source_target_pairs={{0,4},{4,0},{8,12},{12,8},{16,20},{20,16},{24,28},{28,24},{1,5},{5... | collective-permute-start | bytes 1572872 | tf_op jit(solution)/shard_map/ppermute | solution.py:452
  89.0 12.4 %collective-permute-start.24 = (bf16[512,512]{1,0:T(8,128)(2,1)}, bf16[512,512]{1,0:T(8,128)(2,1)}, u32[]{:S(2)}, u32[]{:S(2)}) collective-permute-start(bf16[512,512]{1,0:T(8,128)(2,1)} %collective-permute-done.23.refs_6_), channel_id=1, source_target_pairs={{0,4},{4,0},{8,12},{12,8},{16,20},{20,16},{24,28},{28,24},{1,5},{5... | collective-permute-start | bytes 1572872 | tf_op jit(solution)/shard_map/ppermute | solution.py:452
  90.5 10.9 %collective-permute-start.22 = (bf16[512,512]{1,0:T(8,128)(2,1)}, bf16[512,512]{1,0:T(8,128)(2,1)}, u32[]{:S(2)}, u32[]{:S(2)}) collective-permute-start(bf16[512,512]{1,0:T(8,128)(2,1)} %collective-permute-done.21.refs_4_), channel_id=1, source_target_pairs={{0,4},{4,0},{8,12},{12,8},{16,20},{20,16},{24,28},{28,24},{1,5},{5... | collective-permute-start | bytes 1572872 | tf_op jit(solution)/shard_map/ppermute | solution.py:452
  (18 other events, 369.8 us)
